TPU v7x, 512 devices: a whole 4x4x16 slice. The times are simulated.
512 devices in a mesh: docs: 128 (over z_hi, y, x, core), proj: 4 (over z_lo).
Axes of the slice: x: 4, y: 4, z: 16 (z_hi: 4, z_lo: 4; z = z_hi * 4 + z_lo), core: 2. Of those that a mesh axis runs over, the one named last changes fastest.
Arguments:
- grads: bfloat16 [32768, 4096], P('docs', 'proj'), may hold values from -6 to 6
- precond: bfloat16 [4096, 4096], P('docs', 'proj'), may hold values from -3 to 3, as said below
- offsets: int32 [2], replicated, may hold values from 1 to 127
Outputs:
- influence: float32 [2, 32768, 256], P(None, 'docs')
Inputs may be any that keep to these rules, and one draw needn't show every extreme that they name: `precond`: symmetric.
All inputs are finite; a program needn't handle non-finite values.
Results may differ from a plain program's by a relative error of at most 0.014.
Values may be sent and summed in bfloat16 or wider, within the bound.
No kernel may reach another device: no remote copies, remote signals or barrier semaphores. Data moves between devices by JAX's collectives and lax.ppermute only.
A program may use at most 64 MiB of HBM per device.

v0:
```python
import math

import jax
import jax.numpy as jnp
from jax import lax
from jax.sharding import PartitionSpec as P

K = 4096
ROUNDS = 2


def shifted(value, axis, by):
    size = lax.axis_size(axis)
    return lax.ppermute(value, axis, [(i, (i + by) % size) for i in range(size)])


def fetch_every(block, offset, bits_total):
    current = block
    for bit in range(bits_total):
        moved = shifted(current, "docs", -(1 << bit))
        current = jnp.where(offset >> bit & 1 == 1, moved, current)
    return current


def on_device(grads, precond, offsets):
    whole = lax.all_gather(grads, "proj", axis=1, tiled=True)
    pre = jnp.dot(
        whole,
        lax.all_gather(precond, "docs", axis=0, tiled=True),
        preferred_element_type=jnp.float32,
    ).astype(jnp.bfloat16)
    factor = jnp.float32(1.0 / math.sqrt(K))
    bits_total = (lax.axis_size("docs") - 1).bit_length()
    results = []
    for step in range(ROUNDS):
        partner = fetch_every(grads, offsets[step], bits_total)
        partial_gram = lax.dot_general(
            pre, partner, (((1,), (1,)), ((), ())), preferred_element_type=jnp.float32
        )
        results.append(
            lax.psum(partial_gram.astype(jnp.bfloat16), "proj").astype(jnp.float32) * factor
        )
    return jnp.stack(results, axis=0)


def solution(mesh):
    placed = (P("docs", "proj"), P("docs", "proj"), P())
    return jax.shard_map(
        on_device, mesh=mesh, in_specs=placed, out_specs=P(None, "docs", None), check_vma=False
    )
```

profile of v0, /device:TPU:1, one launch (start us, length us, event | category | flops | bytes accessed | tf_op | source)
XLA Modules:
  0.0 803.5 jit_solution(531640912719454209)
XLA Ops:
  8.1 8.8 %collective-permute-start = (bf16[256,1024]{1,0:T(8,128)(2,1)}, bf16[256,1024]{1,0:T(8,128)(2,1)S(1)}, u32[]{:S(2)}, u32[]{:S(2)}) collective-permute-start(bf16[256,1024]{1,0:T(8,128)(2,1)} %param.3), channel_id=1, source_target_pairs={{0,508},{4,0},{8,4},{12,8},{16,12},{20,16},{24,20},{28,24},{32,28}... | collective-permute-start | bytes 1572872 | tf_op jit(solution)/shard_map/ppermute | solution.py:14
  16.8 1.3 fusion.4
  19.6 1.1 broadcast_select_fusion.6
  20.7 33.0 %collective-permute-start.1 = (bf16[256,1024]{1,0:T(8,128)(2,1)S(1)}, bf16[256,1024]{1,0:T(8,128)(2,1)S(1)}, u32[]{:S(2)}, u32[]{:S(2)}) collective-permute-start(bf16[256,1024]{1,0:T(8,128)(2,1)S(1)} %get-tuple-element.7), channel_id=1, source_target_pairs={{0,504},{4,508},{8,0},{12,4},{16,8},{20,12},{24,16},{28,20},{32,24... | collective-permute-start | bytes 1572872 | tf_op jit(solution)/shard_map/ppermute | solution.py:14
  53.7 1.9 collective-permute-start.7
  56.9 8.6 %collective-permute-done.1 = bf16[256,1024]{1,0:T(8,128)(2,1)S(1)} collective-permute-done((bf16[256,1024]{1,0:T(8,128)(2,1)S(1)}, bf16[256,1024]{1,0:T(8,128)(2,1)S(1)}, u32[]{:S(2)}, u32[]{:S(2)}) %collective-permute-start.1) | collective-permute-done | bytes 524320 | tf_op jit(solution)/shard_map/ppermute | solution.py:14
  65.6 1.9 collective-permute-start.2
  67.5 9.7 %collective-permute-done.7 = bf16[256,1024]{1,0:T(8,128)(2,1)S(1)} collective-permute-done((bf16[256,1024]{1,0:T(8,128)(2,1)S(1)}, bf16[256,1024]{1,0:T(8,128)(2,1)S(1)}, u32[]{:S(2)}, u32[]{:S(2)}) %collective-permute-start.7) | collective-permute-done | bytes 524320 | tf_op jit(solution)/shard_map/ppermute | solution.py:14
  77.3 1.9 collective-permute-start.8
  80.5 9.0 %collective-permute-done.2 = bf16[256,1024]{1,0:T(8,128)(2,1)S(1)} collective-permute-done((bf16[256,1024]{1,0:T(8,128)(2,1)S(1)}, bf16[256,1024]{1,0:T(8,128)(2,1)S(1)}, u32[]{:S(2)}, u32[]{:S(2)}) %collective-permute-start.2) | collective-permute-done | bytes 524320 | tf_op jit(solution)/shard_map/ppermute | solution.py:14
  89.5 1.9 collective-permute-start.3
  91.4 9.2 %collective-permute-done.8 = bf16[256,1024]{1,0:T(8,128)(2,1)S(1)} collective-permute-done((bf16[256,1024]{1,0:T(8,128)(2,1)S(1)}, bf16[256,1024]{1,0:T(8,128)(2,1)S(1)}, u32[]{:S(2)}, u32[]{:S(2)}) %collective-permute-start.8) | collective-permute-done | bytes 524320 | tf_op jit(solution)/shard_map/ppermute | solution.py:14
  100.7 1.9 collective-permute-start.9
  104.0 8.0 collective-permute-done.3
  112.0 1.9 collective-permute-start.4
  113.9 10.6 %collective-permute-done.9 = bf16[256,1024]{1,0:T(8,128)(2,1)S(1)} collective-permute-done((bf16[256,1024]{1,0:T(8,128)(2,1)S(1)}, bf16[256,1024]{1,0:T(8,128)(2,1)S(1)}, u32[]{:S(2)}, u32[]{:S(2)}) %collective-permute-start.9) | collective-permute-done | bytes 524320 | tf_op jit(solution)/shard_map/ppermute | solution.py:14
  124.5 1.9 collective-permute-start.10
  127.8 8.1 %collective-permute-done.4 = bf16[256,1024]{1,0:T(8,128)(2,1)S(1)} collective-permute-done((bf16[256,1024]{1,0:T(8,128)(2,1)S(1)}, bf16[256,1024]{1,0:T(8,128)(2,1)S(1)}, u32[]{:S(2)}, u32[]{:S(2)}) %collective-permute-start.4) | collective-permute-done | bytes 524320 | tf_op jit(solution)/shard_map/ppermute | solution.py:14
  136.0 4.8 collective-permute-start.5
  140.8 6.3 collective-permute-done.10
  147.2 4.8 collective-permute-start.11
  154.6 4.5 collective-permute-done.5
  159.2 7.7 collective-permute-start.6
  167.0 6.2 collective-permute-start.12
  173.3 66.2 %all-gather.3.cloned.1.call-done = bf16[256,4096]{1,0:T(8,128)(2,1)} async-done(((bf16[256,1024]{1,0:T(8,128)(2,1)}), bf16[256,4096]{1,0:T(8,128)(2,1)}) %all-gather.3.cloned.1.call-update) | async-done | bytes 2097168 | tf_op jit(solution)/shard_map/all_gather | solution.py:26
  239.5 493.1 %all-gather.5.cloned.1.call-done = bf16[4096,1024]{1,0:T(8,128)(2,1)} async-done(((bf16[32,1024]{1,0:T(8,128)(2,1)}), bf16[4096,1024]{1,0:T(8,128)(2,1)}) %all-gather.5.cloned.1.call-update) | async-done | bytes 8388624 | tf_op jit(solution)/shard_map/all_gather | solution.py:29
  732.5 6.3 convolution_convert_fusion
  738.9 1.0 convolution_convert_fusion.2
  739.9 1.0 convolution_convert_fusion.1
  740.9 54.2 %all-reduce.3.cloned.1.call-done = (bf16[256,256]{1,0:T(8,128)(2,1)}, bf16[256,256]{1,0:T(8,128)(2,1)}) async-done(((bf16[256,256]{1,0:T(8,128)(2,1)}, bf16[256,256]{1,0:T(8,128)(2,1)}), (bf16[256,256]{1,0:T(8,128)(2,1)}, bf16[256,256]{1,0:T(8,128)(2,1)})) %all-reduce.3.cloned.1.call-update) | async-done | bytes 262160 | tf_op jit(solution)/shard_map/psum | solution.py:41
  795.1 1.0 multiply_bitcast_fusion
  796.1 0.8 pad_maximum_fusion
  (20 shorter events, 2.2 us)
Async XLA Ops:
  6.5 232.9 %all-gather.3.cloned.1.call-start = ((), (), s32[]{:S(2)}) async-start(), calls=%async_computation | async-start | bytes 2621440 | tf_op jit(solution)/shard_map/all_gather | solution.py:26
  7.3 725.3 %all-gather.5.cloned.1.call-start = ((), (), s32[]{:S(2)}) async-start(), calls=%async_computation.1 | async-start | bytes 8454144 | tf_op jit(solution)/shard_map/all_gather | solution.py:29
  8.0 787.1 %all-reduce.3.cloned.1.call-start = ((), (), s32[]{:S(2)}) async-start(), calls=%async_computation.2 | async-start | bytes 524288 | tf_op jit(solution)/shard_map/psum | solution.py:41
  8.1 11.6 %collective-permute-start = (bf16[256,1024]{1,0:T(8,128)(2,1)}, bf16[256,1024]{1,0:T(8,128)(2,1)S(1)}, u32[]{:S(2)}, u32[]{:S(2)}) collective-permute-start(bf16[256,1024]{1,0:T(8,128)(2,1)} %param.3), channel_id=1, source_target_pairs={{0,508},{4,0},{8,4},{12,8},{16,12},{20,16},{24,20},{28,24},{32,28}... | collective-permute-start | bytes 1572872 | tf_op jit(solution)/shard_map/ppermute | solution.py:14
  20.7 44.8 %collective-permute-start.1 = (bf16[256,1024]{1,0:T(8,128)(2,1)S(1)}, bf16[256,1024]{1,0:T(8,128)(2,1)S(1)}, u32[]{:S(2)}, u32[]{:S(2)}) collective-permute-start(bf16[256,1024]{1,0:T(8,128)(2,1)S(1)} %get-tuple-element.7), channel_id=1, source_target_pairs={{0,504},{4,508},{8,0},{12,4},{16,8},{20,12},{24,16},{28,20},{32,24... | collective-permute-start | bytes 1572872 | tf_op jit(solution)/shard_map/ppermute | solution.py:14
  53.7 23.5 %collective-permute-start.7 = (bf16[256,1024]{1,0:T(8,128)(2,1)S(1)}, bf16[256,1024]{1,0:T(8,128)(2,1)S(1)}, u32[]{:S(2)}, u32[]{:S(2)}) collective-permute-start(bf16[256,1024]{1,0:T(8,128)(2,1)S(1)} %get-tuple-element.8), channel_id=1, source_target_pairs={{0,504},{4,508},{8,0},{12,4},{16,8},{20,12},{24,16},{28,20},{32,24... | collective-permute-start | bytes 1572872 | tf_op jit(solution)/shard_map/ppermute | solution.py:14
  65.6 23.8 %collective-permute-start.2 = (bf16[256,1024]{1,0:T(8,128)(2,1)S(1)}, bf16[256,1024]{1,0:T(8,128)(2,1)S(1)}, u32[]{:S(2)}, u32[]{:S(2)}) collective-permute-start(bf16[256,1024]{1,0:T(8,128)(2,1)S(1)} %broadcast_select_fusion.7), channel_id=1, source_target_pairs={{0,496},{4,500},{8,504},{12,508},{16,0},{20,4},{24,8},{28,12},{32,... | collective-permute-start | bytes 1572872 | tf_op jit(solution)/shard_map/ppermute | solution.py:14
  77.3 23.4 %collective-permute-start.8 = (bf16[256,1024]{1,0:T(8,128)(2,1)S(1)}, bf16[256,1024]{1,0:T(8,128)(2,1)S(1)}, u32[]{:S(2)}, u32[]{:S(2)}) collective-permute-start(bf16[256,1024]{1,0:T(8,128)(2,1)S(1)} %broadcast_select_fusion.1), channel_id=1, source_target_pairs={{0,496},{4,500},{8,504},{12,508},{16,0},{20,4},{24,8},{28,12},{32,... | collective-permute-start | bytes 1572872 | tf_op jit(solution)/shard_map/ppermute | solution.py:14
  89.5 22.4 %collective-permute-start.3 = (bf16[256,1024]{1,0:T(8,128)(2,1)S(1)}, bf16[256,1024]{1,0:T(8,128)(2,1)S(1)}, u32[]{:S(2)}, u32[]{:S(2)}) collective-permute-start(bf16[256,1024]{1,0:T(8,128)(2,1)S(1)} %broadcast_select_fusion.8), channel_id=1, source_target_pairs={{0,480},{4,484},{8,488},{12,492},{16,496},{20,500},{24,504},{28,50... | collective-permute-start | bytes 1572872 | tf_op jit(solution)/shard_map/ppermute | solution.py:14
  100.7 23.7 %collective-permute-start.9 = (bf16[256,1024]{1,0:T(8,128)(2,1)S(1)}, bf16[256,1024]{1,0:T(8,128)(2,1)S(1)}, u32[]{:S(2)}, u32[]{:S(2)}) collective-permute-start(bf16[256,1024]{1,0:T(8,128)(2,1)S(1)} %broadcast_select_fusion.2), channel_id=1, source_target_pairs={{0,480},{4,484},{8,488},{12,492},{16,496},{20,500},{24,504},{28,50... | collective-permute-start | bytes 1572872 | tf_op jit(solution)/shard_map/ppermute | solution.py:14
  112.0 23.9 %collective-permute-start.4 = (bf16[256,1024]{1,0:T(8,128)(2,1)S(1)}, bf16[256,1024]{1,0:T(8,128)(2,1)S(1)}, u32[]{:S(2)}, u32[]{:S(2)}) collective-permute-start(bf16[256,1024]{1,0:T(8,128)(2,1)S(1)} %broadcast_select_fusion.9), channel_id=1, source_target_pairs={{0,448},{4,452},{8,456},{12,460},{16,464},{20,468},{24,472},{28,47... | collective-permute-start | bytes 1572872 | tf_op jit(solution)/shard_map/ppermute | solution.py:14
  124.5 22.6 %collective-permute-start.10 = (bf16[256,1024]{1,0:T(8,128)(2,1)S(1)}, bf16[256,1024]{1,0:T(8,128)(2,1)S(1)}, u32[]{:S(2)}, u32[]{:S(2)}) collective-permute-start(bf16[256,1024]{1,0:T(8,128)(2,1)S(1)} %broadcast_select_fusion.3), channel_id=1, source_target_pairs={{0,448},{4,452},{8,456},{12,460},{16,464},{20,468},{24,472},{28,47... | collective-permute-start | bytes 1572872 | tf_op jit(solution)/shard_map/ppermute | solution.py:14
  136.0 23.2 %collective-permute-start.5 = (bf16[256,1024]{1,0:T(8,128)(2,1)S(1)}, bf16[256,1024]{1,0:T(8,128)(2,1)S(1)}, u32[]{:S(2)}, u32[]{:S(2)}) collective-permute-start(bf16[256,1024]{1,0:T(8,128)(2,1)S(1)} %broadcast_select_fusion.10), channel_id=1, source_target_pairs={{0,384},{4,388},{8,392},{12,396},{16,400},{20,404},{24,408},{28,41... | collective-permute-start | bytes 1572872 | tf_op jit(solution)/shard_map/ppermute | solution.py:14
  147.2 19.7 %collective-permute-start.11 = (bf16[256,1024]{1,0:T(8,128)(2,1)S(1)}, bf16[256,1024]{1,0:T(8,128)(2,1)S(1)}, u32[]{:S(2)}, u32[]{:S(2)}) collective-permute-start(bf16[256,1024]{1,0:T(8,128)(2,1)S(1)} %broadcast_select_fusion.4), channel_id=1, source_target_pairs={{0,384},{4,388},{8,392},{12,396},{16,400},{20,404},{24,408},{28,41... | collective-permute-start | bytes 1572872 | tf_op jit(solution)/shard_map/ppermute | solution.py:14
  159.2 579.7 %collective-permute-start.6 = (bf16[256,1024]{1,0:T(8,128)(2,1)S(1)}, bf16[256,1024]{1,0:T(8,128)(2,1)S(1)}, u32[]{:S(2)}, u32[]{:S(2)}) collective-permute-start(bf16[256,1024]{1,0:T(8,128)(2,1)S(1)} %broadcast_select_fusion.11), channel_id=1, source_target_pairs={{0,256},{4,260},{8,264},{12,268},{16,272},{20,276},{24,280},{28,28... | collective-permute-start | bytes 1572872 | tf_op jit(solution)/shard_map/ppermute | solution.py:14
  167.0 572.9 %collective-permute-start.12 = (bf16[256,1024]{1,0:T(8,128)(2,1)S(1)}, bf16[256,1024]{1,0:T(8,128)(2,1)S(1)}, u32[]{:S(2)}, u32[]{:S(2)}) collective-permute-start(bf16[256,1024]{1,0:T(8,128)(2,1)S(1)} %broadcast_select_fusion.5), channel_id=1, source_target_pairs={{0,256},{4,260},{8,264},{12,268},{16,272},{20,276},{24,280},{28,28... | collective-permute-start | bytes 1572872 | tf_op jit(solution)/shard_map/ppermute | solution.py:14
Sparse Core Ops, SparseCore 0:
  9.5 229.9 all-gather.2
  243.7 488.7 all-gather.4
  741.1 54.0 all-reduce.2
where the time goes:
time: 805 us; the launch traced here: 804 us
  waiting for transfers between devices  689 us (86%)
  starting transfers between devices  78.9 us (10%)
  between operations  22.3 us (3%)
  matrix products  8.37 us (1%)
    all_gather x1, waiting for transfers between devices, on_device(): lax.all_gather(precond, 'docs', axis=0, tiled=True)  493 us
    ppermute x13, starting transfers between devices, shifted(): lax.ppermute(value, axis, [(i, (i + by) % size) for i in range(size)])  78.8 us
    ppermute x13, waiting for transfers between devices, shifted(): lax.ppermute(value, axis, [(i, (i + by) % size) for i in range(size)])  74.2 us
    all_gather x1, waiting for transfers between devices, on_device(): whole = lax.all_gather(grads, 'proj', axis=1, tiled=True)  66.2 us
    psum x1, waiting for transfers between devices, on_device(): lax.psum(partial_gram.astype(jnp.bfloat16), 'proj').astype(jnp.float32)  54.2 us
  transfers between devices with their start and end apart: 16, of which 13 were waited for; matrix products, arithmetic and copies ran while one was open for 1% of the time, Pallas kernels for 0%

commit v1 on v0

v1 whole, which is shorter than its diff:
```python
import math

import jax
import jax.numpy as jnp
from jax import lax
from jax.sharding import PartitionSpec as P

K = 4096
ROUNDS = 2
BOTH = ("docs", "proj")


def place(index):
    docs, p = divmod(index, 4)
    return docs >> 5, docs >> 3 & 3, docs >> 1 & 3, docs & 1, p


def number(zh, y, x, c, p):
    return ((zh % 4 * 4 + y % 4) * 4 + x % 4) * 8 + c % 2 * 4 + p % 4


def send(value, to):
    return lax.ppermute(value, BOTH, [(i, number(*to(*place(i)))) for i in range(512)])


def put(buffer, piece, at):
    return lax.dynamic_update_slice(
        buffer, piece[None], (at,) + (0,) * (buffer.ndim - 1)
    )


def gather4(value, mine, move):
    out = jnp.zeros((4,) + value.shape, value.dtype)
    out = put(out, value, mine)
    for t in (1, 2, 3):
        out = put(out, send(value, lambda *at: move(t, *at)), (mine - t) % 4)
    return out


def gather_precond(own):
    docs = lax.axis_index("docs")
    zh, y, x, c = docs >> 5, docs >> 3 & 3, docs >> 1 & 3, docs & 1
    held = gather4(own, zh, lambda t, zh, y, x, c, p: (zh + t, y, x, c, p))
    held = gather4(
        held,
        jnp.where(c == 0, y, x),
        lambda t, zh, y, x, c, p: (zh, y + t * (1 - c), x + t * c, c, p),
    )
    held = gather4(
        held,
        jnp.where(c == 0, x, y),
        lambda t, zh, y, x, c, p: (zh, y + t * c, x + t * (1 - c), c, p),
    )
    other = send(held, lambda zh, y, x, c, p: (zh, y, x, c ^ 1, p))
    first = jnp.where(c == 0, held, other).transpose(2, 1, 0, 3, 4)
    second = jnp.where(c == 0, other, held).transpose(2, 0, 1, 3, 4)
    return jnp.stack([first, second], axis=3).reshape(4096, own.shape[1])


def gather_grads(own):
    p = lax.axis_index("proj")
    parts = gather4(own, p, lambda t, zh, y, x, c, p: (zh, y, x, c, p + t))
    return [parts[i] for i in range(4)]


def sum_over_proj(part):
    p = lax.axis_index("proj")
    low = part.astype(jnp.bfloat16)

    def pick(array, at):
        return lax.dynamic_index_in_dim(array, at % 4, 0, keepdims=False)

    total = pick(part, p)
    for t in (1, 2, 3):
        got = send(pick(low, p + t), lambda zh, y, x, c, p: (zh, y, x, c, p + t))
        total = total + got.astype(jnp.float32)
    return gather4(
        total.astype(jnp.bfloat16), p, lambda t, zh, y, x, c, p: (zh, y, x, c, p + t)
    ).astype(jnp.float32)


def shifted(value, axis, by):
    size = lax.axis_size(axis)
    return lax.ppermute(value, axis, [(i, (i + by) % size) for i in range(size)])


def fetch_every(block, offset, bits_total):
    current = block
    for bit in range(bits_total):
        moved = shifted(current, "docs", -(1 << bit))
        current = jnp.where(offset >> bit & 1 == 1, moved, current)
    return current


def on_device(grads, precond, offsets):
    columns = gather_precond(precond)
    slabs = gather_grads(grads)
    pre = sum(
        jnp.dot(
            slabs[i],
            columns[i * 1024 : (i + 1) * 1024],
            preferred_element_type=jnp.float32,
        )
        for i in range(4)
    ).astype(jnp.bfloat16)
    factor = jnp.float32(1.0 / math.sqrt(K))
    bits_total = (lax.axis_size("docs") - 1).bit_length()
    grams = []
    for step in range(ROUNDS):
        partner = fetch_every(grads, offsets[step], bits_total)
        grams.append(
            lax.dot_general(
                pre, partner, (((1,), (1,)), ((), ())), preferred_element_type=jnp.float32
            )
        )
    whole = sum_over_proj(jnp.stack(grams).reshape(4, 128, 256))
    return whole.reshape(2, 256, 256) * factor


def solution(mesh):
    placed = (P("docs", "proj"), P("docs", "proj"), P())
    return jax.shard_map(
        on_device, mesh=mesh, in_specs=placed, out_specs=P(None, "docs", None), check_vma=False
    )
```

time: 805 us -> 732 us (0.909)
  waiting for transfers between devices: 689 us -> 421 us
  starting transfers between devices: 78.9 us -> 268 us
  between operations: 22.3 us -> 9.87 us
  local copies, waits for them, and re-layouts: 1.34 us -> 12.3 us
    all_gather x2 -> x0, waiting for transfers between devices: 559 us -> none  [the longest x1 493 us: on_device(): lax.all_gather(precond, 'docs', axis=0, tiled=True)]
    ppermute x13, waiting for transfers between devices: 74.2 us -> 257 us  [shifted(): lax.ppermute(value, axis, [(i, (i + by) % size) for i in range(size)])]
    ppermute x0 -> x19, starting transfers between devices: none -> 166 us  [send(): lax.ppermute(value, BOTH, [(i, number(*to(*place(i)))) for i in range(512)])]
    ppermute x0 -> x19, waiting for transfers between devices: none -> 165 us  [send(): lax.ppermute(value, BOTH, [(i, number(*to(*place(i)))) for i in range(512)])]
    psum x1 -> x0, waiting for transfers between devices: 54.2 us -> none  [on_device(): lax.psum(partial_gram.astype(jnp.bfloat16), 'proj').astype(jnp.float32)]
    ppermute x13, starting transfers between devices: 78.8 us -> 102 us  [shifted(): lax.ppermute(value, axis, [(i, (i + by) % size) for i in range(size)])]
    dynamic_update_slice x0 -> x19, local copies, waits for them, and re-layouts: none -> 8.68 us  [put(): lax.dynamic_update_slice(buffer, piece[None], (at,) + (0,) * (buffer.ndim...]
  transfers between devices with their start and end apart: 16 -> 32, of which waited for: 13 -> 17; matrix products, arithmetic and copies ran while one was open for 1% -> 3% of each run, Pallas kernels for 0% -> 0%
where the time goes in v1:
time: 732 us; the launch traced here: 724 us
  waiting for transfers between devices  421 us (58%)
  starting transfers between devices  268 us (37%)
  local copies, waits for them, and re-layouts  12.3 us (2%)
  between operations  9.87 us (1%)
  other arithmetic  8.76 us (1%)
    ppermute x13, waiting for transfers between devices, shifted(): lax.ppermute(value, axis, [(i, (i + by) % size) for i in range(size)])  257 us
    ppermute x19, starting transfers between devices, send(): lax.ppermute(value, BOTH, [(i, number(*to(*place(i)))) for i in range(512)])  166 us
    ppermute x19, waiting for transfers between devices, send(): lax.ppermute(value, BOTH, [(i, number(*to(*place(i)))) for i in range(512)])  165 us
    ppermute x13, starting transfers between devices, shifted(): lax.ppermute(value, axis, [(i, (i + by) % size) for i in range(size)])  102 us
  transfers between devices with their start and end apart: 32, of which 17 were waited for; matrix products, arithmetic and copies ran while one was open for 3% of the time, Pallas kernels for 0%

profile of v1, /device:TPU:1, one launch (start us, length us, event | category | flops | bytes accessed | tf_op | source)
XLA Modules:
  0.0 724.1 jit_solution(14267059614065632265)
XLA Ops:
  0.0 9.6 %collective-permute-start.3 = (bf16[32,1024]{1,0:T(8,128)(2,1)}, bf16[32,1024]{1,0:T(8,128)(2,1)S(1)}, u32[]{:S(2)}, u32[]{:S(2)}) collective-permute-start(bf16[32,1024]{1,0:T(8,128)(2,1)} %param.4), channel_id=1, source_target_pairs={{0,128},{1,129},{2,130},{3,131},{4,132},{5,133},{6,134},{7,135},{8... | collective-permute-start | bytes 196616 | tf_op jit(solution)/shard_map/ppermute | solution.py:23
  9.6 10.6 %collective-permute-start.4 = (bf16[32,1024]{1,0:T(8,128)(2,1)}, bf16[32,1024]{1,0:T(8,128)(2,1)S(1)}, u32[]{:S(2)}, u32[]{:S(2)}) collective-permute-start(bf16[32,1024]{1,0:T(8,128)(2,1)} %param.4), channel_id=1, source_target_pairs={{0,256},{1,257},{2,258},{3,259},{4,260},{5,261},{6,262},{7,263},{8... | collective-permute-start | bytes 196616 | tf_op jit(solution)/shard_map/ppermute | solution.py:23
  20.3 5.2 collective-permute-start.5
  27.7 6.9 collective-permute-done.5
  34.6 3.1 collective-permute-start.6
  37.8 4.4 collective-permute-start.7
  42.1 3.1 collective-permute-start.8
  49.6 3.2 collective-permute-start.9
  52.8 4.3 collective-permute-start.13
  57.1 3.3 collective-permute-start.10
  62.4 3.7 collective-permute-start.11
  66.1 2.6 broadcast_in_dim.81
  71.0 34.9 %collective-permute-start.20 = (bf16[256,1024]{1,0:T(8,128)(2,1)S(1)}, bf16[256,1024]{1,0:T(8,128)(2,1)S(1)}, u32[]{:S(2)}, u32[]{:S(2)}) collective-permute-start(bf16[256,1024]{1,0:T(8,128)(2,1)S(1)} %get-tuple-element.14), channel_id=1, source_target_pairs={{0,504},{4,508},{8,0},{12,4},{16,8},{20,12},{24,16},{28,20},{32,24... | collective-permute-start | bytes 1572872 | tf_op jit(solution)/shard_map/ppermute | solution.py:84
  114.3 46.4 %collective-permute-done.20 = bf16[256,1024]{1,0:T(8,128)(2,1)S(1)} collective-permute-done((bf16[256,1024]{1,0:T(8,128)(2,1)S(1)}, bf16[256,1024]{1,0:T(8,128)(2,1)S(1)}, u32[]{:S(2)}, u32[]{:S(2)}) %collective-permute-start.20) | collective-permute-done | bytes 524320 | tf_op jit(solution)/shard_map/ppermute | solution.py:84
  162.8 51.1 %collective-permute-done.14 = bf16[256,1024]{1,0:T(8,128)(2,1)S(1)} collective-permute-done((bf16[256,1024]{1,0:T(8,128)(2,1)S(1)}, bf16[256,1024]{1,0:T(8,128)(2,1)S(1)}, u32[]{:S(2)}, u32[]{:S(2)}) %collective-permute-start.14) | collective-permute-done | bytes 524320 | tf_op jit(solution)/shard_map/ppermute | solution.py:84
  217.1 50.1 %collective-permute-done.21 = bf16[256,1024]{1,0:T(8,128)(2,1)S(1)} collective-permute-done((bf16[256,1024]{1,0:T(8,128)(2,1)S(1)}, bf16[256,1024]{1,0:T(8,128)(2,1)S(1)}, u32[]{:S(2)}, u32[]{:S(2)}) %collective-permute-start.21) | collective-permute-done | bytes 524320 | tf_op jit(solution)/shard_map/ppermute | solution.py:84
  269.2 47.2 %collective-permute-done.15 = bf16[256,1024]{1,0:T(8,128)(2,1)S(1)} collective-permute-done((bf16[256,1024]{1,0:T(8,128)(2,1)S(1)}, bf16[256,1024]{1,0:T(8,128)(2,1)S(1)}, u32[]{:S(2)}, u32[]{:S(2)}) %collective-permute-start.15) | collective-permute-done | bytes 524320 | tf_op jit(solution)/shard_map/ppermute | solution.py:84
  323.5 20.7 %collective-permute-done.22 = bf16[256,1024]{1,0:T(8,128)(2,1)S(1)} collective-permute-done((bf16[256,1024]{1,0:T(8,128)(2,1)S(1)}, bf16[256,1024]{1,0:T(8,128)(2,1)S(1)}, u32[]{:S(2)}, u32[]{:S(2)}) %collective-permute-start.22) | collective-permute-done | bytes 524320 | tf_op jit(solution)/shard_map/ppermute | solution.py:84
  346.2 25.2 %collective-permute-done.16 = bf16[256,1024]{1,0:T(8,128)(2,1)S(1)} collective-permute-done((bf16[256,1024]{1,0:T(8,128)(2,1)S(1)}, bf16[256,1024]{1,0:T(8,128)(2,1)S(1)}, u32[]{:S(2)}, u32[]{:S(2)}) %collective-permute-start.16) | collective-permute-done | bytes 524320 | tf_op jit(solution)/shard_map/ppermute | solution.py:84
  378.7 34.4 %collective-permute-done = bf16[256,1024]{1,0:T(8,128)(2,1)} collective-permute-done((bf16[256,1024]{1,0:T(8,128)(2,1)}, bf16[256,1024]{1,0:T(8,128)(2,1)}, u32[]{:S(2)}, u32[]{:S(2)}) %collective-permute-start) | collective-permute-done | bytes 524320 | tf_op jit(solution)/shard_map/ppermute | solution.py:23
  416.1 6.3 collective-permute-start.24
  423.5 10.0 %collective-permute-start.18 = (bf16[256,1024]{1,0:T(8,128)(2,1)S(1)}, bf16[256,1024]{1,0:T(8,128)(2,1)S(1)}, u32[]{:S(2)}, u32[]{:S(2)}) collective-permute-start(bf16[256,1024]{1,0:T(8,128)(2,1)S(1)} %broadcast_select_fusion.10), channel_id=1, source_target_pairs={{0,384},{4,388},{8,392},{12,396},{16,400},{20,404},{24,408},{28,41... | collective-permute-start | bytes 1572872 | tf_op jit(solution)/shard_map/ppermute | solution.py:84
  433.5 47.0 %collective-permute-done.1 = bf16[256,1024]{1,0:T(8,128)(2,1)} collective-permute-done((bf16[256,1024]{1,0:T(8,128)(2,1)}, bf16[256,1024]{1,0:T(8,128)(2,1)}, u32[]{:S(2)}, u32[]{:S(2)}) %collective-permute-start.1) | collective-permute-done | bytes 524320 | tf_op jit(solution)/shard_map/ppermute | solution.py:23
  481.6 65.2 %collective-permute-done.2 = bf16[256,1024]{1,0:T(8,128)(2,1)S(1)} collective-permute-done((bf16[256,1024]{1,0:T(8,128)(2,1)}, bf16[256,1024]{1,0:T(8,128)(2,1)S(1)}, u32[]{:S(2)}, u32[]{:S(2)}) %collective-permute-start.2) | collective-permute-done | bytes 524320 | tf_op jit(solution)/shard_map/ppermute | solution.py:23
  547.0 31.6 %collective-permute-start.25 = (bf16[256,1024]{1,0:T(8,128)(2,1)S(1)}, bf16[256,1024]{1,0:T(8,128)(2,1)S(1)}, u32[]{:S(2)}, u32[]{:S(2)}) collective-permute-start(bf16[256,1024]{1,0:T(8,128)(2,1)S(1)} %broadcast_select_fusion.5), channel_id=1, source_target_pairs={{0,256},{4,260},{8,264},{12,268},{16,272},{20,276},{24,280},{28,28... | collective-permute-start | bytes 1572872 | tf_op jit(solution)/shard_map/ppermute | solution.py:84
  580.6 3.8 select_bitcast_fusion.1
  588.5 6.6 collective-permute-done.25
  595.5 9.5 %collective-permute-done.19 = bf16[256,1024]{1,0:T(8,128)(2,1)S(1)} collective-permute-done((bf16[256,1024]{1,0:T(8,128)(2,1)S(1)}, bf16[256,1024]{1,0:T(8,128)(2,1)S(1)}, u32[]{:S(2)}, u32[]{:S(2)}) %collective-permute-start.19) | collective-permute-done | bytes 524320 | tf_op jit(solution)/shard_map/ppermute | solution.py:84
  607.4 97.4 %collective-permute-start.27 = (bf16[128,256]{1,0:T(8,128)(2,1)S(1)}, bf16[128,256]{1,0:T(8,128)(2,1)S(1)}, u32[]{:S(2)}, u32[]{:S(2)}) collective-permute-start(bf16[128,256]{1,0:T(8,128)(2,1)S(1)} %get-tuple-element.17), channel_id=1, source_target_pairs={{0,2},{1,3},{2,0},{3,1},{4,6},{5,7},{6,4},{7,5},{8,10},{9,11},{10,... | collective-permute-start | bytes 196616 | tf_op jit(solution)/shard_map/ppermute | solution.py:23
  704.9 3.4 collective-permute-start.26
  708.3 3.4 collective-permute-done.26
  715.6 5.1 collective-permute-start.31
  (83 shorter events, 55.0 us)
Async XLA Ops:
  0.0 26.4 %collective-permute-start.3 = (bf16[32,1024]{1,0:T(8,128)(2,1)}, bf16[32,1024]{1,0:T(8,128)(2,1)S(1)}, u32[]{:S(2)}, u32[]{:S(2)}) collective-permute-start(bf16[32,1024]{1,0:T(8,128)(2,1)} %param.4), channel_id=1, source_target_pairs={{0,128},{1,129},{2,130},{3,131},{4,132},{5,133},{6,134},{7,135},{8... | collective-permute-start | bytes 196616 | tf_op jit(solution)/shard_map/ppermute | solution.py:23
  9.6 18.0 %collective-permute-start.4 = (bf16[32,1024]{1,0:T(8,128)(2,1)}, bf16[32,1024]{1,0:T(8,128)(2,1)S(1)}, u32[]{:S(2)}, u32[]{:S(2)}) collective-permute-start(bf16[32,1024]{1,0:T(8,128)(2,1)} %param.4), channel_id=1, source_target_pairs={{0,256},{1,257},{2,258},{3,259},{4,260},{5,261},{6,262},{7,263},{8... | collective-permute-start | bytes 196616 | tf_op jit(solution)/shard_map/ppermute | solution.py:23
  20.3 14.3 %collective-permute-start.5 = (bf16[32,1024]{1,0:T(8,128)(2,1)}, bf16[32,1024]{1,0:T(8,128)(2,1)S(1)}, u32[]{:S(2)}, u32[]{:S(2)}) collective-permute-start(bf16[32,1024]{1,0:T(8,128)(2,1)} %param.4), channel_id=1, source_target_pairs={{0,384},{1,385},{2,386},{3,387},{4,388},{5,389},{6,390},{7,391},{8... | collective-permute-start | bytes 196616 | tf_op jit(solution)/shard_map/ppermute | solution.py:23
  34.6 10.8 %collective-permute-start.6 = (bf16[4,32,1024]{2,1,0:T(8,128)(2,1)S(1)}, bf16[4,32,1024]{2,1,0:T(8,128)(2,1)S(1)}, u32[]{:S(2)}, u32[]{:S(2)}) collective-permute-start(bf16[4,32,1024]{2,1,0:T(8,128)(2,1)S(1)} %bitcast_dynamic-update-slice_fusion.16), channel_id=1, source_target_pairs={{0,32},{1,33},{2,34},{3,35},{4,12},{5,13},{6,14},{7,15},{8,40},{9,... | collective-permute-start | bytes 786440 | tf_op jit(solution)/shard_map/ppermute | solution.py:23
  37.8 9.2 %collective-permute-start.7 = (bf16[4,32,1024]{2,1,0:T(8,128)(2,1)S(1)}, bf16[4,32,1024]{2,1,0:T(8,128)(2,1)S(1)}, u32[]{:S(2)}, u32[]{:S(2)}) collective-permute-start(bf16[4,32,1024]{2,1,0:T(8,128)(2,1)S(1)} %bitcast_dynamic-update-slice_fusion.16), channel_id=1, source_target_pairs={{0,64},{1,65},{2,66},{3,67},{4,20},{5,21},{6,22},{7,23},{8,72},{9,... | collective-permute-start | bytes 786440 | tf_op jit(solution)/shard_map/ppermute | solution.py:23
  42.1 7.4 %collective-permute-start.8 = (bf16[4,32,1024]{2,1,0:T(8,128)(2,1)S(1)}, bf16[4,32,1024]{2,1,0:T(8,128)(2,1)S(1)}, u32[]{:S(2)}, u32[]{:S(2)}) collective-permute-start(bf16[4,32,1024]{2,1,0:T(8,128)(2,1)S(1)} %bitcast_dynamic-update-slice_fusion.16), channel_id=1, source_target_pairs={{0,96},{1,97},{2,98},{3,99},{4,28},{5,29},{6,30},{7,31},{8,104},{9... | collective-permute-start | bytes 786440 | tf_op jit(solution)/shard_map/ppermute | solution.py:23
  49.6 58.3 %collective-permute-start.9 = (bf16[4,4,32,1024]{3,2,0,1:T(8,128)(2,1)S(1)}, bf16[4,4,32,1024]{3,2,0,1:T(8,128)(2,1)S(1)}, u32[]{:S(2)}, u32[]{:S(2)}) collective-permute-start(bf16[4,4,32,1024]{3,2,0,1:T(8,128)(2,1)S(1)} %bitcast_dynamic-update-slice_fusion.11), channel_id=1, source_target_pairs={{0,8},{1,9},{2,10},{3,11},{4,36},{5,37},{6,38},{7,39},{8,16},{9,17... | collective-permute-start | bytes 3145736 | tf_op jit(solution)/shard_map/ppermute | solution.py:23
  52.8 17.0 %collective-permute-start.13 = (bf16[256,1024]{1,0:T(8,128)(2,1)}, bf16[256,1024]{1,0:T(8,128)(2,1)}, u32[]{:S(2)}, u32[]{:S(2)}) collective-permute-start(bf16[256,1024]{1,0:T(8,128)(2,1)} %param.3), channel_id=1, source_target_pairs={{0,508},{4,0},{8,4},{12,8},{16,12},{20,16},{24,20},{28,24},{32,28}... | collective-permute-start | bytes 1572872 | tf_op jit(solution)/shard_map/ppermute | solution.py:84
  57.1 51.8 %collective-permute-start.10 = (bf16[4,4,32,1024]{3,2,0,1:T(8,128)(2,1)S(1)}, bf16[4,4,32,1024]{3,2,0,1:T(8,128)(2,1)S(1)}, u32[]{:S(2)}, u32[]{:S(2)}) collective-permute-start(bf16[4,4,32,1024]{3,2,0,1:T(8,128)(2,1)S(1)} %bitcast_dynamic-update-slice_fusion.11), channel_id=1, source_target_pairs={{0,16},{1,17},{2,18},{3,19},{4,68},{5,69},{6,70},{7,71},{8,24},{9,... | collective-permute-start | bytes 3145736 | tf_op jit(solution)/shard_map/ppermute | solution.py:23
  62.4 47.7 %collective-permute-start.11 = (bf16[4,4,32,1024]{3,2,0,1:T(8,128)(2,1)S(1)}, bf16[4,4,32,1024]{3,2,0,1:T(8,128)(2,1)S(1)}, u32[]{:S(2)}, u32[]{:S(2)}) collective-permute-start(bf16[4,4,32,1024]{3,2,0,1:T(8,128)(2,1)S(1)} %bitcast_dynamic-update-slice_fusion.11), channel_id=1, source_target_pairs={{0,24},{1,25},{2,26},{3,27},{4,100},{5,101},{6,102},{7,103},{8,0},... | collective-permute-start | bytes 3145736 | tf_op jit(solution)/shard_map/ppermute | solution.py:23
  71.0 89.8 %collective-permute-start.20 = (bf16[256,1024]{1,0:T(8,128)(2,1)S(1)}, bf16[256,1024]{1,0:T(8,128)(2,1)S(1)}, u32[]{:S(2)}, u32[]{:S(2)}) collective-permute-start(bf16[256,1024]{1,0:T(8,128)(2,1)S(1)} %get-tuple-element.14), channel_id=1, source_target_pairs={{0,504},{4,508},{8,0},{12,4},{16,8},{20,12},{24,16},{28,20},{32,24... | collective-permute-start | bytes 1572872 | tf_op jit(solution)/shard_map/ppermute | solution.py:84
  105.9 108.0 %collective-permute-start.14 = (bf16[256,1024]{1,0:T(8,128)(2,1)S(1)}, bf16[256,1024]{1,0:T(8,128)(2,1)S(1)}, u32[]{:S(2)}, u32[]{:S(2)}) collective-permute-start(bf16[256,1024]{1,0:T(8,128)(2,1)S(1)} %get-tuple-element.13), channel_id=1, source_target_pairs={{0,504},{4,508},{8,0},{12,4},{16,8},{20,12},{24,16},{28,20},{32,24... | collective-permute-start | bytes 1572872 | tf_op jit(solution)/shard_map/ppermute | solution.py:84
  111.1 469.5 %collective-permute-start.12 = (bf16[4,4,4,32,1024]{4,3,1,0,2:T(8,128)(2,1)}, bf16[4,4,4,32,1024]{4,3,1,0,2:T(8,128)(2,1)}, u32[]{:S(2)}, u32[]{:S(2)}) collective-permute-start(bf16[4,4,4,32,1024]{4,3,1,0,2:T(8,128)(2,1)} %bitcast_dynamic-update-slice_fusion.3), channel_id=1, source_target_pairs={{0,4},{1,5},{2,6},{3,7},{4,0},{5,1},{6,2},{7,3},{8,12},{9,13},{10,... | collective-permute-start | bytes 12582920 | tf_op jit(solution)/shard_map/ppermute | solution.py:23
  160.8 106.4 %collective-permute-start.21 = (bf16[256,1024]{1,0:T(8,128)(2,1)S(1)}, bf16[256,1024]{1,0:T(8,128)(2,1)S(1)}, u32[]{:S(2)}, u32[]{:S(2)}) collective-permute-start(bf16[256,1024]{1,0:T(8,128)(2,1)S(1)} %broadcast_select_fusion.1), channel_id=1, source_target_pairs={{0,496},{4,500},{8,504},{12,508},{16,0},{20,4},{24,8},{28,12},{32,... | collective-permute-start | bytes 1572872 | tf_op jit(solution)/shard_map/ppermute | solution.py:84
  213.9 102.5 %collective-permute-start.15 = (bf16[256,1024]{1,0:T(8,128)(2,1)S(1)}, bf16[256,1024]{1,0:T(8,128)(2,1)S(1)}, u32[]{:S(2)}, u32[]{:S(2)}) collective-permute-start(bf16[256,1024]{1,0:T(8,128)(2,1)S(1)} %broadcast_select_fusion.7), channel_id=1, source_target_pairs={{0,496},{4,500},{8,504},{12,508},{16,0},{20,4},{24,8},{28,12},{32,... | collective-permute-start | bytes 1572872 | tf_op jit(solution)/shard_map/ppermute | solution.py:84
  267.3 77.0 %collective-permute-start.22 = (bf16[256,1024]{1,0:T(8,128)(2,1)S(1)}, bf16[256,1024]{1,0:T(8,128)(2,1)S(1)}, u32[]{:S(2)}, u32[]{:S(2)}) collective-permute-start(bf16[256,1024]{1,0:T(8,128)(2,1)S(1)} %broadcast_select_fusion.2), channel_id=1, source_target_pairs={{0,480},{4,484},{8,488},{12,492},{16,496},{20,500},{24,504},{28,50... | collective-permute-start | bytes 1572872 | tf_op jit(solution)/shard_map/ppermute | solution.py:84
  316.4 54.9 %collective-permute-start.16 = (bf16[256,1024]{1,0:T(8,128)(2,1)S(1)}, bf16[256,1024]{1,0:T(8,128)(2,1)S(1)}, u32[]{:S(2)}, u32[]{:S(2)}) collective-permute-start(bf16[256,1024]{1,0:T(8,128)(2,1)S(1)} %broadcast_select_fusion.8), channel_id=1, source_target_pairs={{0,480},{4,484},{8,488},{12,492},{16,496},{20,500},{24,504},{28,50... | collective-permute-start | bytes 1572872 | tf_op jit(solution)/shard_map/ppermute | solution.py:84
  318.4 94.7 %collective-permute-start = (bf16[256,1024]{1,0:T(8,128)(2,1)}, bf16[256,1024]{1,0:T(8,128)(2,1)}, u32[]{:S(2)}, u32[]{:S(2)}) collective-permute-start(bf16[256,1024]{1,0:T(8,128)(2,1)} %param.3), channel_id=1, source_target_pairs={{0,1},{1,2},{2,3},{3,0},{4,5},{5,6},{6,7},{7,4},{8,9},{9,10},{10,1... | collective-permute-start | bytes 1572872 | tf_op jit(solution)/shard_map/ppermute | solution.py:23
  320.3 160.2 %collective-permute-start.1 = (bf16[256,1024]{1,0:T(8,128)(2,1)}, bf16[256,1024]{1,0:T(8,128)(2,1)}, u32[]{:S(2)}, u32[]{:S(2)}) collective-permute-start(bf16[256,1024]{1,0:T(8,128)(2,1)} %param.3), channel_id=1, source_target_pairs={{0,2},{1,3},{2,0},{3,1},{4,6},{5,7},{6,4},{7,5},{8,10},{9,11},{10,... | collective-permute-start | bytes 1572872 | tf_op jit(solution)/shard_map/ppermute | solution.py:23
  344.3 71.7 %collective-permute-start.23 = (bf16[256,1024]{1,0:T(8,128)(2,1)S(1)}, bf16[256,1024]{1,0:T(8,128)(2,1)}, u32[]{:S(2)}, u32[]{:S(2)}) collective-permute-start(bf16[256,1024]{1,0:T(8,128)(2,1)S(1)} %broadcast_select_fusion.3), channel_id=1, source_target_pairs={{0,448},{4,452},{8,456},{12,460},{16,464},{20,468},{24,472},{28,47... | collective-permute-start | bytes 1572872 | tf_op jit(solution)/shard_map/ppermute | solution.py:84
  371.4 51.0 %collective-permute-start.17 = (bf16[256,1024]{1,0:T(8,128)(2,1)S(1)}, bf16[256,1024]{1,0:T(8,128)(2,1)}, u32[]{:S(2)}, u32[]{:S(2)}) collective-permute-start(bf16[256,1024]{1,0:T(8,128)(2,1)S(1)} %broadcast_select_fusion.9), channel_id=1, source_target_pairs={{0,448},{4,452},{8,456},{12,460},{16,464},{20,468},{24,472},{28,47... | collective-permute-start | bytes 1572872 | tf_op jit(solution)/shard_map/ppermute | solution.py:84
  413.0 133.8 %collective-permute-start.2 = (bf16[256,1024]{1,0:T(8,128)(2,1)}, bf16[256,1024]{1,0:T(8,128)(2,1)S(1)}, u32[]{:S(2)}, u32[]{:S(2)}) collective-permute-start(bf16[256,1024]{1,0:T(8,128)(2,1)} %param.3), channel_id=1, source_target_pairs={{0,3},{1,0},{2,1},{3,2},{4,7},{5,4},{6,5},{7,6},{8,11},{9,8},{10,9... | collective-permute-start | bytes 1572872 | tf_op jit(solution)/shard_map/ppermute | solution.py:23
  416.1 130.8 %collective-permute-start.24 = (bf16[256,1024]{1,0:T(8,128)(2,1)S(1)}, bf16[256,1024]{1,0:T(8,128)(2,1)S(1)}, u32[]{:S(2)}, u32[]{:S(2)}) collective-permute-start(bf16[256,1024]{1,0:T(8,128)(2,1)S(1)} %broadcast_select_fusion.4), channel_id=1, source_target_pairs={{0,384},{4,388},{8,392},{12,396},{16,400},{20,404},{24,408},{28,41... | collective-permute-start | bytes 1572872 | tf_op jit(solution)/shard_map/ppermute | solution.py:84
  423.5 155.1 %collective-permute-start.18 = (bf16[256,1024]{1,0:T(8,128)(2,1)S(1)}, bf16[256,1024]{1,0:T(8,128)(2,1)S(1)}, u32[]{:S(2)}, u32[]{:S(2)}) collective-permute-start(bf16[256,1024]{1,0:T(8,128)(2,1)S(1)} %broadcast_select_fusion.10), channel_id=1, source_target_pairs={{0,384},{4,388},{8,392},{12,396},{16,400},{20,404},{24,408},{28,41... | collective-permute-start | bytes 1572872 | tf_op jit(solution)/shard_map/ppermute | solution.py:84
  547.0 48.2 %collective-permute-start.25 = (bf16[256,1024]{1,0:T(8,128)(2,1)S(1)}, bf16[256,1024]{1,0:T(8,128)(2,1)S(1)}, u32[]{:S(2)}, u32[]{:S(2)}) collective-permute-start(bf16[256,1024]{1,0:T(8,128)(2,1)S(1)} %broadcast_select_fusion.5), channel_id=1, source_target_pairs={{0,256},{4,260},{8,264},{12,268},{16,272},{20,276},{24,280},{28,28... | collective-permute-start | bytes 1572872 | tf_op jit(solution)/shard_map/ppermute | solution.py:84
  578.7 26.3 %collective-permute-start.19 = (bf16[256,1024]{1,0:T(8,128)(2,1)S(1)}, bf16[256,1024]{1,0:T(8,128)(2,1)S(1)}, u32[]{:S(2)}, u32[]{:S(2)}) collective-permute-start(bf16[256,1024]{1,0:T(8,128)(2,1)S(1)} %broadcast_select_fusion.11), channel_id=1, source_target_pairs={{0,256},{4,260},{8,264},{12,268},{16,272},{20,276},{24,280},{28,28... | collective-permute-start | bytes 1572872 | tf_op jit(solution)/shard_map/ppermute | solution.py:84
  605.5 102.7 %collective-permute-start.28 = (bf16[128,256]{1,0:T(8,128)(2,1)S(1)}, bf16[128,256]{1,0:T(8,128)(2,1)S(1)}, u32[]{:S(2)}, u32[]{:S(2)}) collective-permute-start(bf16[128,256]{1,0:T(8,128)(2,1)S(1)} %get-tuple-element.16), channel_id=1, source_target_pairs={{0,3},{1,0},{2,1},{3,2},{4,7},{5,4},{6,5},{7,6},{8,11},{9,8},{10,9... | collective-permute-start | bytes 196616 | tf_op jit(solution)/shard_map/ppermute | solution.py:23
  607.4 100.8 %collective-permute-start.27 = (bf16[128,256]{1,0:T(8,128)(2,1)S(1)}, bf16[128,256]{1,0:T(8,128)(2,1)S(1)}, u32[]{:S(2)}, u32[]{:S(2)}) collective-permute-start(bf16[128,256]{1,0:T(8,128)(2,1)S(1)} %get-tuple-element.17), channel_id=1, source_target_pairs={{0,2},{1,3},{2,0},{3,1},{4,6},{5,7},{6,4},{7,5},{8,10},{9,11},{10,... | collective-permute-start | bytes 196616 | tf_op jit(solution)/shard_map/ppermute | solution.py:23
  704.9 6.8 collective-permute-start.26
  711.7 9.0 %collective-permute-start.29 = (bf16[128,256]{1,0:T(8,128)(2,1)S(1)}, bf16[128,256]{1,0:T(8,128)(2,1)S(1)}, u32[]{:S(2)}, u32[]{:S(2)}) collective-permute-start(bf16[128,256]{1,0:T(8,128)(2,1)S(1)} %get-tuple-element.6), channel_id=1, source_target_pairs={{0,1},{1,2},{2,3},{3,0},{4,5},{5,6},{6,7},{7,4},{8,9},{9,10},{10,1... | collective-permute-start | bytes 196616 | tf_op jit(solution)/shard_map/ppermute | solution.py:23
  713.7 7.1 collective-permute-start.30
  715.6 7.6 %collective-permute-start.31 = (bf16[128,256]{1,0:T(8,128)(2,1)S(1)}, bf16[128,256]{1,0:T(8,128)(2,1)S(1)}, u32[]{:S(2)}, u32[]{:S(2)}) collective-permute-start(bf16[128,256]{1,0:T(8,128)(2,1)S(1)} %get-tuple-element.6), channel_id=1, source_target_pairs={{0,3},{1,0},{2,1},{3,2},{4,7},{5,4},{6,5},{7,6},{8,11},{9,8},{10,9... | collective-permute-start | bytes 196616 | tf_op jit(solution)/shard_map/ppermute | solution.py:23
  (1 other events, 35.0 us)

commit v2 on v1

--- a/solution.py
+++ b/solution.py
@@ -8,6 +8,7 @@
 K = 4096
 ROUNDS = 2
 BOTH = ("docs", "proj")
+CHUNKS = 2
 
 
 def place(index):
@@ -57,12 +58,6 @@
     return jnp.stack([first, second], axis=3).reshape(4096, own.shape[1])
 
 
-def gather_grads(own):
-    p = lax.axis_index("proj")
-    parts = gather4(own, p, lambda t, zh, y, x, c, p: (zh, y, x, c, p + t))
-    return [parts[i] for i in range(4)]
-
-
 def sum_over_proj(part):
     p = lax.axis_index("proj")
     low = part.astype(jnp.bfloat16)
@@ -79,22 +74,56 @@
     ).astype(jnp.float32)
 
 
-def shifted(value, axis, by):
-    size = lax.axis_size(axis)
-    return lax.ppermute(value, axis, [(i, (i + by) % size) for i in range(size)])
+def ring(value, by):
+    def move(zh, y, x, c, p):
+        z = 4 * zh + p + by
+        return z // 4, y, x, c, z % 4
+
+    out = []
+    for _ in range(4):
+        value = send(value, move)
+        out.append(value)
+    return out
 
 
-def fetch_every(block, offset, bits_total):
-    current = block
-    for bit in range(bits_total):
-        moved = shifted(current, "docs", -(1 << bit))
-        current = jnp.where(offset >> bit & 1 == 1, moved, current)
-    return current
+def gather_grads(own):
+    p = lax.axis_index("proj")
+    rows = own.shape[0]
+    step = rows // CHUNKS
+    slabs, near = [], []
+    for i in range(CHUNKS):
+        chunk = own[i * step : (i + 1) * step]
+        below = ring(chunk, 1)
+        above = ring(chunk, -1)
+        line = jnp.stack(below[2::-1] + [chunk] + above[:3])
+        slabs.append(lax.dynamic_slice(line, (3 - p, 0, 0), (4,) + chunk.shape))
+        near.append((above[3], below[3]))
+    half = rows // 2
+    up = jnp.concatenate([one[0] for one in near])
+    down = jnp.concatenate([one[1] for one in near])
+    far = jnp.concatenate(
+        [
+            send(up[:half], lambda zh, y, x, c, p: (zh - 1, y, x, c, p)),
+            send(down[half:], lambda zh, y, x, c, p: (zh + 1, y, x, c, p)),
+        ]
+    )
+    return jnp.concatenate(slabs, axis=1), jnp.stack([own, up, far, down])
+
+
+def rotate(value, by):
+    def branch(shift):
+        def move(zh, y, x, c, p):
+            m = (y * 8 + x * 2 + c - shift) % 32
+            return zh, m >> 3, m >> 1 & 3, m & 1, p
+
+        return lambda one: send(one, move) if shift else one
+
+    return lax.switch(by, [branch(shift) for shift in range(32)], value)
 
 
 def on_device(grads, precond, offsets):
     columns = gather_precond(precond)
-    slabs = gather_grads(grads)
+    slabs, blocks = gather_grads(grads)
     pre = sum(
         jnp.dot(
             slabs[i],
@@ -104,10 +133,12 @@
         for i in range(4)
     ).astype(jnp.bfloat16)
     factor = jnp.float32(1.0 / math.sqrt(K))
-    bits_total = (lax.axis_size("docs") - 1).bit_length()
+    m = lax.axis_index("docs") % 32
     grams = []
     for step in range(ROUNDS):
-        partner = fetch_every(grads, offsets[step], bits_total)
+        low = offsets[step] % 32
+        ahead = (offsets[step] // 32 + (m < low)) % 4
+        partner = rotate(lax.dynamic_index_in_dim(blocks, ahead, 0, keepdims=False), low)
         grams.append(
             lax.dot_general(
                 pre, partner, (((1,), (1,)), ((), ())), preferred_element_type=jnp.float32

time: 732 us -> 409 us (0.56)
  waiting for transfers between devices: 421 us -> 57.5 us
  starting transfers between devices: 268 us -> 312 us
  local copies, waits for them, and re-layouts: 12.3 us -> 20.2 us
    ppermute x13 -> x0, waiting for transfers between devices: 257 us -> none  [shifted(): lax.ppermute(value, axis, [(i, (i + by) % size) for i in range(size)])]
    ppermute x19 -> x35, starting transfers between devices: 166 us -> 312 us  [send(): lax.ppermute(value, BOTH, [(i, number(*to(*place(i)))) for i in range(512)])]
    ppermute x19 -> x35, waiting for transfers between devices: 165 us -> 57.5 us  [send(): lax.ppermute(value, BOTH, [(i, number(*to(*place(i)))) for i in range(512)])]
    ppermute x13 -> x0, starting transfers between devices: 102 us -> none  [shifted(): lax.ppermute(value, axis, [(i, (i + by) % size) for i in range(size)])]
  transfers between devices with their start and end apart: 32 -> 35, of which waited for: 17 -> 12; matrix products, arithmetic and copies ran while one was open for 3% -> 5% of each run, Pallas kernels for 0% -> 0%
where the time goes in v2:
time: 409 us; the launch traced here: 406 us
  starting transfers between devices  312 us (76%)
  waiting for transfers between devices  57.5 us (14%)
  local copies, waits for them, and re-layouts  20.2 us (5%)
  other arithmetic  6.2 us (2%)
  between operations  5.95 us (1%)
    ppermute x35, starting transfers between devices, send(): lax.ppermute(value, BOTH, [(i, number(*to(*place(i)))) for i in range(512)])  312 us
    ppermute x35, waiting for transfers between devices, send(): lax.ppermute(value, BOTH, [(i, number(*to(*place(i)))) for i in range(512)])  57.5 us
  transfers between devices with their start and end apart: 35, of which 12 were waited for; matrix products, arithmetic and copies ran while one was open for 5% of the time, Pallas kernels for 0%

profile of v2, /device:TPU:1, one launch (start us, length us, event | category | flops | bytes accessed | tf_op | source)
XLA Modules:
  0.0 405.6 jit_solution(6012334982566294266)
XLA Ops:
  0.0 21.8 %collective-permute-start.74 = (bf16[32,1024]{1,0:T(8,128)(2,1)}, bf16[32,1024]{1,0:T(8,128)(2,1)S(1)}, u32[]{:S(2)}, u32[]{:S(2)}) collective-permute-start(bf16[32,1024]{1,0:T(8,128)(2,1)} %param.68), channel_id=1, source_target_pairs={{0,128},{1,129},{2,130},{3,131},{4,132},{5,133},{6,134},{7,135},{8... | collective-permute-start | bytes 196616 | tf_op jit(solution)/shard_map/ppermute | solution.py:24
  21.8 19.0 %collective-permute-start.75 = (bf16[32,1024]{1,0:T(8,128)(2,1)}, bf16[32,1024]{1,0:T(8,128)(2,1)S(1)}, u32[]{:S(2)}, u32[]{:S(2)}) collective-permute-start(bf16[32,1024]{1,0:T(8,128)(2,1)} %param.68), channel_id=1, source_target_pairs={{0,256},{1,257},{2,258},{3,259},{4,260},{5,261},{6,262},{7,263},{8... | collective-permute-start | bytes 196616 | tf_op jit(solution)/shard_map/ppermute | solution.py:24
  40.8 19.0 %collective-permute-start.76 = (bf16[32,1024]{1,0:T(8,128)(2,1)}, bf16[32,1024]{1,0:T(8,128)(2,1)S(1)}, u32[]{:S(2)}, u32[]{:S(2)}) collective-permute-start(bf16[32,1024]{1,0:T(8,128)(2,1)} %param.68), channel_id=1, source_target_pairs={{0,384},{1,385},{2,386},{3,387},{4,388},{5,389},{6,390},{7,391},{8... | collective-permute-start | bytes 196616 | tf_op jit(solution)/shard_map/ppermute | solution.py:24
  60.8 7.6 %collective-permute-done.76 = bf16[32,1024]{1,0:T(8,128)(2,1)S(1)} collective-permute-done((bf16[32,1024]{1,0:T(8,128)(2,1)}, bf16[32,1024]{1,0:T(8,128)(2,1)S(1)}, u32[]{:S(2)}, u32[]{:S(2)}) %collective-permute-start.76) | collective-permute-done | bytes 65568 | tf_op jit(solution)/shard_map/ppermute | solution.py:24
  68.4 18.9 %collective-permute-start.77 = (bf16[4,32,1024]{2,1,0:T(8,128)(2,1)S(1)}, bf16[4,32,1024]{2,1,0:T(8,128)(2,1)S(1)}, u32[]{:S(2)}, u32[]{:S(2)}) collective-permute-start(bf16[4,32,1024]{2,1,0:T(8,128)(2,1)S(1)} %bitcast_dynamic-update-slice_fusion.26), channel_id=1, source_target_pairs={{0,32},{1,33},{2,34},{3,35},{4,12},{5,13},{6,14},{7,15},{8,40},{9,... | collective-permute-start | bytes 786440 | tf_op jit(solution)/shard_map/ppermute | solution.py:24
  87.4 19.0 %collective-permute-start.78 = (bf16[4,32,1024]{2,1,0:T(8,128)(2,1)S(1)}, bf16[4,32,1024]{2,1,0:T(8,128)(2,1)S(1)}, u32[]{:S(2)}, u32[]{:S(2)}) collective-permute-start(bf16[4,32,1024]{2,1,0:T(8,128)(2,1)S(1)} %bitcast_dynamic-update-slice_fusion.26), channel_id=1, source_target_pairs={{0,64},{1,65},{2,66},{3,67},{4,20},{5,21},{6,22},{7,23},{8,72},{9,... | collective-permute-start | bytes 786440 | tf_op jit(solution)/shard_map/ppermute | solution.py:24
  106.4 19.0 %collective-permute-start.79 = (bf16[4,32,1024]{2,1,0:T(8,128)(2,1)S(1)}, bf16[4,32,1024]{2,1,0:T(8,128)(2,1)S(1)}, u32[]{:S(2)}, u32[]{:S(2)}) collective-permute-start(bf16[4,32,1024]{2,1,0:T(8,128)(2,1)S(1)} %bitcast_dynamic-update-slice_fusion.26), channel_id=1, source_target_pairs={{0,96},{1,97},{2,98},{3,99},{4,28},{5,29},{6,30},{7,31},{8,104},{9... | collective-permute-start | bytes 786440 | tf_op jit(solution)/shard_map/ppermute | solution.py:24
  125.7 5.2 %collective-permute-done.79 = bf16[4,32,1024]{2,1,0:T(8,128)(2,1)S(1)} collective-permute-done((bf16[4,32,1024]{2,1,0:T(8,128)(2,1)S(1)}, bf16[4,32,1024]{2,1,0:T(8,128)(2,1)S(1)}, u32[]{:S(2)}, u32[]{:S(2)}) %collective-permute-start.79) | collective-permute-done | bytes 262176 | tf_op jit(solution)/shard_map/ppermute | solution.py:24
  130.9 19.2 %collective-permute-start.80 = (bf16[4,4,32,1024]{3,2,0,1:T(8,128)(2,1)S(1)}, bf16[4,4,32,1024]{3,2,0,1:T(8,128)(2,1)}, u32[]{:S(2)}, u32[]{:S(2)}) collective-permute-start(bf16[4,4,32,1024]{3,2,0,1:T(8,128)(2,1)S(1)} %bitcast_dynamic-update-slice_fusion.7), channel_id=1, source_target_pairs={{0,8},{1,9},{2,10},{3,11},{4,36},{5,37},{6,38},{7,39},{8,16},{9,17... | collective-permute-start | bytes 3145736 | tf_op jit(solution)/shard_map/ppermute | solution.py:24
  150.0 19.0 %collective-permute-start.81 = (bf16[4,4,32,1024]{3,2,0,1:T(8,128)(2,1)S(1)}, bf16[4,4,32,1024]{3,2,0,1:T(8,128)(2,1)S(1)}, u32[]{:S(2)}, u32[]{:S(2)}) collective-permute-start(bf16[4,4,32,1024]{3,2,0,1:T(8,128)(2,1)S(1)} %bitcast_dynamic-update-slice_fusion.7), channel_id=1, source_target_pairs={{0,16},{1,17},{2,18},{3,19},{4,68},{5,69},{6,70},{7,71},{8,24},{9,... | collective-permute-start | bytes 3145736 | tf_op jit(solution)/shard_map/ppermute | solution.py:24
  169.9 3.4 collective-permute-start.68
  173.3 3.4 collective-permute-start.62
  176.7 5.5 %collective-permute-start.71 = (bf16[128,1024]{1,0:T(8,128)(2,1)}, bf16[128,1024]{1,0:T(8,128)(2,1)S(1)}, u32[]{:S(2)}, u32[]{:S(2)}) collective-permute-start(bf16[128,1024]{1,0:T(8,128)(2,1)} %get-tuple-element.148), channel_id=1, source_target_pairs={{0,387},{1,0},{2,1},{3,2},{4,391},{5,4},{6,5},{7,6},{8,395},{9,8},... | collective-permute-start | bytes 786440 | tf_op jit(solution)/shard_map/ppermute | solution.py:24
  184.6 16.8 %collective-permute-start.82 = (bf16[4,4,32,1024]{3,2,0,1:T(8,128)(2,1)S(1)}, bf16[4,4,32,1024]{3,2,0,1:T(8,128)(2,1)}, u32[]{:S(2)}, u32[]{:S(2)}) collective-permute-start(bf16[4,4,32,1024]{3,2,0,1:T(8,128)(2,1)S(1)} %bitcast_dynamic-update-slice_fusion.7), channel_id=1, source_target_pairs={{0,24},{1,25},{2,26},{3,27},{4,100},{5,101},{6,102},{7,103},{8,0},... | collective-permute-start | bytes 3145736 | tf_op jit(solution)/shard_map/ppermute | solution.py:24
  201.4 8.4 %collective-permute-start.65 = (bf16[128,1024]{1,0:T(8,128)(2,1)}, bf16[128,1024]{1,0:T(8,128)(2,1)S(1)}, u32[]{:S(2)}, u32[]{:S(2)}) collective-permute-start(bf16[128,1024]{1,0:T(8,128)(2,1)} %get-tuple-element.147), channel_id=1, source_target_pairs={{0,387},{1,0},{2,1},{3,2},{4,391},{5,4},{6,5},{7,6},{8,395},{9,8},... | collective-permute-start | bytes 786440 | tf_op jit(solution)/shard_map/ppermute | solution.py:24
  222.6 3.4 collective-permute-start.66
  230.4 2.9 collective-permute-start.64
  234.2 3.9 collective-permute-start.73
  243.7 16.4 %collective-permute-start.83 = (bf16[4,4,4,32,1024]{4,3,1,0,2:T(8,128)(2,1)}, bf16[4,4,4,32,1024]{4,3,1,0,2:T(8,128)(2,1)}, u32[]{:S(2)}, u32[]{:S(2)}) collective-permute-start(bf16[4,4,4,32,1024]{4,3,1,0,2:T(8,128)(2,1)} %bitcast_dynamic-update-slice_fusion.3), channel_id=1, source_target_pairs={{0,4},{1,5},{2,6},{3,7},{4,0},{5,1},{6,2},{7,3},{8,12},{9,13},{10,... | collective-permute-start | bytes 12582920 | tf_op jit(solution)/shard_map/ppermute | solution.py:24
  265.6 8.4 %collective-permute-start.84 = (bf16[128,1024]{1,0:T(8,128)(2,1)}, bf16[128,1024]{1,0:T(8,128)(2,1)S(1)}, u32[]{:S(2)}, u32[]{:S(2)}) collective-permute-start(bf16[128,1024]{1,0:T(8,128)(2,1)} %collective-permute-done.67), channel_id=1, source_target_pairs={{0,387},{1,0},{2,1},{3,2},{4,391},{5,4},{6,5},{7,6},{8,395},{9,8},... | collective-permute-start | bytes 786440 | tf_op jit(solution)/shard_map/ppermute | solution.py:24
  276.0 4.6 %collective-permute-start.85 = (bf16[128,1024]{1,0:T(8,128)(2,1)}, bf16[128,1024]{1,0:T(8,128)(2,1)S(1)}, u32[]{:S(2)}, u32[]{:S(2)}) collective-permute-start(bf16[128,1024]{1,0:T(8,128)(2,1)} %collective-permute-done.73), channel_id=1, source_target_pairs={{0,387},{1,0},{2,1},{3,2},{4,391},{5,4},{6,5},{7,6},{8,395},{9,8},... | collective-permute-start | bytes 786440 | tf_op jit(solution)/shard_map/ppermute | solution.py:24
  290.6 14.4 %collective-permute-start.86 = (bf16[128,1024]{1,0:T(8,128)(2,1)S(1)}, bf16[128,1024]{1,0:T(8,128)(2,1)S(1)}, u32[]{:S(2)}, u32[]{:S(2)}) collective-permute-start(bf16[128,1024]{1,0:T(8,128)(2,1)S(1)} %collective-permute-done.84), channel_id=1, source_target_pairs={{0,384},{1,385},{2,386},{3,387},{4,388},{5,389},{6,390},{7,391},{8... | collective-permute-start | bytes 786440 | tf_op jit(solution)/shard_map/ppermute | solution.py:24
  305.0 19.0 %collective-permute-start.88 = (bf16[128,1024]{1,0:T(8,128)(2,1)S(1)}, bf16[128,1024]{1,0:T(8,128)(2,1)S(1)}, u32[]{:S(2)}, u32[]{:S(2)}) collective-permute-start(bf16[128,1024]{1,0:T(8,128)(2,1)S(1)} %collective-permute-done.87), channel_id=1, source_target_pairs={{0,128},{1,129},{2,130},{3,131},{4,132},{5,133},{6,134},{7,135},{8... | collective-permute-start | bytes 786440 | tf_op jit(solution)/shard_map/ppermute | solution.py:24
  324.2 10.3 %collective-permute-done.86 = bf16[128,1024]{1,0:T(8,128)(2,1)S(1)} collective-permute-done((bf16[128,1024]{1,0:T(8,128)(2,1)S(1)}, bf16[128,1024]{1,0:T(8,128)(2,1)S(1)}, u32[]{:S(2)}, u32[]{:S(2)}) %collective-permute-start.86) | collective-permute-done | bytes 262176 | tf_op jit(solution)/shard_map/ppermute | solution.py:24
  334.5 10.5 %collective-permute-done.88 = bf16[128,1024]{1,0:T(8,128)(2,1)S(1)} collective-permute-done((bf16[128,1024]{1,0:T(8,128)(2,1)S(1)}, bf16[128,1024]{1,0:T(8,128)(2,1)S(1)}, u32[]{:S(2)}, u32[]{:S(2)}) %collective-permute-start.88) | collective-permute-done | bytes 262176 | tf_op jit(solution)/shard_map/ppermute | solution.py:24
  345.5 13.9 %conditional.3 = (bf16[256,1024]{1,0:T(8,128)(2,1)S(1)}) conditional(s32[]{:T(128)} %clamp.7, bf16[256,1024]{1,0:T(8,128)(2,1)S(1)} %get-tuple-element.144, bf16[256,1024]{1,0:T(8,128)(2,1)S(1)} %get-tuple-element.144, bf16[256,1024]{1,0:T(8,128)(2,1)S(1)} %get-tuple-element.144, ...), branch_computations={%region_32.33_spmd, %region_33.34_spmd, %region_34.35_spmd, %regio... | conditional | bytes 3145776 | solution.py:121
  347.6 11.7 %collective-permute-done.47 = bf16[256,1024]{1,0:T(8,128)(2,1)S(1)} collective-permute-done((bf16[256,1024]{1,0:T(8,128)(2,1)S(1)}, bf16[256,1024]{1,0:T(8,128)(2,1)S(1)}, u32[]{:S(2)}, u32[]{:S(2)}) %collective-permute-start.47) | collective-permute-done | bytes 524320 | tf_op jit(solution)/shard_map/cond/branch_17_fun/ppermute | solution.py:24
  359.4 3.8 select_bitcast_fusion.1
  368.1 10.0 %collective-permute-start.90 = (bf16[128,256]{1,0:T(8,128)(2,1)S(1)}, bf16[128,256]{1,0:T(8,128)(2,1)S(1)}, u32[]{:S(2)}, u32[]{:S(2)}) collective-permute-start(bf16[128,256]{1,0:T(8,128)(2,1)S(1)} %get-tuple-element.149), channel_id=1, source_target_pairs={{0,1},{1,2},{2,3},{3,0},{4,5},{5,6},{6,7},{7,4},{8,9},{9,10},{10,1... | collective-permute-start | bytes 196616 | tf_op jit(solution)/shard_map/ppermute | solution.py:24
  378.2 9.4 %collective-permute-start.91 = (bf16[128,256]{1,0:T(8,128)(2,1)S(1)}, bf16[128,256]{1,0:T(8,128)(2,1)S(1)}, u32[]{:S(2)}, u32[]{:S(2)}) collective-permute-start(bf16[128,256]{1,0:T(8,128)(2,1)S(1)} %get-tuple-element.151), channel_id=1, source_target_pairs={{0,2},{1,3},{2,0},{3,1},{4,6},{5,7},{6,4},{7,5},{8,10},{9,11},{10,... | collective-permute-start | bytes 196616 | tf_op jit(solution)/shard_map/ppermute | solution.py:24
  394.6 4.6 %collective-permute-start.94 = (bf16[128,256]{1,0:T(8,128)(2,1)S(1)}, bf16[128,256]{1,0:T(8,128)(2,1)S(1)}, u32[]{:S(2)}, u32[]{:S(2)}) collective-permute-start(bf16[128,256]{1,0:T(8,128)(2,1)S(1)} %get-tuple-element.136), channel_id=1, source_target_pairs={{0,2},{1,3},{2,0},{3,1},{4,6},{5,7},{6,4},{7,5},{8,10},{9,11},{10,... | collective-permute-start | bytes 196616 | tf_op jit(solution)/shard_map/ppermute | solution.py:24
  401.8 2.9 collective-permute-done.95
  (103 shorter events, 58.2 us)
Async XLA Ops:
  0.0 60.8 %collective-permute-start.74 = (bf16[32,1024]{1,0:T(8,128)(2,1)}, bf16[32,1024]{1,0:T(8,128)(2,1)S(1)}, u32[]{:S(2)}, u32[]{:S(2)}) collective-permute-start(bf16[32,1024]{1,0:T(8,128)(2,1)} %param.68), channel_id=1, source_target_pairs={{0,128},{1,129},{2,130},{3,131},{4,132},{5,133},{6,134},{7,135},{8... | collective-permute-start | bytes 196616 | tf_op jit(solution)/shard_map/ppermute | solution.py:24
  21.8 38.9 %collective-permute-start.75 = (bf16[32,1024]{1,0:T(8,128)(2,1)}, bf16[32,1024]{1,0:T(8,128)(2,1)S(1)}, u32[]{:S(2)}, u32[]{:S(2)}) collective-permute-start(bf16[32,1024]{1,0:T(8,128)(2,1)} %param.68), channel_id=1, source_target_pairs={{0,256},{1,257},{2,258},{3,259},{4,260},{5,261},{6,262},{7,263},{8... | collective-permute-start | bytes 196616 | tf_op jit(solution)/shard_map/ppermute | solution.py:24
  40.8 27.6 %collective-permute-start.76 = (bf16[32,1024]{1,0:T(8,128)(2,1)}, bf16[32,1024]{1,0:T(8,128)(2,1)S(1)}, u32[]{:S(2)}, u32[]{:S(2)}) collective-permute-start(bf16[32,1024]{1,0:T(8,128)(2,1)} %param.68), channel_id=1, source_target_pairs={{0,384},{1,385},{2,386},{3,387},{4,388},{5,389},{6,390},{7,391},{8... | collective-permute-start | bytes 196616 | tf_op jit(solution)/shard_map/ppermute | solution.py:24
  68.4 57.1 %collective-permute-start.77 = (bf16[4,32,1024]{2,1,0:T(8,128)(2,1)S(1)}, bf16[4,32,1024]{2,1,0:T(8,128)(2,1)S(1)}, u32[]{:S(2)}, u32[]{:S(2)}) collective-permute-start(bf16[4,32,1024]{2,1,0:T(8,128)(2,1)S(1)} %bitcast_dynamic-update-slice_fusion.26), channel_id=1, source_target_pairs={{0,32},{1,33},{2,34},{3,35},{4,12},{5,13},{6,14},{7,15},{8,40},{9,... | collective-permute-start | bytes 786440 | tf_op jit(solution)/shard_map/ppermute | solution.py:24
  87.4 38.2 %collective-permute-start.78 = (bf16[4,32,1024]{2,1,0:T(8,128)(2,1)S(1)}, bf16[4,32,1024]{2,1,0:T(8,128)(2,1)S(1)}, u32[]{:S(2)}, u32[]{:S(2)}) collective-permute-start(bf16[4,32,1024]{2,1,0:T(8,128)(2,1)S(1)} %bitcast_dynamic-update-slice_fusion.26), channel_id=1, source_target_pairs={{0,64},{1,65},{2,66},{3,67},{4,20},{5,21},{6,22},{7,23},{8,72},{9,... | collective-permute-start | bytes 786440 | tf_op jit(solution)/shard_map/ppermute | solution.py:24
  106.4 24.4 %collective-permute-start.79 = (bf16[4,32,1024]{2,1,0:T(8,128)(2,1)S(1)}, bf16[4,32,1024]{2,1,0:T(8,128)(2,1)S(1)}, u32[]{:S(2)}, u32[]{:S(2)}) collective-permute-start(bf16[4,32,1024]{2,1,0:T(8,128)(2,1)S(1)} %bitcast_dynamic-update-slice_fusion.26), channel_id=1, source_target_pairs={{0,96},{1,97},{2,98},{3,99},{4,28},{5,29},{6,30},{7,31},{8,104},{9... | collective-permute-start | bytes 786440 | tf_op jit(solution)/shard_map/ppermute | solution.py:24
  130.9 91.7 %collective-permute-start.80 = (bf16[4,4,32,1024]{3,2,0,1:T(8,128)(2,1)S(1)}, bf16[4,4,32,1024]{3,2,0,1:T(8,128)(2,1)}, u32[]{:S(2)}, u32[]{:S(2)}) collective-permute-start(bf16[4,4,32,1024]{3,2,0,1:T(8,128)(2,1)S(1)} %bitcast_dynamic-update-slice_fusion.7), channel_id=1, source_target_pairs={{0,8},{1,9},{2,10},{3,11},{4,36},{5,37},{6,38},{7,39},{8,16},{9,17... | collective-permute-start | bytes 3145736 | tf_op jit(solution)/shard_map/ppermute | solution.py:24
  150.0 88.0 %collective-permute-start.81 = (bf16[4,4,32,1024]{3,2,0,1:T(8,128)(2,1)S(1)}, bf16[4,4,32,1024]{3,2,0,1:T(8,128)(2,1)S(1)}, u32[]{:S(2)}, u32[]{:S(2)}) collective-permute-start(bf16[4,4,32,1024]{3,2,0,1:T(8,128)(2,1)S(1)} %bitcast_dynamic-update-slice_fusion.7), channel_id=1, source_target_pairs={{0,16},{1,17},{2,18},{3,19},{4,68},{5,69},{6,70},{7,71},{8,24},{9,... | collective-permute-start | bytes 3145736 | tf_op jit(solution)/shard_map/ppermute | solution.py:24
  169.9 14.7 %collective-permute-start.68 = (bf16[128,1024]{1,0:T(8,128)(2,1)}, bf16[128,1024]{1,0:T(8,128)(2,1)S(1)}, u32[]{:S(2)}, u32[]{:S(2)}) collective-permute-start(bf16[128,1024]{1,0:T(8,128)(2,1)} %get-tuple-element.148), channel_id=1, source_target_pairs={{0,1},{1,2},{2,3},{3,128},{4,5},{5,6},{6,7},{7,132},{8,9},{9,10},{... | collective-permute-start | bytes 786440 | tf_op jit(solution)/shard_map/ppermute | solution.py:24
  173.3 28.1 %collective-permute-start.62 = (bf16[128,1024]{1,0:T(8,128)(2,1)}, bf16[128,1024]{1,0:T(8,128)(2,1)S(1)}, u32[]{:S(2)}, u32[]{:S(2)}) collective-permute-start(bf16[128,1024]{1,0:T(8,128)(2,1)} %get-tuple-element.147), channel_id=1, source_target_pairs={{0,1},{1,2},{2,3},{3,128},{4,5},{5,6},{6,7},{7,132},{8,9},{9,10},{... | collective-permute-start | bytes 786440 | tf_op jit(solution)/shard_map/ppermute | solution.py:24
  176.7 33.2 %collective-permute-start.71 = (bf16[128,1024]{1,0:T(8,128)(2,1)}, bf16[128,1024]{1,0:T(8,128)(2,1)S(1)}, u32[]{:S(2)}, u32[]{:S(2)}) collective-permute-start(bf16[128,1024]{1,0:T(8,128)(2,1)} %get-tuple-element.148), channel_id=1, source_target_pairs={{0,387},{1,0},{2,1},{3,2},{4,391},{5,4},{6,5},{7,6},{8,395},{9,8},... | collective-permute-start | bytes 786440 | tf_op jit(solution)/shard_map/ppermute | solution.py:24
  184.6 56.8 %collective-permute-start.82 = (bf16[4,4,32,1024]{3,2,0,1:T(8,128)(2,1)S(1)}, bf16[4,4,32,1024]{3,2,0,1:T(8,128)(2,1)}, u32[]{:S(2)}, u32[]{:S(2)}) collective-permute-start(bf16[4,4,32,1024]{3,2,0,1:T(8,128)(2,1)S(1)} %bitcast_dynamic-update-slice_fusion.7), channel_id=1, source_target_pairs={{0,24},{1,25},{2,26},{3,27},{4,100},{5,101},{6,102},{7,103},{8,0},... | collective-permute-start | bytes 3145736 | tf_op jit(solution)/shard_map/ppermute | solution.py:24
  201.4 14.0 %collective-permute-start.65 = (bf16[128,1024]{1,0:T(8,128)(2,1)}, bf16[128,1024]{1,0:T(8,128)(2,1)S(1)}, u32[]{:S(2)}, u32[]{:S(2)}) collective-permute-start(bf16[128,1024]{1,0:T(8,128)(2,1)} %get-tuple-element.147), channel_id=1, source_target_pairs={{0,387},{1,0},{2,1},{3,2},{4,391},{5,4},{6,5},{7,6},{8,395},{9,8},... | collective-permute-start | bytes 786440 | tf_op jit(solution)/shard_map/ppermute | solution.py:24
  209.8 10.4 %collective-permute-start.69 = (bf16[128,1024]{1,0:T(8,128)(2,1)S(1)}, bf16[128,1024]{1,0:T(8,128)(2,1)}, u32[]{:S(2)}, u32[]{:S(2)}) collective-permute-start(bf16[128,1024]{1,0:T(8,128)(2,1)S(1)} %collective-permute-done.68), channel_id=1, source_target_pairs={{0,1},{1,2},{2,3},{3,128},{4,5},{5,6},{6,7},{7,132},{8,9},{9,10},{... | collective-permute-start | bytes 786440 | tf_op jit(solution)/shard_map/ppermute | solution.py:24
  215.5 12.9 %collective-permute-start.63 = (bf16[128,1024]{1,0:T(8,128)(2,1)S(1)}, bf16[128,1024]{1,0:T(8,128)(2,1)}, u32[]{:S(2)}, u32[]{:S(2)}) collective-permute-start(bf16[128,1024]{1,0:T(8,128)(2,1)S(1)} %collective-permute-done.62), channel_id=1, source_target_pairs={{0,1},{1,2},{2,3},{3,128},{4,5},{5,6},{6,7},{7,132},{8,9},{9,10},{... | collective-permute-start | bytes 786440 | tf_op jit(solution)/shard_map/ppermute | solution.py:24
  220.3 10.1 %collective-permute-start.72 = (bf16[128,1024]{1,0:T(8,128)(2,1)S(1)}, bf16[128,1024]{1,0:T(8,128)(2,1)}, u32[]{:S(2)}, u32[]{:S(2)}) collective-permute-start(bf16[128,1024]{1,0:T(8,128)(2,1)S(1)} %collective-permute-done.71), channel_id=1, source_target_pairs={{0,387},{1,0},{2,1},{3,2},{4,391},{5,4},{6,5},{7,6},{8,395},{9,8},... | collective-permute-start | bytes 786440 | tf_op jit(solution)/shard_map/ppermute | solution.py:24
  222.6 11.5 %collective-permute-start.66 = (bf16[128,1024]{1,0:T(8,128)(2,1)S(1)}, bf16[128,1024]{1,0:T(8,128)(2,1)}, u32[]{:S(2)}, u32[]{:S(2)}) collective-permute-start(bf16[128,1024]{1,0:T(8,128)(2,1)S(1)} %collective-permute-done.65), channel_id=1, source_target_pairs={{0,387},{1,0},{2,1},{3,2},{4,391},{5,4},{6,5},{7,6},{8,395},{9,8},... | collective-permute-start | bytes 786440 | tf_op jit(solution)/shard_map/ppermute | solution.py:24
  228.3 45.7 %collective-permute-start.70 = (bf16[128,1024]{1,0:T(8,128)(2,1)}, bf16[128,1024]{1,0:T(8,128)(2,1)}, u32[]{:S(2)}, u32[]{:S(2)}) collective-permute-start(bf16[128,1024]{1,0:T(8,128)(2,1)} %collective-permute-done.69), channel_id=1, source_target_pairs={{0,1},{1,2},{2,3},{3,128},{4,5},{5,6},{6,7},{7,132},{8,9},{9,10},{... | collective-permute-start | bytes 786440 | tf_op jit(solution)/shard_map/ppermute | solution.py:24
  230.4 50.2 %collective-permute-start.64 = (bf16[128,1024]{1,0:T(8,128)(2,1)}, bf16[128,1024]{1,0:T(8,128)(2,1)}, u32[]{:S(2)}, u32[]{:S(2)}) collective-permute-start(bf16[128,1024]{1,0:T(8,128)(2,1)} %collective-permute-done.63), channel_id=1, source_target_pairs={{0,1},{1,2},{2,3},{3,128},{4,5},{5,6},{6,7},{7,132},{8,9},{9,10},{... | collective-permute-start | bytes 786440 | tf_op jit(solution)/shard_map/ppermute | solution.py:24
  234.2 41.8 %collective-permute-start.73 = (bf16[128,1024]{1,0:T(8,128)(2,1)}, bf16[128,1024]{1,0:T(8,128)(2,1)}, u32[]{:S(2)}, u32[]{:S(2)}) collective-permute-start(bf16[128,1024]{1,0:T(8,128)(2,1)} %collective-permute-done.72), channel_id=1, source_target_pairs={{0,387},{1,0},{2,1},{3,2},{4,391},{5,4},{6,5},{7,6},{8,395},{9,8},... | collective-permute-start | bytes 786440 | tf_op jit(solution)/shard_map/ppermute | solution.py:24
  238.0 27.6 %collective-permute-start.67 = (bf16[128,1024]{1,0:T(8,128)(2,1)}, bf16[128,1024]{1,0:T(8,128)(2,1)}, u32[]{:S(2)}, u32[]{:S(2)}) collective-permute-start(bf16[128,1024]{1,0:T(8,128)(2,1)} %collective-permute-done.66), channel_id=1, source_target_pairs={{0,387},{1,0},{2,1},{3,2},{4,391},{5,4},{6,5},{7,6},{8,395},{9,8},... | collective-permute-start | bytes 786440 | tf_op jit(solution)/shard_map/ppermute | solution.py:24
  243.7 115.7 %collective-permute-start.83 = (bf16[4,4,4,32,1024]{4,3,1,0,2:T(8,128)(2,1)}, bf16[4,4,4,32,1024]{4,3,1,0,2:T(8,128)(2,1)}, u32[]{:S(2)}, u32[]{:S(2)}) collective-permute-start(bf16[4,4,4,32,1024]{4,3,1,0,2:T(8,128)(2,1)} %bitcast_dynamic-update-slice_fusion.3), channel_id=1, source_target_pairs={{0,4},{1,5},{2,6},{3,7},{4,0},{5,1},{6,2},{7,3},{8,12},{9,13},{10,... | collective-permute-start | bytes 12582920 | tf_op jit(solution)/shard_map/ppermute | solution.py:24
  265.6 25.0 %collective-permute-start.84 = (bf16[128,1024]{1,0:T(8,128)(2,1)}, bf16[128,1024]{1,0:T(8,128)(2,1)S(1)}, u32[]{:S(2)}, u32[]{:S(2)}) collective-permute-start(bf16[128,1024]{1,0:T(8,128)(2,1)} %collective-permute-done.67), channel_id=1, source_target_pairs={{0,387},{1,0},{2,1},{3,2},{4,391},{5,4},{6,5},{7,6},{8,395},{9,8},... | collective-permute-start | bytes 786440 | tf_op jit(solution)/shard_map/ppermute | solution.py:24
  274.1 31.0 %collective-permute-start.87 = (bf16[128,1024]{1,0:T(8,128)(2,1)}, bf16[128,1024]{1,0:T(8,128)(2,1)S(1)}, u32[]{:S(2)}, u32[]{:S(2)}) collective-permute-start(bf16[128,1024]{1,0:T(8,128)(2,1)} %collective-permute-done.70), channel_id=1, source_target_pairs={{0,1},{1,2},{2,3},{3,128},{4,5},{5,6},{6,7},{7,132},{8,9},{9,10},{... | collective-permute-start | bytes 786440 | tf_op jit(solution)/shard_map/ppermute | solution.py:24
  276.0 48.1 %collective-permute-start.85 = (bf16[128,1024]{1,0:T(8,128)(2,1)}, bf16[128,1024]{1,0:T(8,128)(2,1)S(1)}, u32[]{:S(2)}, u32[]{:S(2)}) collective-permute-start(bf16[128,1024]{1,0:T(8,128)(2,1)} %collective-permute-done.73), channel_id=1, source_target_pairs={{0,387},{1,0},{2,1},{3,2},{4,391},{5,4},{6,5},{7,6},{8,395},{9,8},... | collective-permute-start | bytes 786440 | tf_op jit(solution)/shard_map/ppermute | solution.py:24
  280.6 43.6 %collective-permute-start.89 = (bf16[128,1024]{1,0:T(8,128)(2,1)}, bf16[128,1024]{1,0:T(8,128)(2,1)S(1)}, u32[]{:S(2)}, u32[]{:S(2)}) collective-permute-start(bf16[128,1024]{1,0:T(8,128)(2,1)} %collective-permute-done.64), channel_id=1, source_target_pairs={{0,1},{1,2},{2,3},{3,128},{4,5},{5,6},{6,7},{7,132},{8,9},{9,10},{... | collective-permute-start | bytes 786440 | tf_op jit(solution)/shard_map/ppermute | solution.py:24
  290.6 43.9 %collective-permute-start.86 = (bf16[128,1024]{1,0:T(8,128)(2,1)S(1)}, bf16[128,1024]{1,0:T(8,128)(2,1)S(1)}, u32[]{:S(2)}, u32[]{:S(2)}) collective-permute-start(bf16[128,1024]{1,0:T(8,128)(2,1)S(1)} %collective-permute-done.84), channel_id=1, source_target_pairs={{0,384},{1,385},{2,386},{3,387},{4,388},{5,389},{6,390},{7,391},{8... | collective-permute-start | bytes 786440 | tf_op jit(solution)/shard_map/ppermute | solution.py:24
  305.0 40.0 %collective-permute-start.88 = (bf16[128,1024]{1,0:T(8,128)(2,1)S(1)}, bf16[128,1024]{1,0:T(8,128)(2,1)S(1)}, u32[]{:S(2)}, u32[]{:S(2)}) collective-permute-start(bf16[128,1024]{1,0:T(8,128)(2,1)S(1)} %collective-permute-done.87), channel_id=1, source_target_pairs={{0,128},{1,129},{2,130},{3,131},{4,132},{5,133},{6,134},{7,135},{8... | collective-permute-start | bytes 786440 | tf_op jit(solution)/shard_map/ppermute | solution.py:24
  345.7 13.7 %collective-permute-start.47 = (bf16[256,1024]{1,0:T(8,128)(2,1)S(1)}, bf16[256,1024]{1,0:T(8,128)(2,1)S(1)}, u32[]{:S(2)}, u32[]{:S(2)}) collective-permute-start(bf16[256,1024]{1,0:T(8,128)(2,1)S(1)} %param.49), channel_id=1, source_target_pairs={{0,60},{1,61},{2,62},{3,63},{4,64},{5,65},{6,66},{7,67},{8,68},{9,... | collective-permute-start | bytes 1572872 | tf_op jit(solution)/shard_map/cond/branch_17_fun/ppermute | solution.py:24
  368.1 21.4 %collective-permute-start.90 = (bf16[128,256]{1,0:T(8,128)(2,1)S(1)}, bf16[128,256]{1,0:T(8,128)(2,1)S(1)}, u32[]{:S(2)}, u32[]{:S(2)}) collective-permute-start(bf16[128,256]{1,0:T(8,128)(2,1)S(1)} %get-tuple-element.149), channel_id=1, source_target_pairs={{0,1},{1,2},{2,3},{3,0},{4,5},{5,6},{6,7},{7,4},{8,9},{9,10},{10,1... | collective-permute-start | bytes 196616 | tf_op jit(solution)/shard_map/ppermute | solution.py:24
  378.2 12.7 %collective-permute-start.91 = (bf16[128,256]{1,0:T(8,128)(2,1)S(1)}, bf16[128,256]{1,0:T(8,128)(2,1)S(1)}, u32[]{:S(2)}, u32[]{:S(2)}) collective-permute-start(bf16[128,256]{1,0:T(8,128)(2,1)S(1)} %get-tuple-element.151), channel_id=1, source_target_pairs={{0,2},{1,3},{2,0},{3,1},{4,6},{5,7},{6,4},{7,5},{8,10},{9,11},{10,... | collective-permute-start | bytes 196616 | tf_op jit(solution)/shard_map/ppermute | solution.py:24
  392.6 9.1 %collective-permute-start.93 = (bf16[128,256]{1,0:T(8,128)(2,1)S(1)}, bf16[128,256]{1,0:T(8,128)(2,1)S(1)}, u32[]{:S(2)}, u32[]{:S(2)}) collective-permute-start(bf16[128,256]{1,0:T(8,128)(2,1)S(1)} %get-tuple-element.136), channel_id=1, source_target_pairs={{0,1},{1,2},{2,3},{3,0},{4,5},{5,6},{6,7},{7,4},{8,9},{9,10},{10,1... | collective-permute-start | bytes 196616 | tf_op jit(solution)/shard_map/ppermute | solution.py:24
  (7 other events, 247.5 us)

commit v3 on v2

--- a/solution.py
+++ b/solution.py
@@ -111,12 +111,15 @@
 
 
 def rotate(value, by):
-    def branch(shift):
+    def turn(one, shift):
         def move(zh, y, x, c, p):
             m = (y * 8 + x * 2 + c - shift) % 32
             return zh, m >> 3, m >> 1 & 3, m & 1, p
 
-        return lambda one: send(one, move) if shift else one
+        return send(one, move) if shift else one
+
+    def branch(shift):
+        return lambda one: turn(turn(one, shift % 2), shift - shift % 2)
 
     return lax.switch(by, [branch(shift) for shift in range(32)], value)
 

time: 409 us -> 258 us (0.63)
  starting transfers between devices: 312 us -> 151 us
  waiting for transfers between devices: 57.5 us -> 66 us
    ppermute x35 -> x37, starting transfers between devices: 312 us -> 151 us  [send(): lax.ppermute(value, BOTH, [(i, number(*to(*place(i)))) for i in range(512)])]
    ppermute x35 -> x37, waiting for transfers between devices: 57.5 us -> 66 us  [send(): lax.ppermute(value, BOTH, [(i, number(*to(*place(i)))) for i in range(512)])]
  transfers between devices with their start and end apart: 35 -> 37, of which waited for: 12 -> 14; matrix products, arithmetic and copies ran while one was open for 5% -> 8% of each run, Pallas kernels for 0% -> 0%
where the time goes in v3:
time: 258 us; the launch traced here: 254 us
  starting transfers between devices  151 us (59%)
  waiting for transfers between devices  66 us (26%)
  local copies, waits for them, and re-layouts  20.2 us (8%)
  other arithmetic  6.2 us (2%)
  between operations  6.15 us (2%)
  matrix products  3.66 us (1%)
    ppermute x37, starting transfers between devices, send(): lax.ppermute(value, BOTH, [(i, number(*to(*place(i)))) for i in range(512)])  151 us
    ppermute x37, waiting for transfers between devices, send(): lax.ppermute(value, BOTH, [(i, number(*to(*place(i)))) for i in range(512)])  66 us
    dynamic_update_slice x15, local copies, waits for them, and re-layouts, put(): lax.dynamic_update_slice(buffer, piece[None], (at,) + (0,) * (buffer.ndim...  7.83 us
    unnamed x19, local copies, waits for them, and re-layouts  5.98 us
  transfers between devices with their start and end apart: 37, of which 14 were waited for; matrix products, arithmetic and copies ran while one was open for 8% of the time, Pallas kernels for 0%

profile of v3, /device:TPU:1, one launch (start us, length us, event | category | flops | bytes accessed | tf_op | source)
XLA Modules:
  0.0 253.8 jit_solution(13146267418142847640)
XLA Ops:
  0.0 9.8 %collective-permute-start.104 = (bf16[32,1024]{1,0:T(8,128)(2,1)}, bf16[32,1024]{1,0:T(8,128)(2,1)S(1)}, u32[]{:S(2)}, u32[]{:S(2)}) collective-permute-start(bf16[32,1024]{1,0:T(8,128)(2,1)} %param.68), channel_id=1, source_target_pairs={{0,128},{1,129},{2,130},{3,131},{4,132},{5,133},{6,134},{7,135},{8... | collective-permute-start | bytes 196616 | tf_op jit(solution)/shard_map/ppermute | solution.py:24
  9.8 10.6 %collective-permute-start.105 = (bf16[32,1024]{1,0:T(8,128)(2,1)}, bf16[32,1024]{1,0:T(8,128)(2,1)S(1)}, u32[]{:S(2)}, u32[]{:S(2)}) collective-permute-start(bf16[32,1024]{1,0:T(8,128)(2,1)} %param.68), channel_id=1, source_target_pairs={{0,256},{1,257},{2,258},{3,259},{4,260},{5,261},{6,262},{7,263},{8... | collective-permute-start | bytes 196616 | tf_op jit(solution)/shard_map/ppermute | solution.py:24
  20.4 5.2 %collective-permute-start.106 = (bf16[32,1024]{1,0:T(8,128)(2,1)}, bf16[32,1024]{1,0:T(8,128)(2,1)S(1)}, u32[]{:S(2)}, u32[]{:S(2)}) collective-permute-start(bf16[32,1024]{1,0:T(8,128)(2,1)} %param.68), channel_id=1, source_target_pairs={{0,384},{1,385},{2,386},{3,387},{4,388},{5,389},{6,390},{7,391},{8... | collective-permute-start | bytes 196616 | tf_op jit(solution)/shard_map/ppermute | solution.py:24
  27.8 6.9 %collective-permute-done.106 = bf16[32,1024]{1,0:T(8,128)(2,1)S(1)} collective-permute-done((bf16[32,1024]{1,0:T(8,128)(2,1)}, bf16[32,1024]{1,0:T(8,128)(2,1)S(1)}, u32[]{:S(2)}, u32[]{:S(2)}) %collective-permute-start.106) | collective-permute-done | bytes 65568 | tf_op jit(solution)/shard_map/ppermute | solution.py:24
  34.7 3.1 %collective-permute-start.107 = (bf16[4,32,1024]{2,1,0:T(8,128)(2,1)S(1)}, bf16[4,32,1024]{2,1,0:T(8,128)(2,1)S(1)}, u32[]{:S(2)}, u32[]{:S(2)}) collective-permute-start(bf16[4,32,1024]{2,1,0:T(8,128)(2,1)S(1)} %bitcast_dynamic-update-slice_fusion.26), channel_id=1, source_target_pairs={{0,32},{1,33},{2,34},{3,35},{4,12},{5,13},{6,14},{7,15},{8,40},{9,... | collective-permute-start | bytes 786440 | tf_op jit(solution)/shard_map/ppermute | solution.py:24
  37.9 4.4 %collective-permute-start.108 = (bf16[4,32,1024]{2,1,0:T(8,128)(2,1)S(1)}, bf16[4,32,1024]{2,1,0:T(8,128)(2,1)S(1)}, u32[]{:S(2)}, u32[]{:S(2)}) collective-permute-start(bf16[4,32,1024]{2,1,0:T(8,128)(2,1)S(1)} %bitcast_dynamic-update-slice_fusion.26), channel_id=1, source_target_pairs={{0,64},{1,65},{2,66},{3,67},{4,20},{5,21},{6,22},{7,23},{8,72},{9,... | collective-permute-start | bytes 786440 | tf_op jit(solution)/shard_map/ppermute | solution.py:24
  42.3 3.1 %collective-permute-start.109 = (bf16[4,32,1024]{2,1,0:T(8,128)(2,1)S(1)}, bf16[4,32,1024]{2,1,0:T(8,128)(2,1)S(1)}, u32[]{:S(2)}, u32[]{:S(2)}) collective-permute-start(bf16[4,32,1024]{2,1,0:T(8,128)(2,1)S(1)} %bitcast_dynamic-update-slice_fusion.26), channel_id=1, source_target_pairs={{0,96},{1,97},{2,98},{3,99},{4,28},{5,29},{6,30},{7,31},{8,104},{9... | collective-permute-start | bytes 786440 | tf_op jit(solution)/shard_map/ppermute | solution.py:24
  49.7 3.2 %collective-permute-start.110 = (bf16[4,4,32,1024]{3,2,0,1:T(8,128)(2,1)S(1)}, bf16[4,4,32,1024]{3,2,0,1:T(8,128)(2,1)}, u32[]{:S(2)}, u32[]{:S(2)}) collective-permute-start(bf16[4,4,32,1024]{3,2,0,1:T(8,128)(2,1)S(1)} %bitcast_dynamic-update-slice_fusion.7), channel_id=1, source_target_pairs={{0,8},{1,9},{2,10},{3,11},{4,36},{5,37},{6,38},{7,39},{8,16},{9,17... | collective-permute-start | bytes 3145736 | tf_op jit(solution)/shard_map/ppermute | solution.py:24
  52.9 4.5 %collective-permute-start.111 = (bf16[4,4,32,1024]{3,2,0,1:T(8,128)(2,1)S(1)}, bf16[4,4,32,1024]{3,2,0,1:T(8,128)(2,1)S(1)}, u32[]{:S(2)}, u32[]{:S(2)}) collective-permute-start(bf16[4,4,32,1024]{3,2,0,1:T(8,128)(2,1)S(1)} %bitcast_dynamic-update-slice_fusion.7), channel_id=1, source_target_pairs={{0,16},{1,17},{2,18},{3,19},{4,68},{5,69},{6,70},{7,71},{8,24},{9,... | collective-permute-start | bytes 3145736 | tf_op jit(solution)/shard_map/ppermute | solution.py:24
  62.1 4.6 %collective-permute-start.101 = (bf16[128,1024]{1,0:T(8,128)(2,1)}, bf16[128,1024]{1,0:T(8,128)(2,1)S(1)}, u32[]{:S(2)}, u32[]{:S(2)}) collective-permute-start(bf16[128,1024]{1,0:T(8,128)(2,1)} %get-tuple-element.148), channel_id=1, source_target_pairs={{0,387},{1,0},{2,1},{3,2},{4,391},{5,4},{6,5},{7,6},{8,395},{9,8},... | collective-permute-start | bytes 786440 | tf_op jit(solution)/shard_map/ppermute | solution.py:24
  67.2 3.0 %collective-permute-start.112 = (bf16[4,4,32,1024]{3,2,0,1:T(8,128)(2,1)S(1)}, bf16[4,4,32,1024]{3,2,0,1:T(8,128)(2,1)}, u32[]{:S(2)}, u32[]{:S(2)}) collective-permute-start(bf16[4,4,32,1024]{3,2,0,1:T(8,128)(2,1)S(1)} %bitcast_dynamic-update-slice_fusion.7), channel_id=1, source_target_pairs={{0,24},{1,25},{2,26},{3,27},{4,100},{5,101},{6,102},{7,103},{8,0},... | collective-permute-start | bytes 3145736 | tf_op jit(solution)/shard_map/ppermute | solution.py:24
  74.8 3.0 %collective-permute-start.99 = (bf16[128,1024]{1,0:T(8,128)(2,1)S(1)}, bf16[128,1024]{1,0:T(8,128)(2,1)}, u32[]{:S(2)}, u32[]{:S(2)}) collective-permute-start(bf16[128,1024]{1,0:T(8,128)(2,1)S(1)} %collective-permute-done.98), channel_id=1, source_target_pairs={{0,1},{1,2},{2,3},{3,128},{4,5},{5,6},{6,7},{7,132},{8,9},{9,10},{... | collective-permute-start | bytes 786440 | tf_op jit(solution)/shard_map/ppermute | solution.py:24
  83.4 4.6 %collective-permute-start.102 = (bf16[128,1024]{1,0:T(8,128)(2,1)S(1)}, bf16[128,1024]{1,0:T(8,128)(2,1)}, u32[]{:S(2)}, u32[]{:S(2)}) collective-permute-start(bf16[128,1024]{1,0:T(8,128)(2,1)S(1)} %collective-permute-done.101), channel_id=1, source_target_pairs={{0,387},{1,0},{2,1},{3,2},{4,391},{5,4},{6,5},{7,6},{8,395},{9,8},... | collective-permute-start | bytes 786440 | tf_op jit(solution)/shard_map/ppermute | solution.py:24
  92.6 3.2 %collective-permute-start.100 = (bf16[128,1024]{1,0:T(8,128)(2,1)}, bf16[128,1024]{1,0:T(8,128)(2,1)}, u32[]{:S(2)}, u32[]{:S(2)}) collective-permute-start(bf16[128,1024]{1,0:T(8,128)(2,1)} %collective-permute-done.99), channel_id=1, source_target_pairs={{0,1},{1,2},{2,3},{3,128},{4,5},{5,6},{6,7},{7,132},{8,9},{9,10},{... | collective-permute-start | bytes 786440 | tf_op jit(solution)/shard_map/ppermute | solution.py:24
  97.7 4.6 %collective-permute-start.103 = (bf16[128,1024]{1,0:T(8,128)(2,1)}, bf16[128,1024]{1,0:T(8,128)(2,1)}, u32[]{:S(2)}, u32[]{:S(2)}) collective-permute-start(bf16[128,1024]{1,0:T(8,128)(2,1)} %collective-permute-done.102), channel_id=1, source_target_pairs={{0,387},{1,0},{2,1},{3,2},{4,391},{5,4},{6,5},{7,6},{8,395},{9,8},... | collective-permute-start | bytes 786440 | tf_op jit(solution)/shard_map/ppermute | solution.py:24
  108.0 9.5 %collective-permute-start.113 = (bf16[4,4,4,32,1024]{4,3,1,0,2:T(8,128)(2,1)}, bf16[4,4,4,32,1024]{4,3,1,0,2:T(8,128)(2,1)}, u32[]{:S(2)}, u32[]{:S(2)}) collective-permute-start(bf16[4,4,4,32,1024]{4,3,1,0,2:T(8,128)(2,1)} %bitcast_dynamic-update-slice_fusion.3), channel_id=1, source_target_pairs={{0,4},{1,5},{2,6},{3,7},{4,0},{5,1},{6,2},{7,3},{8,12},{9,13},{10,... | collective-permute-start | bytes 12582920 | tf_op jit(solution)/shard_map/ppermute | solution.py:24
  128.6 4.0 %collective-permute-start.115 = (bf16[128,1024]{1,0:T(8,128)(2,1)}, bf16[128,1024]{1,0:T(8,128)(2,1)S(1)}, u32[]{:S(2)}, u32[]{:S(2)}) collective-permute-start(bf16[128,1024]{1,0:T(8,128)(2,1)} %collective-permute-done.103), channel_id=1, source_target_pairs={{0,387},{1,0},{2,1},{3,2},{4,391},{5,4},{6,5},{7,6},{8,395},{9,8},... | collective-permute-start | bytes 786440 | tf_op jit(solution)/shard_map/ppermute | solution.py:24
  142.6 5.5 %collective-permute-start.116 = (bf16[128,1024]{1,0:T(8,128)(2,1)S(1)}, bf16[128,1024]{1,0:T(8,128)(2,1)S(1)}, u32[]{:S(2)}, u32[]{:S(2)}) collective-permute-start(bf16[128,1024]{1,0:T(8,128)(2,1)S(1)} %collective-permute-done.114), channel_id=1, source_target_pairs={{0,384},{1,385},{2,386},{3,387},{4,388},{5,389},{6,390},{7,391},{8... | collective-permute-start | bytes 786440 | tf_op jit(solution)/shard_map/ppermute | solution.py:24
  148.1 3.7 %collective-permute-start.118 = (bf16[128,1024]{1,0:T(8,128)(2,1)S(1)}, bf16[128,1024]{1,0:T(8,128)(2,1)S(1)}, u32[]{:S(2)}, u32[]{:S(2)}) collective-permute-start(bf16[128,1024]{1,0:T(8,128)(2,1)S(1)} %collective-permute-done.117), channel_id=1, source_target_pairs={{0,128},{1,129},{2,130},{3,131},{4,132},{5,133},{6,134},{7,135},{8... | collective-permute-start | bytes 786440 | tf_op jit(solution)/shard_map/ppermute | solution.py:24
  152.0 15.5 %collective-permute-done.116 = bf16[128,1024]{1,0:T(8,128)(2,1)S(1)} collective-permute-done((bf16[128,1024]{1,0:T(8,128)(2,1)S(1)}, bf16[128,1024]{1,0:T(8,128)(2,1)S(1)}, u32[]{:S(2)}, u32[]{:S(2)}) %collective-permute-start.116) | collective-permute-done | bytes 262176 | tf_op jit(solution)/shard_map/ppermute | solution.py:24
  168.4 24.4 %conditional.2 = (bf16[256,1024]{1,0:T(8,128)(2,1)S(1)}) conditional(s32[]{:T(128)} %clamp.6, bf16[256,1024]{1,0:T(8,128)(2,1)S(1)} %get-tuple-element.143, bf16[256,1024]{1,0:T(8,128)(2,1)S(1)} %get-tuple-element.143, bf16[256,1024]{1,0:T(8,128)(2,1)S(1)} %get-tuple-element.143, ...), branch_computations={%region_0.1_spmd, %region_1.2_spmd, %region_2.3_spmd, %region_3.4_... | conditional | bytes 5242968 | solution.py:124
  168.5 7.6 %collective-permute-start.8 = (bf16[256,1024]{1,0:T(8,128)(2,1)S(1)}, bf16[256,1024]{1,0:T(8,128)(2,1)S(1)}, u32[]{:S(2)}, u32[]{:S(2)}) collective-permute-start(bf16[256,1024]{1,0:T(8,128)(2,1)S(1)} %param.7), channel_id=1, source_target_pairs={{0,124},{1,125},{2,126},{3,127},{4,0},{5,1},{6,2},{7,3},{8,4},{9,5... | collective-permute-start | bytes 1572872 | tf_op jit(solution)/shard_map/cond/branch_7_fun/ppermute | solution.py:24
  181.5 11.1 %collective-permute-done.9 = bf16[256,1024]{1,0:T(8,128)(2,1)S(1)} collective-permute-done((bf16[256,1024]{1,0:T(8,128)(2,1)S(1)}, bf16[256,1024]{1,0:T(8,128)(2,1)S(1)}, u32[]{:S(2)}, u32[]{:S(2)}) %collective-permute-start.9) | collective-permute-done | bytes 524320 | tf_op jit(solution)/shard_map/cond/branch_7_fun/ppermute | solution.py:24
  192.8 18.0 %conditional.3 = (bf16[256,1024]{1,0:T(8,128)(2,1)S(1)}) conditional(s32[]{:T(128)} %clamp.7, bf16[256,1024]{1,0:T(8,128)(2,1)S(1)} %get-tuple-element.144, bf16[256,1024]{1,0:T(8,128)(2,1)S(1)} %get-tuple-element.144, bf16[256,1024]{1,0:T(8,128)(2,1)S(1)} %get-tuple-element.144, ...), branch_computations={%region_32.33_spmd, %region_33.34_spmd, %region_34.35_spmd, %regio... | conditional | bytes 5242968 | solution.py:124
  192.8 3.4 %collective-permute-start.53 = (bf16[256,1024]{1,0:T(8,128)(2,1)S(1)}, bf16[256,1024]{1,0:T(8,128)(2,1)S(1)}, u32[]{:S(2)}, u32[]{:S(2)}) collective-permute-start(bf16[256,1024]{1,0:T(8,128)(2,1)S(1)} %param.38), channel_id=1, source_target_pairs={{0,104},{1,105},{2,106},{3,107},{4,108},{5,109},{6,110},{7,111},{8... | collective-permute-start | bytes 1572872 | tf_op jit(solution)/shard_map/cond/branch_6_fun/ppermute | solution.py:24
  196.2 14.5 %collective-permute-done.53 = bf16[256,1024]{1,0:T(8,128)(2,1)S(1)} collective-permute-done((bf16[256,1024]{1,0:T(8,128)(2,1)S(1)}, bf16[256,1024]{1,0:T(8,128)(2,1)S(1)}, u32[]{:S(2)}, u32[]{:S(2)}) %collective-permute-start.53) | collective-permute-done | bytes 524320 | tf_op jit(solution)/shard_map/cond/branch_6_fun/ppermute | solution.py:24
  210.8 3.8 %select_bitcast_fusion.1 = (bf16[4,4,4,1,32,1024]{5,4,1,2,0,3:T(8,128)(2,1)S(1)}, bf16[4,4,4,1,32,1024]{5,4,3,2,1,0:T(8,128)(2,1)S(1)}) fusion(bf16[4,4,4,32,1024]{4,3,1,0,2:T(8,128)(2,1)} %bitcast_dynamic-update-slice_fusion.3, bf16[4,4,4,32,1024]{4,3,1,0,2:T(8,128)(2,1)} %collective-permute-done.113, pred[]{:T(512)S(6)} %eq.28), kind=kLoop, calls=%fused_computation.7 | loop fusion | flops 4194304 | bytes 16777216 | tf_op jit(solution)/shard_map/stack | solution.py:58
  219.5 11.1 %collective-permute-start.120 = (bf16[128,256]{1,0:T(8,128)(2,1)S(1)}, bf16[128,256]{1,0:T(8,128)(2,1)S(1)}, u32[]{:S(2)}, u32[]{:S(2)}) collective-permute-start(bf16[128,256]{1,0:T(8,128)(2,1)S(1)} %get-tuple-element.149), channel_id=1, source_target_pairs={{0,1},{1,2},{2,3},{3,0},{4,5},{5,6},{6,7},{7,4},{8,9},{9,10},{10,1... | collective-permute-start | bytes 196616 | tf_op jit(solution)/shard_map/ppermute | solution.py:24
  230.6 4.6 %collective-permute-start.121 = (bf16[128,256]{1,0:T(8,128)(2,1)S(1)}, bf16[128,256]{1,0:T(8,128)(2,1)S(1)}, u32[]{:S(2)}, u32[]{:S(2)}) collective-permute-start(bf16[128,256]{1,0:T(8,128)(2,1)S(1)} %get-tuple-element.151), channel_id=1, source_target_pairs={{0,2},{1,3},{2,0},{3,1},{4,6},{5,7},{6,4},{7,5},{8,10},{9,11},{10,... | collective-permute-start | bytes 196616 | tf_op jit(solution)/shard_map/ppermute | solution.py:24
  242.8 3.6 %collective-permute-start.124 = (bf16[128,256]{1,0:T(8,128)(2,1)S(1)}, bf16[128,256]{1,0:T(8,128)(2,1)S(1)}, u32[]{:S(2)}, u32[]{:S(2)}) collective-permute-start(bf16[128,256]{1,0:T(8,128)(2,1)S(1)} %get-tuple-element.136), channel_id=1, source_target_pairs={{0,2},{1,3},{2,0},{3,1},{4,6},{5,7},{6,4},{7,5},{8,10},{9,11},{10,... | collective-permute-start | bytes 196616 | tf_op jit(solution)/shard_map/ppermute | solution.py:24
  246.4 3.3 %collective-permute-start.125 = (bf16[128,256]{1,0:T(8,128)(2,1)S(1)}, bf16[128,256]{1,0:T(8,128)(2,1)S(1)}, u32[]{:S(2)}, u32[]{:S(2)}) collective-permute-start(bf16[128,256]{1,0:T(8,128)(2,1)S(1)} %get-tuple-element.136), channel_id=1, source_target_pairs={{0,3},{1,0},{2,1},{3,2},{4,7},{5,4},{6,5},{7,6},{8,11},{9,8},{10,9... | collective-permute-start | bytes 196616 | tf_op jit(solution)/shard_map/ppermute | solution.py:24
  249.8 3.2 %collective-permute-done.125 = bf16[128,256]{1,0:T(8,128)(2,1)S(1)} collective-permute-done((bf16[128,256]{1,0:T(8,128)(2,1)S(1)}, bf16[128,256]{1,0:T(8,128)(2,1)S(1)}, u32[]{:S(2)}, u32[]{:S(2)}) %collective-permute-start.125) | collective-permute-done | bytes 65568 | tf_op jit(solution)/shard_map/ppermute | solution.py:24
  (108 shorter events, 69.4 us)
Async XLA Ops:
  0.0 26.5 %collective-permute-start.104 = (bf16[32,1024]{1,0:T(8,128)(2,1)}, bf16[32,1024]{1,0:T(8,128)(2,1)S(1)}, u32[]{:S(2)}, u32[]{:S(2)}) collective-permute-start(bf16[32,1024]{1,0:T(8,128)(2,1)} %param.68), channel_id=1, source_target_pairs={{0,128},{1,129},{2,130},{3,131},{4,132},{5,133},{6,134},{7,135},{8... | collective-permute-start | bytes 196616 | tf_op jit(solution)/shard_map/ppermute | solution.py:24
  9.8 18.0 %collective-permute-start.105 = (bf16[32,1024]{1,0:T(8,128)(2,1)}, bf16[32,1024]{1,0:T(8,128)(2,1)S(1)}, u32[]{:S(2)}, u32[]{:S(2)}) collective-permute-start(bf16[32,1024]{1,0:T(8,128)(2,1)} %param.68), channel_id=1, source_target_pairs={{0,256},{1,257},{2,258},{3,259},{4,260},{5,261},{6,262},{7,263},{8... | collective-permute-start | bytes 196616 | tf_op jit(solution)/shard_map/ppermute | solution.py:24
  20.4 14.3 %collective-permute-start.106 = (bf16[32,1024]{1,0:T(8,128)(2,1)}, bf16[32,1024]{1,0:T(8,128)(2,1)S(1)}, u32[]{:S(2)}, u32[]{:S(2)}) collective-permute-start(bf16[32,1024]{1,0:T(8,128)(2,1)} %param.68), channel_id=1, source_target_pairs={{0,384},{1,385},{2,386},{3,387},{4,388},{5,389},{6,390},{7,391},{8... | collective-permute-start | bytes 196616 | tf_op jit(solution)/shard_map/ppermute | solution.py:24
  34.7 10.8 %collective-permute-start.107 = (bf16[4,32,1024]{2,1,0:T(8,128)(2,1)S(1)}, bf16[4,32,1024]{2,1,0:T(8,128)(2,1)S(1)}, u32[]{:S(2)}, u32[]{:S(2)}) collective-permute-start(bf16[4,32,1024]{2,1,0:T(8,128)(2,1)S(1)} %bitcast_dynamic-update-slice_fusion.26), channel_id=1, source_target_pairs={{0,32},{1,33},{2,34},{3,35},{4,12},{5,13},{6,14},{7,15},{8,40},{9,... | collective-permute-start | bytes 786440 | tf_op jit(solution)/shard_map/ppermute | solution.py:24
  37.9 9.2 %collective-permute-start.108 = (bf16[4,32,1024]{2,1,0:T(8,128)(2,1)S(1)}, bf16[4,32,1024]{2,1,0:T(8,128)(2,1)S(1)}, u32[]{:S(2)}, u32[]{:S(2)}) collective-permute-start(bf16[4,32,1024]{2,1,0:T(8,128)(2,1)S(1)} %bitcast_dynamic-update-slice_fusion.26), channel_id=1, source_target_pairs={{0,64},{1,65},{2,66},{3,67},{4,20},{5,21},{6,22},{7,23},{8,72},{9,... | collective-permute-start | bytes 786440 | tf_op jit(solution)/shard_map/ppermute | solution.py:24
  49.7 38.3 %collective-permute-start.110 = (bf16[4,4,32,1024]{3,2,0,1:T(8,128)(2,1)S(1)}, bf16[4,4,32,1024]{3,2,0,1:T(8,128)(2,1)}, u32[]{:S(2)}, u32[]{:S(2)}) collective-permute-start(bf16[4,4,32,1024]{3,2,0,1:T(8,128)(2,1)S(1)} %bitcast_dynamic-update-slice_fusion.7), channel_id=1, source_target_pairs={{0,8},{1,9},{2,10},{3,11},{4,36},{5,37},{6,38},{7,39},{8,16},{9,17... | collective-permute-start | bytes 3145736 | tf_op jit(solution)/shard_map/ppermute | solution.py:24
  52.9 49.4 %collective-permute-start.111 = (bf16[4,4,32,1024]{3,2,0,1:T(8,128)(2,1)S(1)}, bf16[4,4,32,1024]{3,2,0,1:T(8,128)(2,1)S(1)}, u32[]{:S(2)}, u32[]{:S(2)}) collective-permute-start(bf16[4,4,32,1024]{3,2,0,1:T(8,128)(2,1)S(1)} %bitcast_dynamic-update-slice_fusion.7), channel_id=1, source_target_pairs={{0,16},{1,17},{2,18},{3,19},{4,68},{5,69},{6,70},{7,71},{8,24},{9,... | collective-permute-start | bytes 3145736 | tf_op jit(solution)/shard_map/ppermute | solution.py:24
  58.3 8.9 %collective-permute-start.98 = (bf16[128,1024]{1,0:T(8,128)(2,1)}, bf16[128,1024]{1,0:T(8,128)(2,1)S(1)}, u32[]{:S(2)}, u32[]{:S(2)}) collective-permute-start(bf16[128,1024]{1,0:T(8,128)(2,1)} %get-tuple-element.148), channel_id=1, source_target_pairs={{0,1},{1,2},{2,3},{3,128},{4,5},{5,6},{6,7},{7,132},{8,9},{9,10},{... | collective-permute-start | bytes 786440 | tf_op jit(solution)/shard_map/ppermute | solution.py:24
  60.2 12.3 %collective-permute-start.92 = (bf16[128,1024]{1,0:T(8,128)(2,1)}, bf16[128,1024]{1,0:T(8,128)(2,1)S(1)}, u32[]{:S(2)}, u32[]{:S(2)}) collective-permute-start(bf16[128,1024]{1,0:T(8,128)(2,1)} %get-tuple-element.147), channel_id=1, source_target_pairs={{0,1},{1,2},{2,3},{3,128},{4,5},{5,6},{6,7},{7,132},{8,9},{9,10},{... | collective-permute-start | bytes 786440 | tf_op jit(solution)/shard_map/ppermute | solution.py:24
  62.1 12.6 %collective-permute-start.101 = (bf16[128,1024]{1,0:T(8,128)(2,1)}, bf16[128,1024]{1,0:T(8,128)(2,1)S(1)}, u32[]{:S(2)}, u32[]{:S(2)}) collective-permute-start(bf16[128,1024]{1,0:T(8,128)(2,1)} %get-tuple-element.148), channel_id=1, source_target_pairs={{0,387},{1,0},{2,1},{3,2},{4,391},{5,4},{6,5},{7,6},{8,395},{9,8},... | collective-permute-start | bytes 786440 | tf_op jit(solution)/shard_map/ppermute | solution.py:24
  67.2 38.4 %collective-permute-start.112 = (bf16[4,4,32,1024]{3,2,0,1:T(8,128)(2,1)S(1)}, bf16[4,4,32,1024]{3,2,0,1:T(8,128)(2,1)}, u32[]{:S(2)}, u32[]{:S(2)}) collective-permute-start(bf16[4,4,32,1024]{3,2,0,1:T(8,128)(2,1)S(1)} %bitcast_dynamic-update-slice_fusion.7), channel_id=1, source_target_pairs={{0,24},{1,25},{2,26},{3,27},{4,100},{5,101},{6,102},{7,103},{8,0},... | collective-permute-start | bytes 3145736 | tf_op jit(solution)/shard_map/ppermute | solution.py:24
  72.5 9.0 %collective-permute-start.95 = (bf16[128,1024]{1,0:T(8,128)(2,1)}, bf16[128,1024]{1,0:T(8,128)(2,1)S(1)}, u32[]{:S(2)}, u32[]{:S(2)}) collective-permute-start(bf16[128,1024]{1,0:T(8,128)(2,1)} %get-tuple-element.147), channel_id=1, source_target_pairs={{0,387},{1,0},{2,1},{3,2},{4,391},{5,4},{6,5},{7,6},{8,395},{9,8},... | collective-permute-start | bytes 786440 | tf_op jit(solution)/shard_map/ppermute | solution.py:24
  74.8 8.6 %collective-permute-start.99 = (bf16[128,1024]{1,0:T(8,128)(2,1)S(1)}, bf16[128,1024]{1,0:T(8,128)(2,1)}, u32[]{:S(2)}, u32[]{:S(2)}) collective-permute-start(bf16[128,1024]{1,0:T(8,128)(2,1)S(1)} %collective-permute-done.98), channel_id=1, source_target_pairs={{0,1},{1,2},{2,3},{3,128},{4,5},{5,6},{6,7},{7,132},{8,9},{9,10},{... | collective-permute-start | bytes 786440 | tf_op jit(solution)/shard_map/ppermute | solution.py:24
  81.5 11.1 %collective-permute-start.93 = (bf16[128,1024]{1,0:T(8,128)(2,1)S(1)}, bf16[128,1024]{1,0:T(8,128)(2,1)}, u32[]{:S(2)}, u32[]{:S(2)}) collective-permute-start(bf16[128,1024]{1,0:T(8,128)(2,1)S(1)} %collective-permute-done.92), channel_id=1, source_target_pairs={{0,1},{1,2},{2,3},{3,128},{4,5},{5,6},{6,7},{7,132},{8,9},{9,10},{... | collective-permute-start | bytes 786440 | tf_op jit(solution)/shard_map/ppermute | solution.py:24
  83.4 12.3 %collective-permute-start.102 = (bf16[128,1024]{1,0:T(8,128)(2,1)S(1)}, bf16[128,1024]{1,0:T(8,128)(2,1)}, u32[]{:S(2)}, u32[]{:S(2)}) collective-permute-start(bf16[128,1024]{1,0:T(8,128)(2,1)S(1)} %collective-permute-done.101), channel_id=1, source_target_pairs={{0,387},{1,0},{2,1},{3,2},{4,391},{5,4},{6,5},{7,6},{8,395},{9,8},... | collective-permute-start | bytes 786440 | tf_op jit(solution)/shard_map/ppermute | solution.py:24
  88.0 9.7 %collective-permute-start.96 = (bf16[128,1024]{1,0:T(8,128)(2,1)S(1)}, bf16[128,1024]{1,0:T(8,128)(2,1)}, u32[]{:S(2)}, u32[]{:S(2)}) collective-permute-start(bf16[128,1024]{1,0:T(8,128)(2,1)S(1)} %collective-permute-done.95), channel_id=1, source_target_pairs={{0,387},{1,0},{2,1},{3,2},{4,391},{5,4},{6,5},{7,6},{8,395},{9,8},... | collective-permute-start | bytes 786440 | tf_op jit(solution)/shard_map/ppermute | solution.py:24
  92.6 33.5 %collective-permute-start.100 = (bf16[128,1024]{1,0:T(8,128)(2,1)}, bf16[128,1024]{1,0:T(8,128)(2,1)}, u32[]{:S(2)}, u32[]{:S(2)}) collective-permute-start(bf16[128,1024]{1,0:T(8,128)(2,1)} %collective-permute-done.99), channel_id=1, source_target_pairs={{0,1},{1,2},{2,3},{3,128},{4,5},{5,6},{6,7},{7,132},{8,9},{9,10},{... | collective-permute-start | bytes 786440 | tf_op jit(solution)/shard_map/ppermute | solution.py:24
  95.7 36.8 %collective-permute-start.94 = (bf16[128,1024]{1,0:T(8,128)(2,1)}, bf16[128,1024]{1,0:T(8,128)(2,1)}, u32[]{:S(2)}, u32[]{:S(2)}) collective-permute-start(bf16[128,1024]{1,0:T(8,128)(2,1)} %collective-permute-done.93), channel_id=1, source_target_pairs={{0,1},{1,2},{2,3},{3,128},{4,5},{5,6},{6,7},{7,132},{8,9},{9,10},{... | collective-permute-start | bytes 786440 | tf_op jit(solution)/shard_map/ppermute | solution.py:24
  97.7 30.9 %collective-permute-start.103 = (bf16[128,1024]{1,0:T(8,128)(2,1)}, bf16[128,1024]{1,0:T(8,128)(2,1)}, u32[]{:S(2)}, u32[]{:S(2)}) collective-permute-start(bf16[128,1024]{1,0:T(8,128)(2,1)} %collective-permute-done.102), channel_id=1, source_target_pairs={{0,387},{1,0},{2,1},{3,2},{4,391},{5,4},{6,5},{7,6},{8,395},{9,8},... | collective-permute-start | bytes 786440 | tf_op jit(solution)/shard_map/ppermute | solution.py:24
  102.3 21.0 %collective-permute-start.97 = (bf16[128,1024]{1,0:T(8,128)(2,1)}, bf16[128,1024]{1,0:T(8,128)(2,1)}, u32[]{:S(2)}, u32[]{:S(2)}) collective-permute-start(bf16[128,1024]{1,0:T(8,128)(2,1)} %collective-permute-done.96), channel_id=1, source_target_pairs={{0,387},{1,0},{2,1},{3,2},{4,391},{5,4},{6,5},{7,6},{8,395},{9,8},... | collective-permute-start | bytes 786440 | tf_op jit(solution)/shard_map/ppermute | solution.py:24
  108.0 102.8 %collective-permute-start.113 = (bf16[4,4,4,32,1024]{4,3,1,0,2:T(8,128)(2,1)}, bf16[4,4,4,32,1024]{4,3,1,0,2:T(8,128)(2,1)}, u32[]{:S(2)}, u32[]{:S(2)}) collective-permute-start(bf16[4,4,4,32,1024]{4,3,1,0,2:T(8,128)(2,1)} %bitcast_dynamic-update-slice_fusion.3), channel_id=1, source_target_pairs={{0,4},{1,5},{2,6},{3,7},{4,0},{5,1},{6,2},{7,3},{8,12},{9,13},{10,... | collective-permute-start | bytes 12582920 | tf_op jit(solution)/shard_map/ppermute | solution.py:24
  123.3 19.3 %collective-permute-start.114 = (bf16[128,1024]{1,0:T(8,128)(2,1)}, bf16[128,1024]{1,0:T(8,128)(2,1)S(1)}, u32[]{:S(2)}, u32[]{:S(2)}) collective-permute-start(bf16[128,1024]{1,0:T(8,128)(2,1)} %collective-permute-done.97), channel_id=1, source_target_pairs={{0,387},{1,0},{2,1},{3,2},{4,391},{5,4},{6,5},{7,6},{8,395},{9,8},... | collective-permute-start | bytes 786440 | tf_op jit(solution)/shard_map/ppermute | solution.py:24
  126.1 22.0 %collective-permute-start.117 = (bf16[128,1024]{1,0:T(8,128)(2,1)}, bf16[128,1024]{1,0:T(8,128)(2,1)S(1)}, u32[]{:S(2)}, u32[]{:S(2)}) collective-permute-start(bf16[128,1024]{1,0:T(8,128)(2,1)} %collective-permute-done.100), channel_id=1, source_target_pairs={{0,1},{1,2},{2,3},{3,128},{4,5},{5,6},{6,7},{7,132},{8,9},{9,10},{... | collective-permute-start | bytes 786440 | tf_op jit(solution)/shard_map/ppermute | solution.py:24
  128.6 23.3 %collective-permute-start.115 = (bf16[128,1024]{1,0:T(8,128)(2,1)}, bf16[128,1024]{1,0:T(8,128)(2,1)S(1)}, u32[]{:S(2)}, u32[]{:S(2)}) collective-permute-start(bf16[128,1024]{1,0:T(8,128)(2,1)} %collective-permute-done.103), channel_id=1, source_target_pairs={{0,387},{1,0},{2,1},{3,2},{4,391},{5,4},{6,5},{7,6},{8,395},{9,8},... | collective-permute-start | bytes 786440 | tf_op jit(solution)/shard_map/ppermute | solution.py:24
  132.6 19.4 %collective-permute-start.119 = (bf16[128,1024]{1,0:T(8,128)(2,1)}, bf16[128,1024]{1,0:T(8,128)(2,1)S(1)}, u32[]{:S(2)}, u32[]{:S(2)}) collective-permute-start(bf16[128,1024]{1,0:T(8,128)(2,1)} %collective-permute-done.94), channel_id=1, source_target_pairs={{0,1},{1,2},{2,3},{3,128},{4,5},{5,6},{6,7},{7,132},{8,9},{9,10},{... | collective-permute-start | bytes 786440 | tf_op jit(solution)/shard_map/ppermute | solution.py:24
  142.6 24.9 %collective-permute-start.116 = (bf16[128,1024]{1,0:T(8,128)(2,1)S(1)}, bf16[128,1024]{1,0:T(8,128)(2,1)S(1)}, u32[]{:S(2)}, u32[]{:S(2)}) collective-permute-start(bf16[128,1024]{1,0:T(8,128)(2,1)S(1)} %collective-permute-done.114), channel_id=1, source_target_pairs={{0,384},{1,385},{2,386},{3,387},{4,388},{5,389},{6,390},{7,391},{8... | collective-permute-start | bytes 786440 | tf_op jit(solution)/shard_map/ppermute | solution.py:24
  148.1 19.9 %collective-permute-start.118 = (bf16[128,1024]{1,0:T(8,128)(2,1)S(1)}, bf16[128,1024]{1,0:T(8,128)(2,1)S(1)}, u32[]{:S(2)}, u32[]{:S(2)}) collective-permute-start(bf16[128,1024]{1,0:T(8,128)(2,1)S(1)} %collective-permute-done.117), channel_id=1, source_target_pairs={{0,128},{1,129},{2,130},{3,131},{4,132},{5,133},{6,134},{7,135},{8... | collective-permute-start | bytes 786440 | tf_op jit(solution)/shard_map/ppermute | solution.py:24
  168.5 10.5 %collective-permute-start.8 = (bf16[256,1024]{1,0:T(8,128)(2,1)S(1)}, bf16[256,1024]{1,0:T(8,128)(2,1)S(1)}, u32[]{:S(2)}, u32[]{:S(2)}) collective-permute-start(bf16[256,1024]{1,0:T(8,128)(2,1)S(1)} %param.7), channel_id=1, source_target_pairs={{0,124},{1,125},{2,126},{3,127},{4,0},{5,1},{6,2},{7,3},{8,4},{9,5... | collective-permute-start | bytes 1572872 | tf_op jit(solution)/shard_map/cond/branch_7_fun/ppermute | solution.py:24
  179.0 13.6 %collective-permute-start.9 = (bf16[256,1024]{1,0:T(8,128)(2,1)S(1)}, bf16[256,1024]{1,0:T(8,128)(2,1)S(1)}, u32[]{:S(2)}, u32[]{:S(2)}) collective-permute-start(bf16[256,1024]{1,0:T(8,128)(2,1)S(1)} %collective-permute-done.8), channel_id=1, source_target_pairs={{0,104},{1,105},{2,106},{3,107},{4,108},{5,109},{6,110},{7,111},{8... | collective-permute-start | bytes 1572872 | tf_op jit(solution)/shard_map/cond/branch_7_fun/ppermute | solution.py:24
  192.8 17.9 %collective-permute-start.53 = (bf16[256,1024]{1,0:T(8,128)(2,1)S(1)}, bf16[256,1024]{1,0:T(8,128)(2,1)S(1)}, u32[]{:S(2)}, u32[]{:S(2)}) collective-permute-start(bf16[256,1024]{1,0:T(8,128)(2,1)S(1)} %param.38), channel_id=1, source_target_pairs={{0,104},{1,105},{2,106},{3,107},{4,108},{5,109},{6,110},{7,111},{8... | collective-permute-start | bytes 1572872 | tf_op jit(solution)/shard_map/cond/branch_6_fun/ppermute | solution.py:24
  219.5 17.7 %collective-permute-start.120 = (bf16[128,256]{1,0:T(8,128)(2,1)S(1)}, bf16[128,256]{1,0:T(8,128)(2,1)S(1)}, u32[]{:S(2)}, u32[]{:S(2)}) collective-permute-start(bf16[128,256]{1,0:T(8,128)(2,1)S(1)} %get-tuple-element.149), channel_id=1, source_target_pairs={{0,1},{1,2},{2,3},{3,0},{4,5},{5,6},{6,7},{7,4},{8,9},{9,10},{10,1... | collective-permute-start | bytes 196616 | tf_op jit(solution)/shard_map/ppermute | solution.py:24
  240.6 9.1 %collective-permute-start.123 = (bf16[128,256]{1,0:T(8,128)(2,1)S(1)}, bf16[128,256]{1,0:T(8,128)(2,1)S(1)}, u32[]{:S(2)}, u32[]{:S(2)}) collective-permute-start(bf16[128,256]{1,0:T(8,128)(2,1)S(1)} %get-tuple-element.136), channel_id=1, source_target_pairs={{0,1},{1,2},{2,3},{3,0},{4,5},{5,6},{6,7},{7,4},{8,9},{9,10},{10,1... | collective-permute-start | bytes 196616 | tf_op jit(solution)/shard_map/ppermute | solution.py:24
  (9 other events, 143.3 us)

commit v4 on v0

v4 whole, which is shorter than its diff:
```python
import math

import jax
import jax.numpy as jnp
from jax import lax
from jax.sharding import PartitionSpec as P

K = 4096
BOTH = ("docs", "proj")


def place(index):
    docs, p = divmod(index, 4)
    return docs >> 5, docs >> 3 & 3, docs >> 1 & 3, docs & 1, p


def number(zh, y, x, c, p):
    return ((zh % 4 * 4 + y % 4) * 4 + x % 4) * 8 + c % 2 * 4 + p % 4


def send(value, to):
    return lax.ppermute(value, BOTH, [(i, number(*to(*place(i)))) for i in range(512)])


def tied(first, second):
    return lax.optimization_barrier((first, second))


def put(buffer, piece, at):
    return lax.dynamic_update_slice(
        buffer, piece[None], (at,) + (0,) * (buffer.ndim - 1)
    )


def gather4(value, mine, move):
    out = jnp.zeros((4,) + value.shape, value.dtype)
    out = put(out, value, mine)
    for t in (1, 2, 3):
        out = put(out, send(value, lambda *at: move(t, *at)), (mine - t) % 4)
    return out


def along_zh(t, zh, y, x, c, p):
    return zh + t, y, x, c, p


def along_first(t, zh, y, x, c, p):
    return zh, y + t * (1 - c), x + t * c, c, p


def along_second(t, zh, y, x, c, p):
    return zh, y + t * c, x + t * (1 - c), c, p


def up_z(zh, y, x, c, p):
    z = 4 * zh + p + 1
    return z // 4, y, x, c, z % 4


def down_z(zh, y, x, c, p):
    z = 4 * zh + p - 1
    return z // 4, y, x, c, z % 4


def rotate(value, by, extra):
    def turn(one, shift):
        def move(zh, y, x, c, p):
            m = (y * 8 + x * 2 + c - shift) % 32
            return zh, m >> 3, m >> 1 & 3, m & 1, p

        return send(one, move) if shift else one

    def branch(shift):
        def run(one, more):
            return turn(turn(one, shift % 2), shift - shift % 2), exchange(more)

        return run

    return lax.switch(by, [branch(shift) for shift in range(32)], value, extra)


def exchange(part):
    if part is None:
        return None
    return [
        send(part, lambda zh, y, x, c, p: (zh, y, x, c, p + t)) for t in (1, 2, 3)
    ]


def total(part, others):
    for other in others:
        part = part + other.astype(jnp.float32)
    return part * jnp.float32(1.0 / math.sqrt(K))


def on_device(grads, precond, offsets):
    docs, p = lax.axis_index("docs"), lax.axis_index("proj")
    zh, y, x, c = docs >> 5, docs >> 3 & 3, docs >> 1 & 3, docs & 1
    m = docs % 32

    below, above = [send(grads, up_z)], [send(grads, down_z)]
    held = gather4(precond, (zh - p) % 4, along_zh)
    held, step = tied(held, (below[0], above[0]))
    below.append(send(step[0], up_z))
    above.append(send(step[1], down_z))
    held = gather4(held, jnp.where(c == 0, y, x), along_first)
    held, step = tied(held, (below[1], above[1]))
    below.append(send(step[0], up_z))
    above.append(send(step[1], down_z))
    held = gather4(held, jnp.where(c == 0, x, y), along_second)
    below.append(send(below[2], up_z))
    above.append(send(above[2], down_z))
    held, step = tied(held, (below[3], above[3]))
    below[3], above[3] = step
    other = send(held, lambda zh, y, x, c, p: (zh, y, x, c ^ 1, p))

    half = grads.shape[0] // 2
    far = jnp.concatenate(
        [
            send(above[3][:half], lambda *at: along_zh(-1, *at)),
            send(below[3][half:], lambda *at: along_zh(1, *at)),
        ]
    )

    first = jnp.where(c == 0, held, other).transpose(2, 1, 0, 3, 4)
    second = jnp.where(c == 0, other, held).transpose(2, 0, 1, 3, 4)
    rows = jnp.stack([first, second], axis=3).reshape(4, 1024, precond.shape[1])
    slabs = [grads] + [
        jnp.where(p + i < 4, above[i - 1], below[3 - i]) for i in (1, 2, 3)
    ]
    pre = sum(
        jnp.dot(slabs[i], rows[i], preferred_element_type=jnp.float32) for i in range(4)
    ).astype(jnp.bfloat16)
    far, pre = tied(far, pre)

    blocks = [grads, above[3], far, below[3]]

    def partner(round_, extra):
        low = offsets[round_] % 32
        ahead = (offsets[round_] // 32 + (m < low)) % 4
        value = blocks[0]
        for i in (1, 2, 3):
            value = jnp.where(ahead == i, blocks[i], value)
        return rotate(value, low, extra)

    def gram(other):
        return lax.dot_general(
            pre, other, (((1,), (1,)), ((), ())), preferred_element_type=jnp.float32
        )

    one = gram(partner(0, None)[0])
    moved, ones = partner(1, one.astype(jnp.bfloat16))
    two = gram(moved)
    twos = exchange(two.astype(jnp.bfloat16))
    return jnp.stack([total(one, ones), total(two, twos)])


def solution(mesh):
    placed = (P("docs", "proj"), P("docs", "proj"), P())
    return jax.shard_map(
        on_device, mesh=mesh, in_specs=placed, out_specs=P(None, "docs", None), check_vma=False
    )
```

time: 805 us -> 229 us (0.28)
  waiting for transfers between devices: 689 us -> 64.5 us
  starting transfers between devices: 78.9 us -> 129 us
  between operations: 22.3 us -> 6.29 us
  local copies, waits for them, and re-layouts: 1.34 us -> 12 us
    all_gather x2 -> x0, waiting for transfers between devices: 559 us -> none  [the longest x1 493 us: on_device(): lax.all_gather(precond, 'docs', axis=0, tiled=True)]
    psum x1 -> x0, waiting for transfers between devices: 54.2 us -> none  [on_device(): lax.psum(partial_gram.astype(jnp.bfloat16), 'proj').astype(jnp.float32)]
    ppermute x13 -> x29, starting transfers between devices: 78.8 us -> 129 us  [send(): lax.ppermute(value, BOTH, [(i, number(*to(*place(i)))) for i in range(512)])]
    ppermute x13 -> x29, waiting for transfers between devices: 74.2 us -> 64.5 us  [send(): lax.ppermute(value, BOTH, [(i, number(*to(*place(i)))) for i in range(512)])]
  transfers between devices with their start and end apart: 16 -> 29, of which waited for: 13 -> 14; matrix products, arithmetic and copies ran while one was open for 1% -> 6% of each run, Pallas kernels for 0% -> 0%
where the time goes in v4:
time: 229 us; the launch traced here: 227 us
  starting transfers between devices  129 us (56%)
  waiting for transfers between devices  64.5 us (28%)
  local copies, waits for them, and re-layouts  12 us (5%)
  other arithmetic  7.88 us (3%)
  matrix products  7.6 us (3%)
  between operations  6.29 us (3%)
    ppermute x29, starting transfers between devices, send(): lax.ppermute(value, BOTH, [(i, number(*to(*place(i)))) for i in range(512)])  129 us
    ppermute x29, waiting for transfers between devices, send(): lax.ppermute(value, BOTH, [(i, number(*to(*place(i)))) for i in range(512)])  64.5 us
    dynamic_update_slice x12, local copies, waits for them, and re-layouts, put(): lax.dynamic_update_slice(buffer, piece[None], (at,) + (0,) * (buffer.ndim...  7.79 us
    dot_general x4, matrix products, on_device(): jnp.dot(slabs[i], rows[i], preferred_element_type=jnp.float32)  5.87 us
    another operation x2, other arithmetic, on_device(): rows = jnp.stack([first, second], axis=3).reshape(4, 1024, precond.shape[1])  4.88 us
  transfers between devices with their start and end apart: 29, of which 14 were waited for; matrix products, arithmetic and copies ran while one was open for 6% of the time, Pallas kernels for 0%

profile of v4, /device:TPU:1, one launch (start us, length us, event | category | flops | bytes accessed | tf_op | source)
XLA Modules:
  0.0 227.5 jit_solution(5337689333668950250)
XLA Ops:
  0.0 9.6 %collective-permute-start.188 = (bf16[32,1024]{1,0:T(8,128)(2,1)}, bf16[32,1024]{1,0:T(8,128)(2,1)S(1)}, u32[]{:S(2)}, u32[]{:S(2)}) collective-permute-start(bf16[32,1024]{1,0:T(8,128)(2,1)} %param.68), channel_id=1, source_target_pairs={{0,128},{1,129},{2,130},{3,131},{4,132},{5,133},{6,134},{7,135},{8... | collective-permute-start | bytes 196616 | tf_op jit(solution)/shard_map/ppermute | solution.py:22
  9.6 10.6 %collective-permute-start.189 = (bf16[32,1024]{1,0:T(8,128)(2,1)}, bf16[32,1024]{1,0:T(8,128)(2,1)S(1)}, u32[]{:S(2)}, u32[]{:S(2)}) collective-permute-start(bf16[32,1024]{1,0:T(8,128)(2,1)} %param.68), channel_id=1, source_target_pairs={{0,256},{1,257},{2,258},{3,259},{4,260},{5,261},{6,262},{7,263},{8... | collective-permute-start | bytes 196616 | tf_op jit(solution)/shard_map/ppermute | solution.py:22
  20.3 5.2 %collective-permute-start.190 = (bf16[32,1024]{1,0:T(8,128)(2,1)}, bf16[32,1024]{1,0:T(8,128)(2,1)S(1)}, u32[]{:S(2)}, u32[]{:S(2)}) collective-permute-start(bf16[32,1024]{1,0:T(8,128)(2,1)} %param.68), channel_id=1, source_target_pairs={{0,384},{1,385},{2,386},{3,387},{4,388},{5,389},{6,390},{7,391},{8... | collective-permute-start | bytes 196616 | tf_op jit(solution)/shard_map/ppermute | solution.py:22
  28.1 3.8 %collective-permute-start.192 = (bf16[256,1024]{1,0:T(8,128)(2,1)}, bf16[256,1024]{1,0:T(8,128)(2,1)S(1)}, u32[]{:S(2)}, u32[]{:S(2)}) collective-permute-start(bf16[256,1024]{1,0:T(8,128)(2,1)} %param.67), channel_id=1, source_target_pairs={{0,387},{1,0},{2,1},{3,2},{4,391},{5,4},{6,5},{7,6},{8,395},{9,8},... | collective-permute-start | bytes 1572872 | tf_op jit(solution)/shard_map/ppermute | solution.py:22
  34.6 6.1 %collective-permute-done.191 = bf16[256,1024]{1,0:T(8,128)(2,1)S(1)} collective-permute-done((bf16[256,1024]{1,0:T(8,128)(2,1)}, bf16[256,1024]{1,0:T(8,128)(2,1)S(1)}, u32[]{:S(2)}, u32[]{:S(2)}) %collective-permute-start.191) | collective-permute-done | bytes 524320 | tf_op jit(solution)/shard_map/ppermute | solution.py:22
  43.4 3.1 %collective-permute-start.193 = (bf16[4,32,1024]{2,1,0:T(8,128)(2,1)S(1)}, bf16[4,32,1024]{2,1,0:T(8,128)(2,1)S(1)}, u32[]{:S(2)}, u32[]{:S(2)}) collective-permute-start(bf16[4,32,1024]{2,1,0:T(8,128)(2,1)S(1)} %bitcast_dynamic-update-slice_fusion.8), channel_id=1, source_target_pairs={{0,32},{1,33},{2,34},{3,35},{4,12},{5,13},{6,14},{7,15},{8,40},{9,... | collective-permute-start | bytes 786440 | tf_op jit(solution)/shard_map/ppermute | solution.py:22
  46.6 4.4 %collective-permute-start.194 = (bf16[4,32,1024]{2,1,0:T(8,128)(2,1)S(1)}, bf16[4,32,1024]{2,1,0:T(8,128)(2,1)S(1)}, u32[]{:S(2)}, u32[]{:S(2)}) collective-permute-start(bf16[4,32,1024]{2,1,0:T(8,128)(2,1)S(1)} %bitcast_dynamic-update-slice_fusion.8), channel_id=1, source_target_pairs={{0,64},{1,65},{2,66},{3,67},{4,20},{5,21},{6,22},{7,23},{8,72},{9,... | collective-permute-start | bytes 786440 | tf_op jit(solution)/shard_map/ppermute | solution.py:22
  51.0 3.1 %collective-permute-start.195 = (bf16[4,32,1024]{2,1,0:T(8,128)(2,1)S(1)}, bf16[4,32,1024]{2,1,0:T(8,128)(2,1)S(1)}, u32[]{:S(2)}, u32[]{:S(2)}) collective-permute-start(bf16[4,32,1024]{2,1,0:T(8,128)(2,1)S(1)} %bitcast_dynamic-update-slice_fusion.8), channel_id=1, source_target_pairs={{0,96},{1,97},{2,98},{3,99},{4,28},{5,29},{6,30},{7,31},{8,104},{9... | collective-permute-start | bytes 786440 | tf_op jit(solution)/shard_map/ppermute | solution.py:22
  56.4 4.2 %collective-permute-start.197 = (bf16[256,1024]{1,0:T(8,128)(2,1)S(1)}, bf16[256,1024]{1,0:T(8,128)(2,1)}, u32[]{:S(2)}, u32[]{:S(2)}) collective-permute-start(bf16[256,1024]{1,0:T(8,128)(2,1)S(1)} %collective-permute-done.192), channel_id=1, source_target_pairs={{0,387},{1,0},{2,1},{3,2},{4,391},{5,4},{6,5},{7,6},{8,395},{9,8},... | collective-permute-start | bytes 1572872 | tf_op jit(solution)/shard_map/ppermute | solution.py:22
  60.8 6.9 %collective-permute-done.196 = bf16[256,1024]{1,0:T(8,128)(2,1)} collective-permute-done((bf16[256,1024]{1,0:T(8,128)(2,1)S(1)}, bf16[256,1024]{1,0:T(8,128)(2,1)}, u32[]{:S(2)}, u32[]{:S(2)}) %collective-permute-start.196) | collective-permute-done | bytes 524320 | tf_op jit(solution)/shard_map/ppermute | solution.py:22
  68.8 4.1 %collective-permute-start.198 = (bf16[4,4,32,1024]{3,2,0,1:T(8,128)(2,1)S(1)}, bf16[4,4,32,1024]{3,2,0,1:T(8,128)(2,1)}, u32[]{:S(2)}, u32[]{:S(2)}) collective-permute-start(bf16[4,4,32,1024]{3,2,0,1:T(8,128)(2,1)S(1)} %bitcast_dynamic-update-slice_fusion.7), channel_id=1, source_target_pairs={{0,8},{1,9},{2,10},{3,11},{4,36},{5,37},{6,38},{7,39},{8,16},{9,17... | collective-permute-start | bytes 3145736 | tf_op jit(solution)/shard_map/ppermute | solution.py:22
  72.9 6.7 %collective-permute-start.199 = (bf16[4,4,32,1024]{3,2,0,1:T(8,128)(2,1)S(1)}, bf16[4,4,32,1024]{3,2,0,1:T(8,128)(2,1)S(1)}, u32[]{:S(2)}, u32[]{:S(2)}) collective-permute-start(bf16[4,4,32,1024]{3,2,0,1:T(8,128)(2,1)S(1)} %bitcast_dynamic-update-slice_fusion.7), channel_id=1, source_target_pairs={{0,16},{1,17},{2,18},{3,19},{4,68},{5,69},{6,70},{7,71},{8,24},{9,... | collective-permute-start | bytes 3145736 | tf_op jit(solution)/shard_map/ppermute | solution.py:22
  79.6 3.6 %collective-permute-start.201 = (bf16[256,1024]{1,0:T(8,128)(2,1)}, bf16[256,1024]{1,0:T(8,128)(2,1)}, u32[]{:S(2)}, u32[]{:S(2)}) collective-permute-start(bf16[256,1024]{1,0:T(8,128)(2,1)} %collective-permute-done.196), channel_id=1, source_target_pairs={{0,1},{1,2},{2,3},{3,128},{4,5},{5,6},{6,7},{7,132},{8,9},{9,10},{... | collective-permute-start | bytes 1572872 | tf_op jit(solution)/shard_map/ppermute | solution.py:22
  83.3 3.5 %collective-permute-start.203 = (bf16[256,1024]{1,0:T(8,128)(2,1)}, bf16[256,1024]{1,0:T(8,128)(2,1)}, u32[]{:S(2)}, u32[]{:S(2)}) collective-permute-start(bf16[256,1024]{1,0:T(8,128)(2,1)} %collective-permute-done.197), channel_id=1, source_target_pairs={{0,387},{1,0},{2,1},{3,2},{4,391},{5,4},{6,5},{7,6},{8,395},{9,8},... | collective-permute-start | bytes 1572872 | tf_op jit(solution)/shard_map/ppermute | solution.py:22
  93.3 3.9 %collective-permute-done.201 = bf16[256,1024]{1,0:T(8,128)(2,1)} collective-permute-done((bf16[256,1024]{1,0:T(8,128)(2,1)}, bf16[256,1024]{1,0:T(8,128)(2,1)}, u32[]{:S(2)}, u32[]{:S(2)}) %collective-permute-start.201) | collective-permute-done | bytes 524320 | tf_op jit(solution)/shard_map/ppermute | solution.py:22
  99.1 4.8 %collective-permute-start.204 = (bf16[256,1024]{1,0:T(8,128)(2,1)}, bf16[256,1024]{1,0:T(8,128)(2,1)S(1)}, u32[]{:S(2)}, u32[]{:S(2)}) collective-permute-start(bf16[256,1024]{1,0:T(8,128)(2,1)} %collective-permute-done.203), channel_id=1, source_target_pairs={{0,387},{1,0},{2,1},{3,2},{4,391},{5,4},{6,5},{7,6},{8,395},{9,8},... | collective-permute-start | bytes 1572872 | tf_op jit(solution)/shard_map/ppermute | solution.py:22
  109.7 4.3 %collective-permute-done.202 = bf16[256,1024]{1,0:T(8,128)(2,1)S(1)} collective-permute-done((bf16[256,1024]{1,0:T(8,128)(2,1)}, bf16[256,1024]{1,0:T(8,128)(2,1)S(1)}, u32[]{:S(2)}, u32[]{:S(2)}) %collective-permute-start.202) | collective-permute-done | bytes 524320 | tf_op jit(solution)/shard_map/ppermute | solution.py:22
  115.3 3.0 %collective-permute-start.207 = (bf16[4,4,4,32,1024]{4,3,1,0,2:T(8,128)(2,1)}, bf16[4,4,4,32,1024]{4,3,1,0,2:T(8,128)(2,1)}, u32[]{:S(2)}, u32[]{:S(2)}) collective-permute-start(bf16[4,4,4,32,1024]{4,3,1,0,2:T(8,128)(2,1)} %bitcast_dynamic-update-slice_fusion.3), channel_id=1, source_target_pairs={{0,4},{1,5},{2,6},{3,7},{4,0},{5,1},{6,2},{7,3},{8,12},{9,13},{10,... | collective-permute-start | bytes 12582920 | tf_op jit(solution)/shard_map/ppermute | solution.py:22
  118.3 6.2 %collective-permute-start.205 = (bf16[128,1024]{1,0:T(8,128)(2,1)S(1)}, bf16[128,1024]{1,0:T(8,128)(2,1)S(1)}, u32[]{:S(2)}, u32[]{:S(2)}) collective-permute-start(bf16[128,1024]{1,0:T(8,128)(2,1)S(1)} %slice.30), channel_id=1, source_target_pairs={{0,384},{1,385},{2,386},{3,387},{4,388},{5,389},{6,390},{7,391},{8... | collective-permute-start | bytes 786440 | tf_op jit(solution)/shard_map/ppermute | solution.py:22
  124.5 3.0 %collective-permute-start.206 = (bf16[128,1024]{1,0:T(8,128)(2,1)S(1)}, bf16[128,1024]{1,0:T(8,128)(2,1)S(1)}, u32[]{:S(2)}, u32[]{:S(2)}) collective-permute-start(bf16[128,1024]{1,0:T(8,128)(2,1)S(1)} %slice.31), channel_id=1, source_target_pairs={{0,128},{1,129},{2,130},{3,131},{4,132},{5,133},{6,134},{7,135},{8... | collective-permute-start | bytes 786440 | tf_op jit(solution)/shard_map/ppermute | solution.py:22
  133.9 8.8 %collective-permute-done.205 = bf16[128,1024]{1,0:T(8,128)(2,1)S(1)} collective-permute-done((bf16[128,1024]{1,0:T(8,128)(2,1)S(1)}, bf16[128,1024]{1,0:T(8,128)(2,1)S(1)}, u32[]{:S(2)}, u32[]{:S(2)}) %collective-permute-start.205) | collective-permute-done | bytes 262176 | tf_op jit(solution)/shard_map/ppermute | solution.py:22
  142.7 3.8 %select_bitcast_fusion.1 = (bf16[4,4,4,1,32,1024]{5,4,1,2,0,3:T(8,128)(2,1)S(1)}, bf16[4,4,4,1,32,1024]{5,4,3,2,1,0:T(8,128)(2,1)S(1)}) fusion(bf16[4,4,4,32,1024]{4,3,1,0,2:T(8,128)(2,1)} %bitcast_dynamic-update-slice_fusion.3, bf16[4,4,4,32,1024]{4,3,1,0,2:T(8,128)(2,1)} %collective-permute-done.207, pred[]{:T(512)S(6)} %eq.40), kind=kLoop, calls=%fused_computation.7 | loop fusion | flops 4194304 | bytes 16777216 | tf_op jit(solution)/shard_map/stack | solution.py:127
  154.5 26.5 %conditional.4 = (bf16[256,1024]{1,0:T(8,128)(2,1)S(1)}) conditional(s32[]{:T(128)} %clamp.6, bf16[256,1024]{1,0:T(8,128)(2,1)S(1)} %get-tuple-element.329, bf16[256,1024]{1,0:T(8,128)(2,1)S(1)} %get-tuple-element.329, bf16[256,1024]{1,0:T(8,128)(2,1)S(1)} %get-tuple-element.329, ...), branch_computations={%region_0.1_spmd, %region_1.2_spmd, %region_2.3_spmd, %region_3.4_... | conditional | bytes 5242968 | solution.py:79
  157.3 9.0 %collective-permute-done.14 = bf16[256,1024]{1,0:T(8,128)(2,1)S(1)} collective-permute-done((bf16[256,1024]{1,0:T(8,128)(2,1)S(1)}, bf16[256,1024]{1,0:T(8,128)(2,1)S(1)}, u32[]{:S(2)}, u32[]{:S(2)}) %collective-permute-start.14) | collective-permute-done | bytes 524320 | tf_op jit(solution)/shard_map/cond/branch_11_fun/ppermute | solution.py:22
  166.3 6.6 %collective-permute-start.15 = (bf16[256,1024]{1,0:T(8,128)(2,1)S(1)}, bf16[256,1024]{1,0:T(8,128)(2,1)S(1)}, u32[]{:S(2)}, u32[]{:S(2)}) collective-permute-start(bf16[256,1024]{1,0:T(8,128)(2,1)S(1)} %collective-permute-done.14), channel_id=1, source_target_pairs={{0,88},{1,89},{2,90},{3,91},{4,92},{5,93},{6,94},{7,95},{8,96},{9,... | collective-permute-start | bytes 1572872 | tf_op jit(solution)/shard_map/cond/branch_11_fun/ppermute | solution.py:22
  172.9 8.0 %collective-permute-done.15 = bf16[256,1024]{1,0:T(8,128)(2,1)S(1)} collective-permute-done((bf16[256,1024]{1,0:T(8,128)(2,1)S(1)}, bf16[256,1024]{1,0:T(8,128)(2,1)S(1)}, u32[]{:S(2)}, u32[]{:S(2)}) %collective-permute-start.15) | collective-permute-done | bytes 524320 | tf_op jit(solution)/shard_map/cond/branch_11_fun/ppermute | solution.py:22
  181.5 28.6 %conditional.6 = (bf16[256,1024]{1,0:T(8,128)(2,1)}, bf16[256,256]{1,0:T(8,128)(2,1)}, bf16[256,256]{1,0:T(8,128)(2,1)}, bf16[256,256]{1,0:T(8,128)(2,1)}) conditional(s32[]{:T(128)} %clamp.7, (bf16[256,256]{1,0:T(8,128)(2,1)S(1)}, bf16[256,1024]{1,0:T(8,128)(2,1)}) %tuple.495, (bf16[256,1024]{1,0:T(8,128)(2,1)}, ...), branch_computations={%region_32.33_spmd, %region_33.34_spmd, %region_34.35_spmd, %regio... | conditional | bytes 5767400
  185.3 15.4 %collective-permute-start.51 = (bf16[256,256]{1,0:T(8,128)(2,1)S(1)}, bf16[256,256]{1,0:T(8,128)(2,1)}, u32[]{:S(2)}, u32[]{:S(2)}) collective-permute-start(bf16[256,256]{1,0:T(8,128)(2,1)S(1)} %get-tuple-element.221), channel_id=1, source_target_pairs={{0,2},{1,3},{2,0},{3,1},{4,6},{5,7},{6,4},{7,5},{8,10},{9,11},{10,... | collective-permute-start | bytes 393224 | tf_op jit(solution)/shard_map/cond/branch_1_fun/ppermute | solution.py:22
  203.5 5.3 %collective-permute-done.51 = bf16[256,256]{1,0:T(8,128)(2,1)} collective-permute-done((bf16[256,256]{1,0:T(8,128)(2,1)S(1)}, bf16[256,256]{1,0:T(8,128)(2,1)}, u32[]{:S(2)}, u32[]{:S(2)}) %collective-permute-start.51) | collective-permute-done | bytes 131104 | tf_op jit(solution)/shard_map/cond/branch_1_fun/ppermute | solution.py:22
  211.5 3.7 %collective-permute-start.208 = (bf16[256,256]{1,0:T(8,128)(2,1)S(1)}, bf16[256,256]{1,0:T(8,128)(2,1)S(1)}, u32[]{:S(2)}, u32[]{:S(2)}) collective-permute-start(bf16[256,256]{1,0:T(8,128)(2,1)S(1)} %get-tuple-element.334), channel_id=1, source_target_pairs={{0,1},{1,2},{2,3},{3,0},{4,5},{5,6},{6,7},{7,4},{8,9},{9,10},{10,1... | collective-permute-start | bytes 393224 | tf_op jit(solution)/shard_map/ppermute | solution.py:22
  217.1 4.0 %collective-permute-start.210 = (bf16[256,256]{1,0:T(8,128)(2,1)S(1)}, bf16[256,256]{1,0:T(8,128)(2,1)S(1)}, u32[]{:S(2)}, u32[]{:S(2)}) collective-permute-start(bf16[256,256]{1,0:T(8,128)(2,1)S(1)} %get-tuple-element.334), channel_id=1, source_target_pairs={{0,3},{1,0},{2,1},{3,2},{4,7},{5,4},{6,5},{7,6},{8,11},{9,8},{10,9... | collective-permute-start | bytes 393224 | tf_op jit(solution)/shard_map/ppermute | solution.py:22
  222.2 4.3 %collective-permute-done.209 = bf16[256,256]{1,0:T(8,128)(2,1)S(1)} collective-permute-done((bf16[256,256]{1,0:T(8,128)(2,1)S(1)}, bf16[256,256]{1,0:T(8,128)(2,1)S(1)}, u32[]{:S(2)}, u32[]{:S(2)}) %collective-permute-start.209) | collective-permute-done | bytes 131104 | tf_op jit(solution)/shard_map/ppermute | solution.py:22
  (73 shorter events, 51.9 us)
Async XLA Ops:
  0.0 32.9 %collective-permute-start.188 = (bf16[32,1024]{1,0:T(8,128)(2,1)}, bf16[32,1024]{1,0:T(8,128)(2,1)S(1)}, u32[]{:S(2)}, u32[]{:S(2)}) collective-permute-start(bf16[32,1024]{1,0:T(8,128)(2,1)} %param.68), channel_id=1, source_target_pairs={{0,128},{1,129},{2,130},{3,131},{4,132},{5,133},{6,134},{7,135},{8... | collective-permute-start | bytes 196616 | tf_op jit(solution)/shard_map/ppermute | solution.py:22
  9.6 23.3 %collective-permute-start.189 = (bf16[32,1024]{1,0:T(8,128)(2,1)}, bf16[32,1024]{1,0:T(8,128)(2,1)S(1)}, u32[]{:S(2)}, u32[]{:S(2)}) collective-permute-start(bf16[32,1024]{1,0:T(8,128)(2,1)} %param.68), channel_id=1, source_target_pairs={{0,256},{1,257},{2,258},{3,259},{4,260},{5,261},{6,262},{7,263},{8... | collective-permute-start | bytes 196616 | tf_op jit(solution)/shard_map/ppermute | solution.py:22
  20.3 14.3 %collective-permute-start.190 = (bf16[32,1024]{1,0:T(8,128)(2,1)}, bf16[32,1024]{1,0:T(8,128)(2,1)S(1)}, u32[]{:S(2)}, u32[]{:S(2)}) collective-permute-start(bf16[32,1024]{1,0:T(8,128)(2,1)} %param.68), channel_id=1, source_target_pairs={{0,384},{1,385},{2,386},{3,387},{4,388},{5,389},{6,390},{7,391},{8... | collective-permute-start | bytes 196616 | tf_op jit(solution)/shard_map/ppermute | solution.py:22
  25.5 15.2 %collective-permute-start.191 = (bf16[256,1024]{1,0:T(8,128)(2,1)}, bf16[256,1024]{1,0:T(8,128)(2,1)S(1)}, u32[]{:S(2)}, u32[]{:S(2)}) collective-permute-start(bf16[256,1024]{1,0:T(8,128)(2,1)} %param.67), channel_id=1, source_target_pairs={{0,1},{1,2},{2,3},{3,128},{4,5},{5,6},{6,7},{7,132},{8,9},{9,10},{... | collective-permute-start | bytes 1572872 | tf_op jit(solution)/shard_map/ppermute | solution.py:22
  28.1 15.3 %collective-permute-start.192 = (bf16[256,1024]{1,0:T(8,128)(2,1)}, bf16[256,1024]{1,0:T(8,128)(2,1)S(1)}, u32[]{:S(2)}, u32[]{:S(2)}) collective-permute-start(bf16[256,1024]{1,0:T(8,128)(2,1)} %param.67), channel_id=1, source_target_pairs={{0,387},{1,0},{2,1},{3,2},{4,391},{5,4},{6,5},{7,6},{8,395},{9,8},... | collective-permute-start | bytes 1572872 | tf_op jit(solution)/shard_map/ppermute | solution.py:22
  40.7 52.6 %copy-start.1 = (bf16[256,1024]{1,0:T(8,128)(2,1)}, bf16[256,1024]{1,0:T(8,128)(2,1)S(1)}, u32[]{:S(2)}) copy-start(bf16[256,1024]{1,0:T(8,128)(2,1)S(1)} %collective-permute-done.191) | copy-start | bytes 1572868
  43.4 25.4 %copy-start.3 = (bf16[256,1024]{1,0:T(8,128)(2,1)}, bf16[256,1024]{1,0:T(8,128)(2,1)S(1)}, u32[]{:S(2)}) copy-start(bf16[256,1024]{1,0:T(8,128)(2,1)S(1)} %collective-permute-done.192) | copy-start | bytes 1572868
  43.4 17.3 %collective-permute-start.193 = (bf16[4,32,1024]{2,1,0:T(8,128)(2,1)S(1)}, bf16[4,32,1024]{2,1,0:T(8,128)(2,1)S(1)}, u32[]{:S(2)}, u32[]{:S(2)}) collective-permute-start(bf16[4,32,1024]{2,1,0:T(8,128)(2,1)S(1)} %bitcast_dynamic-update-slice_fusion.8), channel_id=1, source_target_pairs={{0,32},{1,33},{2,34},{3,35},{4,12},{5,13},{6,14},{7,15},{8,40},{9,... | collective-permute-start | bytes 786440 | tf_op jit(solution)/shard_map/ppermute | solution.py:22
  46.6 14.2 %collective-permute-start.194 = (bf16[4,32,1024]{2,1,0:T(8,128)(2,1)S(1)}, bf16[4,32,1024]{2,1,0:T(8,128)(2,1)S(1)}, u32[]{:S(2)}, u32[]{:S(2)}) collective-permute-start(bf16[4,32,1024]{2,1,0:T(8,128)(2,1)S(1)} %bitcast_dynamic-update-slice_fusion.8), channel_id=1, source_target_pairs={{0,64},{1,65},{2,66},{3,67},{4,20},{5,21},{6,22},{7,23},{8,72},{9,... | collective-permute-start | bytes 786440 | tf_op jit(solution)/shard_map/ppermute | solution.py:22
  51.0 9.8 %collective-permute-start.195 = (bf16[4,32,1024]{2,1,0:T(8,128)(2,1)S(1)}, bf16[4,32,1024]{2,1,0:T(8,128)(2,1)S(1)}, u32[]{:S(2)}, u32[]{:S(2)}) collective-permute-start(bf16[4,32,1024]{2,1,0:T(8,128)(2,1)S(1)} %bitcast_dynamic-update-slice_fusion.8), channel_id=1, source_target_pairs={{0,96},{1,97},{2,98},{3,99},{4,28},{5,29},{6,30},{7,31},{8,104},{9... | collective-permute-start | bytes 786440 | tf_op jit(solution)/shard_map/ppermute | solution.py:22
  54.0 13.7 %collective-permute-start.196 = (bf16[256,1024]{1,0:T(8,128)(2,1)S(1)}, bf16[256,1024]{1,0:T(8,128)(2,1)}, u32[]{:S(2)}, u32[]{:S(2)}) collective-permute-start(bf16[256,1024]{1,0:T(8,128)(2,1)S(1)} %collective-permute-done.191), channel_id=1, source_target_pairs={{0,1},{1,2},{2,3},{3,128},{4,5},{5,6},{6,7},{7,132},{8,9},{9,10},{... | collective-permute-start | bytes 1572872 | tf_op jit(solution)/shard_map/ppermute | solution.py:22
  56.4 12.4 %collective-permute-start.197 = (bf16[256,1024]{1,0:T(8,128)(2,1)S(1)}, bf16[256,1024]{1,0:T(8,128)(2,1)}, u32[]{:S(2)}, u32[]{:S(2)}) collective-permute-start(bf16[256,1024]{1,0:T(8,128)(2,1)S(1)} %collective-permute-done.192), channel_id=1, source_target_pairs={{0,387},{1,0},{2,1},{3,2},{4,391},{5,4},{6,5},{7,6},{8,395},{9,8},... | collective-permute-start | bytes 1572872 | tf_op jit(solution)/shard_map/ppermute | solution.py:22
  68.8 35.2 %collective-permute-start.198 = (bf16[4,4,32,1024]{3,2,0,1:T(8,128)(2,1)S(1)}, bf16[4,4,32,1024]{3,2,0,1:T(8,128)(2,1)}, u32[]{:S(2)}, u32[]{:S(2)}) collective-permute-start(bf16[4,4,32,1024]{3,2,0,1:T(8,128)(2,1)S(1)} %bitcast_dynamic-update-slice_fusion.7), channel_id=1, source_target_pairs={{0,8},{1,9},{2,10},{3,11},{4,36},{5,37},{6,38},{7,39},{8,16},{9,17... | collective-permute-start | bytes 3145736 | tf_op jit(solution)/shard_map/ppermute | solution.py:22
  72.9 33.4 %collective-permute-start.199 = (bf16[4,4,32,1024]{3,2,0,1:T(8,128)(2,1)S(1)}, bf16[4,4,32,1024]{3,2,0,1:T(8,128)(2,1)S(1)}, u32[]{:S(2)}, u32[]{:S(2)}) collective-permute-start(bf16[4,4,32,1024]{3,2,0,1:T(8,128)(2,1)S(1)} %bitcast_dynamic-update-slice_fusion.7), channel_id=1, source_target_pairs={{0,16},{1,17},{2,18},{3,19},{4,68},{5,69},{6,70},{7,71},{8,24},{9,... | collective-permute-start | bytes 3145736 | tf_op jit(solution)/shard_map/ppermute | solution.py:22
  79.6 17.5 %collective-permute-start.201 = (bf16[256,1024]{1,0:T(8,128)(2,1)}, bf16[256,1024]{1,0:T(8,128)(2,1)}, u32[]{:S(2)}, u32[]{:S(2)}) collective-permute-start(bf16[256,1024]{1,0:T(8,128)(2,1)} %collective-permute-done.196), channel_id=1, source_target_pairs={{0,1},{1,2},{2,3},{3,128},{4,5},{5,6},{6,7},{7,132},{8,9},{9,10},{... | collective-permute-start | bytes 1572872 | tf_op jit(solution)/shard_map/ppermute | solution.py:22
  83.3 15.8 %collective-permute-start.203 = (bf16[256,1024]{1,0:T(8,128)(2,1)}, bf16[256,1024]{1,0:T(8,128)(2,1)}, u32[]{:S(2)}, u32[]{:S(2)}) collective-permute-start(bf16[256,1024]{1,0:T(8,128)(2,1)} %collective-permute-done.197), channel_id=1, source_target_pairs={{0,387},{1,0},{2,1},{3,2},{4,391},{5,4},{6,5},{7,6},{8,395},{9,8},... | collective-permute-start | bytes 1572872 | tf_op jit(solution)/shard_map/ppermute | solution.py:22
  86.7 20.6 %collective-permute-start.200 = (bf16[4,4,32,1024]{3,2,0,1:T(8,128)(2,1)S(1)}, bf16[4,4,32,1024]{3,2,0,1:T(8,128)(2,1)}, u32[]{:S(2)}, u32[]{:S(2)}) collective-permute-start(bf16[4,4,32,1024]{3,2,0,1:T(8,128)(2,1)S(1)} %bitcast_dynamic-update-slice_fusion.7), channel_id=1, source_target_pairs={{0,24},{1,25},{2,26},{3,27},{4,100},{5,101},{6,102},{7,103},{8,0},... | collective-permute-start | bytes 3145736 | tf_op jit(solution)/shard_map/ppermute | solution.py:22
  93.3 34.2 %copy-start.5 = (s32[2]{0:T(128)S(1)}, s32[2]{0:T(128)}, u32[]{:S(2)}) copy-start(s32[2]{0:T(128)} %param.69) | copy-start | bytes 28
  97.2 16.8 %collective-permute-start.202 = (bf16[256,1024]{1,0:T(8,128)(2,1)}, bf16[256,1024]{1,0:T(8,128)(2,1)S(1)}, u32[]{:S(2)}, u32[]{:S(2)}) collective-permute-start(bf16[256,1024]{1,0:T(8,128)(2,1)} %collective-permute-done.201), channel_id=1, source_target_pairs={{0,1},{1,2},{2,3},{3,128},{4,5},{5,6},{6,7},{7,132},{8,9},{9,10},{... | collective-permute-start | bytes 1572872 | tf_op jit(solution)/shard_map/ppermute | solution.py:22
  99.1 16.2 %collective-permute-start.204 = (bf16[256,1024]{1,0:T(8,128)(2,1)}, bf16[256,1024]{1,0:T(8,128)(2,1)S(1)}, u32[]{:S(2)}, u32[]{:S(2)}) collective-permute-start(bf16[256,1024]{1,0:T(8,128)(2,1)} %collective-permute-done.203), channel_id=1, source_target_pairs={{0,387},{1,0},{2,1},{3,2},{4,391},{5,4},{6,5},{7,6},{8,395},{9,8},... | collective-permute-start | bytes 1572872 | tf_op jit(solution)/shard_map/ppermute | solution.py:22
  115.3 27.4 %collective-permute-start.207 = (bf16[4,4,4,32,1024]{4,3,1,0,2:T(8,128)(2,1)}, bf16[4,4,4,32,1024]{4,3,1,0,2:T(8,128)(2,1)}, u32[]{:S(2)}, u32[]{:S(2)}) collective-permute-start(bf16[4,4,4,32,1024]{4,3,1,0,2:T(8,128)(2,1)} %bitcast_dynamic-update-slice_fusion.3), channel_id=1, source_target_pairs={{0,4},{1,5},{2,6},{3,7},{4,0},{5,1},{6,2},{7,3},{8,12},{9,13},{10,... | collective-permute-start | bytes 12582920 | tf_op jit(solution)/shard_map/ppermute | solution.py:22
  118.3 24.3 %collective-permute-start.205 = (bf16[128,1024]{1,0:T(8,128)(2,1)S(1)}, bf16[128,1024]{1,0:T(8,128)(2,1)S(1)}, u32[]{:S(2)}, u32[]{:S(2)}) collective-permute-start(bf16[128,1024]{1,0:T(8,128)(2,1)S(1)} %slice.30), channel_id=1, source_target_pairs={{0,384},{1,385},{2,386},{3,387},{4,388},{5,389},{6,390},{7,391},{8... | collective-permute-start | bytes 786440 | tf_op jit(solution)/shard_map/ppermute | solution.py:22
  124.5 18.1 %collective-permute-start.206 = (bf16[128,1024]{1,0:T(8,128)(2,1)S(1)}, bf16[128,1024]{1,0:T(8,128)(2,1)S(1)}, u32[]{:S(2)}, u32[]{:S(2)}) collective-permute-start(bf16[128,1024]{1,0:T(8,128)(2,1)S(1)} %slice.31), channel_id=1, source_target_pairs={{0,128},{1,129},{2,130},{3,131},{4,132},{5,133},{6,134},{7,135},{8... | collective-permute-start | bytes 786440 | tf_op jit(solution)/shard_map/ppermute | solution.py:22
  154.5 11.7 %collective-permute-start.14 = (bf16[256,1024]{1,0:T(8,128)(2,1)S(1)}, bf16[256,1024]{1,0:T(8,128)(2,1)S(1)}, u32[]{:S(2)}, u32[]{:S(2)}) collective-permute-start(bf16[256,1024]{1,0:T(8,128)(2,1)S(1)} %param.11), channel_id=1, source_target_pairs={{0,124},{1,125},{2,126},{3,127},{4,0},{5,1},{6,2},{7,3},{8,4},{9,5... | collective-permute-start | bytes 1572872 | tf_op jit(solution)/shard_map/cond/branch_11_fun/ppermute | solution.py:22
  166.3 14.6 %collective-permute-start.15 = (bf16[256,1024]{1,0:T(8,128)(2,1)S(1)}, bf16[256,1024]{1,0:T(8,128)(2,1)S(1)}, u32[]{:S(2)}, u32[]{:S(2)}) collective-permute-start(bf16[256,1024]{1,0:T(8,128)(2,1)S(1)} %collective-permute-done.14), channel_id=1, source_target_pairs={{0,88},{1,89},{2,90},{3,91},{4,92},{5,93},{6,94},{7,95},{8,96},{9,... | collective-permute-start | bytes 1572872 | tf_op jit(solution)/shard_map/cond/branch_11_fun/ppermute | solution.py:22
  181.5 21.2 %collective-permute-start.49 = (bf16[256,1024]{1,0:T(8,128)(2,1)}, bf16[256,1024]{1,0:T(8,128)(2,1)S(1)}, u32[]{:S(2)}, u32[]{:S(2)}) collective-permute-start(bf16[256,1024]{1,0:T(8,128)(2,1)} %get-tuple-element.220), channel_id=1, source_target_pairs={{0,124},{1,125},{2,126},{3,127},{4,0},{5,1},{6,2},{7,3},{8,4},{9,5... | collective-permute-start | bytes 1572872 | tf_op jit(solution)/shard_map/cond/branch_1_fun/ppermute | solution.py:22
  183.4 20.1 %collective-permute-start.50 = (bf16[256,256]{1,0:T(8,128)(2,1)S(1)}, bf16[256,256]{1,0:T(8,128)(2,1)}, u32[]{:S(2)}, u32[]{:S(2)}) collective-permute-start(bf16[256,256]{1,0:T(8,128)(2,1)S(1)} %get-tuple-element.221), channel_id=1, source_target_pairs={{0,1},{1,2},{2,3},{3,0},{4,5},{5,6},{6,7},{7,4},{8,9},{9,10},{10,1... | collective-permute-start | bytes 393224 | tf_op jit(solution)/shard_map/cond/branch_1_fun/ppermute | solution.py:22
  185.3 23.4 %collective-permute-start.51 = (bf16[256,256]{1,0:T(8,128)(2,1)S(1)}, bf16[256,256]{1,0:T(8,128)(2,1)}, u32[]{:S(2)}, u32[]{:S(2)}) collective-permute-start(bf16[256,256]{1,0:T(8,128)(2,1)S(1)} %get-tuple-element.221), channel_id=1, source_target_pairs={{0,2},{1,3},{2,0},{3,1},{4,6},{5,7},{6,4},{7,5},{8,10},{9,11},{10,... | collective-permute-start | bytes 393224 | tf_op jit(solution)/shard_map/cond/branch_1_fun/ppermute | solution.py:22
  200.8 9.3 %collective-permute-start.52 = (bf16[256,256]{1,0:T(8,128)(2,1)S(1)}, bf16[256,256]{1,0:T(8,128)(2,1)}, u32[]{:S(2)}, u32[]{:S(2)}) collective-permute-start(bf16[256,256]{1,0:T(8,128)(2,1)S(1)} %get-tuple-element.221), channel_id=1, source_target_pairs={{0,3},{1,0},{2,1},{3,2},{4,7},{5,4},{6,5},{7,6},{8,11},{9,8},{10,9... | collective-permute-start | bytes 393224 | tf_op jit(solution)/shard_map/cond/branch_1_fun/ppermute | solution.py:22
  211.5 10.8 %collective-permute-start.208 = (bf16[256,256]{1,0:T(8,128)(2,1)S(1)}, bf16[256,256]{1,0:T(8,128)(2,1)S(1)}, u32[]{:S(2)}, u32[]{:S(2)}) collective-permute-start(bf16[256,256]{1,0:T(8,128)(2,1)S(1)} %get-tuple-element.334), channel_id=1, source_target_pairs={{0,1},{1,2},{2,3},{3,0},{4,5},{5,6},{6,7},{7,4},{8,9},{9,10},{10,1... | collective-permute-start | bytes 393224 | tf_op jit(solution)/shard_map/ppermute | solution.py:22
  215.2 11.4 %collective-permute-start.209 = (bf16[256,256]{1,0:T(8,128)(2,1)S(1)}, bf16[256,256]{1,0:T(8,128)(2,1)S(1)}, u32[]{:S(2)}, u32[]{:S(2)}) collective-permute-start(bf16[256,256]{1,0:T(8,128)(2,1)S(1)} %get-tuple-element.334), channel_id=1, source_target_pairs={{0,2},{1,3},{2,0},{3,1},{4,6},{5,7},{6,4},{7,5},{8,10},{9,11},{10,... | collective-permute-start | bytes 393224 | tf_op jit(solution)/shard_map/ppermute | solution.py:22
  217.1 9.4 %collective-permute-start.210 = (bf16[256,256]{1,0:T(8,128)(2,1)S(1)}, bf16[256,256]{1,0:T(8,128)(2,1)S(1)}, u32[]{:S(2)}, u32[]{:S(2)}) collective-permute-start(bf16[256,256]{1,0:T(8,128)(2,1)S(1)} %get-tuple-element.334), channel_id=1, source_target_pairs={{0,3},{1,0},{2,1},{3,2},{4,7},{5,4},{6,5},{7,6},{8,11},{9,8},{10,9... | collective-permute-start | bytes 393224 | tf_op jit(solution)/shard_map/ppermute | solution.py:22
  (3 other events, 8.4 us)

commit v5 on v4

v5 whole, which is shorter than its diff:
```python
import math

import jax
import jax.numpy as jnp
from jax import lax
from jax.sharding import PartitionSpec as P

K = 4096
BOTH = ("docs", "proj")


def place(index):
    docs, p = divmod(index, 4)
    return docs >> 5, docs >> 3 & 3, docs >> 1 & 3, docs & 1, p


def number(zh, y, x, c, p):
    return ((zh % 4 * 4 + y % 4) * 4 + x % 4) * 8 + c % 2 * 4 + p % 4


def send(value, to):
    return lax.ppermute(value, BOTH, [(i, number(*to(*place(i)))) for i in range(512)])


def after(value, *others):
    return lax.optimization_barrier((value,) + others)[0]


def put(buffer, piece, at):
    return lax.dynamic_update_slice(
        buffer, piece[None], (at,) + (0,) * (buffer.ndim - 1)
    )


def gather4(value, mine, move):
    out = jnp.zeros((4,) + value.shape, value.dtype)
    out = put(out, value, mine)
    for t in (1, 2, 3):
        out = put(out, send(value, lambda *at: move(t, *at)), (mine - t) % 4)
    return out


def along_zh(t, zh, y, x, c, p):
    return zh + t, y, x, c, p


def groups(key):
    found = {}
    for docs in range(128):
        found.setdefault(key(*place(4 * docs)[:4]), []).append(docs)
    return list(found.values())


FIRST = groups(lambda zh, y, x, c: (zh, c, y if c else x))
SECOND = groups(lambda zh, y, x, c: (zh, c, x if c else y))
CORES = groups(lambda zh, y, x, c: (zh, y, x))


def gather(value, which):
    return lax.all_gather(value, "docs", axis_index_groups=which)


def up_z(zh, y, x, c, p):
    z = 4 * zh + p + 1
    return z // 4, y, x, c, z % 4


def down_z(zh, y, x, c, p):
    z = 4 * zh + p - 1
    return z // 4, y, x, c, z % 4


def rotate(value, by):
    def branch(shift):
        def move(zh, y, x, c, p):
            m = (y * 8 + x * 2 + c - shift) % 32
            return zh, m >> 3, m >> 1 & 3, m & 1, p

        return lambda one: send(one, move) if shift else one

    return lax.switch(by, [branch(shift) for shift in range(32)], value)


def on_device(grads, precond, offsets):
    docs, p = lax.axis_index("docs"), lax.axis_index("proj")
    zh, m = docs // 32, docs % 32

    below, above = [grads], [grads]
    for _ in range(4):
        below.append(send(below[-1], up_z))
        above.append(send(above[-1], down_z))
    held = gather4(precond, (zh - p) % 4, along_zh)
    for step, which in ((1, FIRST), (2, SECOND), (4, CORES)):
        held = gather(after(held, below[step], above[step]), which)

    half = grads.shape[0] // 2
    far = jnp.concatenate(
        [
            send(above[4][:half], lambda *at: along_zh(-1, *at)),
            send(below[4][half:], lambda *at: along_zh(1, *at)),
        ]
    )
    blocks = [grads, above[4], far, below[4]]

    def partner(round_):
        low = offsets[round_] % 32
        ahead = (offsets[round_] // 32 + (m < low)) % 4
        value = blocks[0]
        for i in (1, 2, 3):
            value = jnp.where(ahead == i, blocks[i], value)
        return rotate(value, low)

    partners = [partner(0), partner(1)]

    rows = jnp.stack(
        [held[0].transpose(2, 1, 0, 3, 4), held[1].transpose(2, 0, 1, 3, 4)], axis=3
    ).reshape(4, 1024, precond.shape[1])
    slabs = [grads] + [
        jnp.where(p + i < 4, above[i], below[4 - i]) for i in (1, 2, 3)
    ]
    pre = sum(
        jnp.dot(slabs[i], rows[i], preferred_element_type=jnp.float32) for i in range(4)
    ).astype(jnp.bfloat16)
    grams = jnp.stack(
        [
            lax.dot_general(
                pre, other, (((1,), (1,)), ((), ())), preferred_element_type=jnp.float32
            )
            for other in partners
        ]
    )
    parts = lax.all_gather(grams.astype(jnp.bfloat16), "proj").astype(jnp.float32)
    return jnp.sum(parts, axis=0) * jnp.float32(1.0 / math.sqrt(K))


def solution(mesh):
    placed = (P("docs", "proj"), P("docs", "proj"), P())
    return jax.shard_map(
        on_device, mesh=mesh, in_specs=placed, out_specs=P(None, "docs", None), check_vma=False
    )
```

time: 229 us -> 248 us (1.083)
  waiting for transfers between devices: 64.5 us -> 139 us
  starting transfers between devices: 129 us -> 71.2 us
  between operations: 6.29 us -> 18.8 us
  other arithmetic: 7.88 us -> 3.96 us
  local copies, waits for them, and re-layouts: 12 us -> 8.59 us
  matrix products: 7.6 us -> 4.35 us
    all_gather x0 -> x4, waiting for transfers between devices: none -> 60.6 us  [the longest x1 38.7 us: on_device(): lax.all_gather(grams.astype(jnp.bfloat16), 'proj').astype(jnp.float32)]
    ppermute x29 -> x15, starting transfers between devices: 129 us -> 71.1 us  [send(): lax.ppermute(value, BOTH, [(i, number(*to(*place(i)))) for i in range(512)])]
    ppermute x29 -> x15, waiting for transfers between devices: 64.5 us -> 78.8 us  [send(): lax.ppermute(value, BOTH, [(i, number(*to(*place(i)))) for i in range(512)])]
    dynamic_update_slice x12 -> x4, local copies, waits for them, and re-layouts: 7.79 us -> 0.87 us  [put(): lax.dynamic_update_slice(buffer, piece[None], (at,) + (0,) * (buffer.ndim...]
    another operation x5 -> x2, other arithmetic: 6.88 us -> 1.54 us  [the longest x1 0.81 us: on_device(): jnp.stack([held[0].transpose(2, 1, 0, 3, 4), held[1].transpose(2, 0, 1, 3...]
    slice x2 -> x3, local copies, waits for them, and re-layouts: 0.04 us -> 3.98 us  [the longest x1 3.94 us: on_device(): held[1].transpose(2, 0, 1, 3, 4)]
    broadcast_in_dim x3 -> x1, local copies, waits for them, and re-layouts: 2.7 us -> 0.02 us  [gather4(): out = jnp.zeros((4,) + value.shape, value.dtype)]
  transfers between devices with their start and end apart: 29 -> 19, of which waited for: 14 -> 13; matrix products, arithmetic and copies ran while one was open for 6% -> 1% of each run, Pallas kernels for 0% -> 0%
where the time goes in v5:
time: 248 us; the launch traced here: 247 us
  waiting for transfers between devices  139 us (56%)
  starting transfers between devices  71.2 us (29%)
  between operations  18.8 us (8%)
  local copies, waits for them, and re-layouts  8.59 us (3%)
  matrix products  4.35 us (2%)
  other arithmetic  3.96 us (2%)
    ppermute x15, waiting for transfers between devices, send(): lax.ppermute(value, BOTH, [(i, number(*to(*place(i)))) for i in range(512)])  78.8 us
    ppermute x15, starting transfers between devices, send(): lax.ppermute(value, BOTH, [(i, number(*to(*place(i)))) for i in range(512)])  71.1 us
    all_gather x1, waiting for transfers between devices, on_device(): lax.all_gather(grams.astype(jnp.bfloat16), 'proj').astype(jnp.float32)  38.7 us
    all_gather x3, waiting for transfers between devices, gather(): return lax.all_gather(value, 'docs', axis_index_groups=which)  21.9 us
  transfers between devices with their start and end apart: 19, of which 13 were waited for; matrix products, arithmetic and copies ran while one was open for 1% of the time, Pallas kernels for 0%

profile of v5, /device:TPU:1, one launch (start us, length us, event | category | flops | bytes accessed | tf_op | source)
XLA Modules:
  0.0 246.8 jit_solution(3381983042517170851)
XLA Ops:
  6.5 11.9 %collective-permute-start.66 = (bf16[256,1024]{1,0:T(8,128)(2,1)}, bf16[256,1024]{1,0:T(8,128)(2,1)S(1)}, u32[]{:S(2)}, u32[]{:S(2)}) collective-permute-start(bf16[256,1024]{1,0:T(8,128)(2,1)} %param.67), channel_id=1, source_target_pairs={{0,387},{1,0},{2,1},{3,2},{4,391},{5,4},{6,5},{7,6},{8,395},{9,8},... | collective-permute-start | bytes 1572872 | tf_op jit(solution)/shard_map/ppermute | solution.py:22
  18.5 1.9 collective-permute-start.65
  20.4 1.9 collective-permute-start.62
  22.3 10.3 %collective-permute-start.63 = (bf16[32,1024]{1,0:T(8,128)(2,1)}, bf16[32,1024]{1,0:T(8,128)(2,1)S(1)}, u32[]{:S(2)}, u32[]{:S(2)}) collective-permute-start(bf16[32,1024]{1,0:T(8,128)(2,1)} %param.68), channel_id=1, source_target_pairs={{0,256},{1,257},{2,258},{3,259},{4,260},{5,261},{6,262},{7,263},{8... | collective-permute-start | bytes 196616 | tf_op jit(solution)/shard_map/ppermute | solution.py:22
  32.6 4.7 %collective-permute-start.64 = (bf16[32,1024]{1,0:T(8,128)(2,1)}, bf16[32,1024]{1,0:T(8,128)(2,1)S(1)}, u32[]{:S(2)}, u32[]{:S(2)}) collective-permute-start(bf16[32,1024]{1,0:T(8,128)(2,1)} %param.68), channel_id=1, source_target_pairs={{0,384},{1,385},{2,386},{3,387},{4,388},{5,389},{6,390},{7,391},{8... | collective-permute-start | bytes 196616 | tf_op jit(solution)/shard_map/ppermute | solution.py:22
  38.3 5.5 %collective-permute-done.63 = bf16[32,1024]{1,0:T(8,128)(2,1)S(1)} collective-permute-done((bf16[32,1024]{1,0:T(8,128)(2,1)}, bf16[32,1024]{1,0:T(8,128)(2,1)S(1)}, u32[]{:S(2)}, u32[]{:S(2)}) %collective-permute-start.63) | collective-permute-done | bytes 65568 | tf_op jit(solution)/shard_map/ppermute | solution.py:22
  44.9 5.2 %collective-permute-start.68 = (bf16[256,1024]{1,0:T(8,128)(2,1)S(1)}, bf16[256,1024]{1,0:T(8,128)(2,1)S(1)}, u32[]{:S(2)}, u32[]{:S(2)}) collective-permute-start(bf16[256,1024]{1,0:T(8,128)(2,1)S(1)} %collective-permute-done.66), channel_id=1, source_target_pairs={{0,387},{1,0},{2,1},{3,2},{4,391},{5,4},{6,5},{7,6},{8,395},{9,8},... | collective-permute-start | bytes 1572872 | tf_op jit(solution)/shard_map/ppermute | solution.py:22
  50.2 1.9 collective-permute-start.67
  52.1 6.0 %collective-permute-done.68 = bf16[256,1024]{1,0:T(8,128)(2,1)S(1)} collective-permute-done((bf16[256,1024]{1,0:T(8,128)(2,1)S(1)}, bf16[256,1024]{1,0:T(8,128)(2,1)S(1)}, u32[]{:S(2)}, u32[]{:S(2)}) %collective-permute-start.68) | collective-permute-done | bytes 524320 | tf_op jit(solution)/shard_map/ppermute | solution.py:22
  58.2 5.0 %collective-permute-done.67 = bf16[256,1024]{1,0:T(8,128)(2,1)S(1)} collective-permute-done((bf16[256,1024]{1,0:T(8,128)(2,1)S(1)}, bf16[256,1024]{1,0:T(8,128)(2,1)S(1)}, u32[]{:S(2)}, u32[]{:S(2)}) %collective-permute-start.67) | collective-permute-done | bytes 524320 | tf_op jit(solution)/shard_map/ppermute | solution.py:22
  63.2 11.0 %all-gather.10.cloned.1.call-done = bf16[16,32,1024]{2,1,0:T(8,128)(2,1)} async-done(((bf16[4,32,1024]{2,1,0:T(8,128)(2,1)}), bf16[16,32,1024]{2,1,0:T(8,128)(2,1)}) %all-gather.10.cloned.1.call-update) | async-done | bytes 1048592 | tf_op jit(solution)/shard_map/all_gather | solution.py:60
  74.2 5.7 %collective-permute-start.71 = (bf16[256,1024]{1,0:T(8,128)(2,1)S(1)}, bf16[256,1024]{1,0:T(8,128)(2,1)S(1)}, u32[]{:S(2)}, u32[]{:S(2)}) collective-permute-start(bf16[256,1024]{1,0:T(8,128)(2,1)S(1)} %collective-permute-done.68), channel_id=1, source_target_pairs={{0,387},{1,0},{2,1},{3,2},{4,391},{5,4},{6,5},{7,6},{8,395},{9,8},... | collective-permute-start | bytes 1572872 | tf_op jit(solution)/shard_map/ppermute | solution.py:22
  79.9 1.9 collective-permute-start.69
  81.9 6.7 %collective-permute-done.71 = bf16[256,1024]{1,0:T(8,128)(2,1)S(1)} collective-permute-done((bf16[256,1024]{1,0:T(8,128)(2,1)S(1)}, bf16[256,1024]{1,0:T(8,128)(2,1)S(1)}, u32[]{:S(2)}, u32[]{:S(2)}) %collective-permute-start.71) | collective-permute-done | bytes 524320 | tf_op jit(solution)/shard_map/ppermute | solution.py:22
  88.6 5.3 %collective-permute-start.72 = (bf16[256,1024]{1,0:T(8,128)(2,1)S(1)}, bf16[256,1024]{1,0:T(8,128)(2,1)S(1)}, u32[]{:S(2)}, u32[]{:S(2)}) collective-permute-start(bf16[256,1024]{1,0:T(8,128)(2,1)S(1)} %collective-permute-done.71), channel_id=1, source_target_pairs={{0,387},{1,0},{2,1},{3,2},{4,391},{5,4},{6,5},{7,6},{8,395},{9,8},... | collective-permute-start | bytes 1572872 | tf_op jit(solution)/shard_map/ppermute | solution.py:22
  93.9 1.9 collective-permute-start.70
  95.8 5.7 %collective-permute-done.72 = bf16[256,1024]{1,0:T(8,128)(2,1)S(1)} collective-permute-done((bf16[256,1024]{1,0:T(8,128)(2,1)S(1)}, bf16[256,1024]{1,0:T(8,128)(2,1)S(1)}, u32[]{:S(2)}, u32[]{:S(2)}) %collective-permute-start.72) | collective-permute-done | bytes 524320 | tf_op jit(solution)/shard_map/ppermute | solution.py:22
  101.6 5.2 %collective-permute-done.70 = bf16[256,1024]{1,0:T(8,128)(2,1)S(1)} collective-permute-done((bf16[256,1024]{1,0:T(8,128)(2,1)S(1)}, bf16[256,1024]{1,0:T(8,128)(2,1)S(1)}, u32[]{:S(2)}, u32[]{:S(2)}) %collective-permute-start.70) | collective-permute-done | bytes 524320 | tf_op jit(solution)/shard_map/ppermute | solution.py:22
  106.8 10.9 %all-gather.12.cloned.1.call-done = bf16[16,4,32,1024]{3,2,1,0:T(8,128)(2,1)} async-done(((bf16[4,4,32,1024]{3,2,1,0:T(8,128)(2,1)}), bf16[16,4,32,1024]{3,2,1,0:T(8,128)(2,1)}) %all-gather.12.cloned.1.call-update) | async-done | bytes 4194320 | tf_op jit(solution)/shard_map/all_gather | solution.py:60
  117.8 8.2 %collective-permute-start.73 = (bf16[128,1024]{1,0:T(8,128)(2,1)S(1)}, bf16[128,1024]{1,0:T(8,128)(2,1)S(1)}, u32[]{:S(2)}, u32[]{:S(2)}) collective-permute-start(bf16[128,1024]{1,0:T(8,128)(2,1)S(1)} %slice.56), channel_id=1, source_target_pairs={{0,384},{1,385},{2,386},{3,387},{4,388},{5,389},{6,390},{7,391},{8... | collective-permute-start | bytes 786440 | tf_op jit(solution)/shard_map/ppermute | solution.py:22
  126.0 1.9 collective-permute-start.74
  133.8 15.0 %collective-permute-done.73 = bf16[128,1024]{1,0:T(8,128)(2,1)S(1)} collective-permute-done((bf16[128,1024]{1,0:T(8,128)(2,1)S(1)}, bf16[128,1024]{1,0:T(8,128)(2,1)S(1)}, u32[]{:S(2)}, u32[]{:S(2)}) %collective-permute-start.73) | collective-permute-done | bytes 262176 | tf_op jit(solution)/shard_map/ppermute | solution.py:22
  149.1 19.5 %conditional.2 = (bf16[256,1024]{1,0:T(8,128)(2,1)S(1)}) conditional(s32[]{:T(128)} %clamp.6, bf16[256,1024]{1,0:T(8,128)(2,1)S(1)} %get-tuple-element.147, bf16[256,1024]{1,0:T(8,128)(2,1)S(1)} %get-tuple-element.147, bf16[256,1024]{1,0:T(8,128)(2,1)S(1)} %get-tuple-element.147, ...), branch_computations={%region_0.1_spmd, %region_1.2_spmd, %region_2.3_spmd, %region_3.4_... | conditional | bytes 3145776 | solution.py:81
  149.1 4.9 %collective-permute-start.28 = (bf16[256,1024]{1,0:T(8,128)(2,1)S(1)}, bf16[256,1024]{1,0:T(8,128)(2,1)S(1)}, u32[]{:S(2)}, u32[]{:S(2)}) collective-permute-start(bf16[256,1024]{1,0:T(8,128)(2,1)S(1)} %param.29), channel_id=1, source_target_pairs={{0,12},{1,13},{2,14},{3,15},{4,16},{5,17},{6,18},{7,19},{8,20},{9,... | collective-permute-start | bytes 1572872 | tf_op jit(solution)/shard_map/cond/branch_29_fun/ppermute | solution.py:22
  154.1 14.5 %collective-permute-done.28 = bf16[256,1024]{1,0:T(8,128)(2,1)S(1)} collective-permute-done((bf16[256,1024]{1,0:T(8,128)(2,1)S(1)}, bf16[256,1024]{1,0:T(8,128)(2,1)S(1)}, u32[]{:S(2)}, u32[]{:S(2)}) %collective-permute-start.28) | collective-permute-done | bytes 524320 | tf_op jit(solution)/shard_map/cond/branch_29_fun/ppermute | solution.py:22
  168.6 18.4 %conditional.3 = (bf16[256,1024]{1,0:T(8,128)(2,1)S(1)}) conditional(s32[]{:T(128)} %clamp.7, bf16[256,1024]{1,0:T(8,128)(2,1)S(1)} %get-tuple-element.148, bf16[256,1024]{1,0:T(8,128)(2,1)S(1)} %get-tuple-element.148, bf16[256,1024]{1,0:T(8,128)(2,1)S(1)} %get-tuple-element.148, ...), branch_computations={%region_32.33_spmd, %region_33.34_spmd, %region_34.35_spmd, %regio... | conditional | bytes 3145776 | solution.py:81
  168.7 3.4 %collective-permute-start.43 = (bf16[256,1024]{1,0:T(8,128)(2,1)S(1)}, bf16[256,1024]{1,0:T(8,128)(2,1)S(1)}, u32[]{:S(2)}, u32[]{:S(2)}) collective-permute-start(bf16[256,1024]{1,0:T(8,128)(2,1)S(1)} %param.45), channel_id=1, source_target_pairs={{0,76},{1,77},{2,78},{3,79},{4,80},{5,81},{6,82},{7,83},{8,84},{9,... | collective-permute-start | bytes 1572872 | tf_op jit(solution)/shard_map/cond/branch_13_fun/ppermute | solution.py:22
  172.1 14.7 %collective-permute-done.43 = bf16[256,1024]{1,0:T(8,128)(2,1)S(1)} collective-permute-done((bf16[256,1024]{1,0:T(8,128)(2,1)S(1)}, bf16[256,1024]{1,0:T(8,128)(2,1)S(1)}, u32[]{:S(2)}, u32[]{:S(2)}) %collective-permute-start.43) | collective-permute-done | bytes 524320 | tf_op jit(solution)/shard_map/cond/branch_13_fun/ppermute | solution.py:22
  187.0 3.9 %fusion.14 = (bf16[4,4,4,32,1024]{4,3,2,1,0:T(8,128)(2,1)S(1)}, bf16[4,4,4,32,1024]{4,3,2,1,0:T(8,128)(2,1)S(1)}) fusion(bf16[8,4,4,32,1024]{4,3,2,1,0:T(8,128)(2,1)} %all-gather.14.cloned.1.call-done), kind=kLoop, calls=%fused_computation.39 | loop fusion | bytes 16777216 | tf_op jit(solution)/shard_map/slice | solution.py:116
  195.8 1.0 fusion.3
  199.3 38.7 %all-gather.8.cloned.1.call-done = bf16[4,2,256,256]{3,2,1,0:T(8,128)(2,1)} async-done(((bf16[1,2,256,256]{3,2,1,0:T(8,128)(2,1)}), bf16[4,2,256,256]{3,2,1,0:T(8,128)(2,1)}) %all-gather.8.cloned.1.call-update) | async-done | bytes 1048592 | tf_op jit(solution)/shard_map/all_gather | solution.py:132
  238.0 1.4 convert_reduce_fusion
  (64 shorter events, 11.1 us)
Async XLA Ops:
  6.5 67.6 %all-gather.10.cloned.1.call-start = ((), (), s32[]{:S(2)}) async-start(), calls=%async_computation.1 | async-start | bytes 1310720 | tf_op jit(solution)/shard_map/all_gather | solution.py:60
  6.5 37.6 %collective-permute-start.66 = (bf16[256,1024]{1,0:T(8,128)(2,1)}, bf16[256,1024]{1,0:T(8,128)(2,1)S(1)}, u32[]{:S(2)}, u32[]{:S(2)}) collective-permute-start(bf16[256,1024]{1,0:T(8,128)(2,1)} %param.67), channel_id=1, source_target_pairs={{0,387},{1,0},{2,1},{3,2},{4,391},{5,4},{6,5},{7,6},{8,395},{9,8},... | collective-permute-start | bytes 1572872 | tf_op jit(solution)/shard_map/ppermute | solution.py:22
  18.5 25.7 %collective-permute-start.65 = (bf16[256,1024]{1,0:T(8,128)(2,1)}, bf16[256,1024]{1,0:T(8,128)(2,1)S(1)}, u32[]{:S(2)}, u32[]{:S(2)}) collective-permute-start(bf16[256,1024]{1,0:T(8,128)(2,1)} %param.67), channel_id=1, source_target_pairs={{0,1},{1,2},{2,3},{3,128},{4,5},{5,6},{6,7},{7,132},{8,9},{9,10},{... | collective-permute-start | bytes 1572872 | tf_op jit(solution)/shard_map/ppermute | solution.py:22
  20.4 17.8 %collective-permute-start.62 = (bf16[32,1024]{1,0:T(8,128)(2,1)}, bf16[32,1024]{1,0:T(8,128)(2,1)S(1)}, u32[]{:S(2)}, u32[]{:S(2)}) collective-permute-start(bf16[32,1024]{1,0:T(8,128)(2,1)} %param.68), channel_id=1, source_target_pairs={{0,128},{1,129},{2,130},{3,131},{4,132},{5,133},{6,134},{7,135},{8... | collective-permute-start | bytes 196616 | tf_op jit(solution)/shard_map/ppermute | solution.py:22
  22.3 21.4 %collective-permute-start.63 = (bf16[32,1024]{1,0:T(8,128)(2,1)}, bf16[32,1024]{1,0:T(8,128)(2,1)S(1)}, u32[]{:S(2)}, u32[]{:S(2)}) collective-permute-start(bf16[32,1024]{1,0:T(8,128)(2,1)} %param.68), channel_id=1, source_target_pairs={{0,256},{1,257},{2,258},{3,259},{4,260},{5,261},{6,262},{7,263},{8... | collective-permute-start | bytes 196616 | tf_op jit(solution)/shard_map/ppermute | solution.py:22
  32.6 11.5 %collective-permute-start.64 = (bf16[32,1024]{1,0:T(8,128)(2,1)}, bf16[32,1024]{1,0:T(8,128)(2,1)S(1)}, u32[]{:S(2)}, u32[]{:S(2)}) collective-permute-start(bf16[32,1024]{1,0:T(8,128)(2,1)} %param.68), channel_id=1, source_target_pairs={{0,384},{1,385},{2,386},{3,387},{4,388},{5,389},{6,390},{7,391},{8... | collective-permute-start | bytes 196616 | tf_op jit(solution)/shard_map/ppermute | solution.py:22
  44.2 0.7 copy-start.1
  44.2 73.5 %copy-start.2 = (bf16[256,1024]{1,0:T(8,128)(2,1)}, bf16[256,1024]{1,0:T(8,128)(2,1)S(1)}, u32[]{:S(2)}) copy-start(bf16[256,1024]{1,0:T(8,128)(2,1)S(1)} %collective-permute-done.66) | copy-start | bytes 1572868
  44.9 72.7 %all-gather.12.cloned.1.call-start = ((), (), s32[]{:S(2)}) async-start(), calls=%async_computation.2 | async-start | bytes 5242880 | tf_op jit(solution)/shard_map/all_gather | solution.py:60
  44.9 13.2 %collective-permute-start.68 = (bf16[256,1024]{1,0:T(8,128)(2,1)S(1)}, bf16[256,1024]{1,0:T(8,128)(2,1)S(1)}, u32[]{:S(2)}, u32[]{:S(2)}) collective-permute-start(bf16[256,1024]{1,0:T(8,128)(2,1)S(1)} %collective-permute-done.66), channel_id=1, source_target_pairs={{0,387},{1,0},{2,1},{3,2},{4,391},{5,4},{6,5},{7,6},{8,395},{9,8},... | collective-permute-start | bytes 1572872 | tf_op jit(solution)/shard_map/ppermute | solution.py:22
  50.2 13.0 %collective-permute-start.67 = (bf16[256,1024]{1,0:T(8,128)(2,1)S(1)}, bf16[256,1024]{1,0:T(8,128)(2,1)S(1)}, u32[]{:S(2)}, u32[]{:S(2)}) collective-permute-start(bf16[256,1024]{1,0:T(8,128)(2,1)S(1)} %collective-permute-done.65), channel_id=1, source_target_pairs={{0,1},{1,2},{2,3},{3,128},{4,5},{5,6},{6,7},{7,132},{8,9},{9,10},{... | collective-permute-start | bytes 1572872 | tf_op jit(solution)/shard_map/ppermute | solution.py:22
  58.1 59.5 %copy-start.4 = (bf16[256,1024]{1,0:T(8,128)(2,1)}, bf16[256,1024]{1,0:T(8,128)(2,1)S(1)}, u32[]{:S(2)}) copy-start(bf16[256,1024]{1,0:T(8,128)(2,1)S(1)} %collective-permute-done.68) | copy-start | bytes 1572868
  63.2 30.7 %copy-start.6 = (bf16[256,1024]{1,0:T(8,128)(2,1)}, bf16[256,1024]{1,0:T(8,128)(2,1)S(1)}, u32[]{:S(2)}) copy-start(bf16[256,1024]{1,0:T(8,128)(2,1)S(1)} %collective-permute-done.67) | copy-start | bytes 1572868
  74.2 112.8 %all-gather.14.cloned.1.call-start = ((), (), s32[]{:S(2)}) async-start(), calls=%async_computation.3 | async-start | bytes 12582912 | tf_op jit(solution)/shard_map/all_gather | solution.py:60
  74.2 14.3 %collective-permute-start.71 = (bf16[256,1024]{1,0:T(8,128)(2,1)S(1)}, bf16[256,1024]{1,0:T(8,128)(2,1)S(1)}, u32[]{:S(2)}, u32[]{:S(2)}) collective-permute-start(bf16[256,1024]{1,0:T(8,128)(2,1)S(1)} %collective-permute-done.68), channel_id=1, source_target_pairs={{0,387},{1,0},{2,1},{3,2},{4,391},{5,4},{6,5},{7,6},{8,395},{9,8},... | collective-permute-start | bytes 1572872 | tf_op jit(solution)/shard_map/ppermute | solution.py:22
  79.9 14.0 %collective-permute-start.69 = (bf16[256,1024]{1,0:T(8,128)(2,1)S(1)}, bf16[256,1024]{1,0:T(8,128)(2,1)S(1)}, u32[]{:S(2)}, u32[]{:S(2)}) collective-permute-start(bf16[256,1024]{1,0:T(8,128)(2,1)S(1)} %collective-permute-done.67), channel_id=1, source_target_pairs={{0,1},{1,2},{2,3},{3,128},{4,5},{5,6},{6,7},{7,132},{8,9},{9,10},{... | collective-permute-start | bytes 1572872 | tf_op jit(solution)/shard_map/ppermute | solution.py:22
  88.6 13.0 %copy-start.8 = (bf16[256,1024]{1,0:T(8,128)(2,1)}, bf16[256,1024]{1,0:T(8,128)(2,1)S(1)}, u32[]{:S(2)}) copy-start(bf16[256,1024]{1,0:T(8,128)(2,1)S(1)} %collective-permute-done.71) | copy-start | bytes 1572868
  88.6 13.0 %collective-permute-start.72 = (bf16[256,1024]{1,0:T(8,128)(2,1)S(1)}, bf16[256,1024]{1,0:T(8,128)(2,1)S(1)}, u32[]{:S(2)}, u32[]{:S(2)}) collective-permute-start(bf16[256,1024]{1,0:T(8,128)(2,1)S(1)} %collective-permute-done.71), channel_id=1, source_target_pairs={{0,387},{1,0},{2,1},{3,2},{4,391},{5,4},{6,5},{7,6},{8,395},{9,8},... | collective-permute-start | bytes 1572872 | tf_op jit(solution)/shard_map/ppermute | solution.py:22
  93.9 7.7 %copy-start.10 = (bf16[256,1024]{1,0:T(8,128)(2,1)}, bf16[256,1024]{1,0:T(8,128)(2,1)S(1)}, u32[]{:S(2)}) copy-start(bf16[256,1024]{1,0:T(8,128)(2,1)S(1)} %collective-permute-done.69) | copy-start | bytes 1572868
  93.9 12.9 %collective-permute-start.70 = (bf16[256,1024]{1,0:T(8,128)(2,1)S(1)}, bf16[256,1024]{1,0:T(8,128)(2,1)S(1)}, u32[]{:S(2)}, u32[]{:S(2)}) collective-permute-start(bf16[256,1024]{1,0:T(8,128)(2,1)S(1)} %collective-permute-done.69), channel_id=1, source_target_pairs={{0,1},{1,2},{2,3},{3,128},{4,5},{5,6},{6,7},{7,132},{8,9},{9,10},{... | collective-permute-start | bytes 1572872 | tf_op jit(solution)/shard_map/ppermute | solution.py:22
  117.6 10.3 %copy-start.12 = (s32[2]{0:T(128)S(1)}, s32[2]{0:T(128)}, u32[]{:S(2)}) copy-start(s32[2]{0:T(128)} %param.69) | copy-start | bytes 28
  117.7 31.2 %copy-start = (bf16[256,1024]{1,0:T(8,128)(2,1)S(1)}, bf16[256,1024]{1,0:T(8,128)(2,1)}, u32[]{:S(2)}) copy-start(bf16[256,1024]{1,0:T(8,128)(2,1)} %param.67) | copy-start | bytes 1572868
  117.7 120.3 %all-gather.8.cloned.1.call-start = ((), (), s32[]{:S(2)}) async-start(), calls=%async_computation | async-start | bytes 1310720 | tf_op jit(solution)/shard_map/all_gather | solution.py:132
  117.8 31.1 %collective-permute-start.73 = (bf16[128,1024]{1,0:T(8,128)(2,1)S(1)}, bf16[128,1024]{1,0:T(8,128)(2,1)S(1)}, u32[]{:S(2)}, u32[]{:S(2)}) collective-permute-start(bf16[128,1024]{1,0:T(8,128)(2,1)S(1)} %slice.56), channel_id=1, source_target_pairs={{0,384},{1,385},{2,386},{3,387},{4,388},{5,389},{6,390},{7,391},{8... | collective-permute-start | bytes 786440 | tf_op jit(solution)/shard_map/ppermute | solution.py:22
  126.0 22.8 %collective-permute-start.74 = (bf16[128,1024]{1,0:T(8,128)(2,1)S(1)}, bf16[128,1024]{1,0:T(8,128)(2,1)S(1)}, u32[]{:S(2)}, u32[]{:S(2)}) collective-permute-start(bf16[128,1024]{1,0:T(8,128)(2,1)S(1)} %slice.57), channel_id=1, source_target_pairs={{0,128},{1,129},{2,130},{3,131},{4,132},{5,133},{6,134},{7,135},{8... | collective-permute-start | bytes 786440 | tf_op jit(solution)/shard_map/ppermute | solution.py:22
  149.1 19.4 %collective-permute-start.28 = (bf16[256,1024]{1,0:T(8,128)(2,1)S(1)}, bf16[256,1024]{1,0:T(8,128)(2,1)S(1)}, u32[]{:S(2)}, u32[]{:S(2)}) collective-permute-start(bf16[256,1024]{1,0:T(8,128)(2,1)S(1)} %param.29), channel_id=1, source_target_pairs={{0,12},{1,13},{2,14},{3,15},{4,16},{5,17},{6,18},{7,19},{8,20},{9,... | collective-permute-start | bytes 1572872 | tf_op jit(solution)/shard_map/cond/branch_29_fun/ppermute | solution.py:22
  168.7 18.1 %collective-permute-start.43 = (bf16[256,1024]{1,0:T(8,128)(2,1)S(1)}, bf16[256,1024]{1,0:T(8,128)(2,1)S(1)}, u32[]{:S(2)}, u32[]{:S(2)}) collective-permute-start(bf16[256,1024]{1,0:T(8,128)(2,1)S(1)} %param.45), channel_id=1, source_target_pairs={{0,76},{1,77},{2,78},{3,79},{4,80},{5,81},{6,82},{7,83},{8,84},{9,... | collective-permute-start | bytes 1572872 | tf_op jit(solution)/shard_map/cond/branch_13_fun/ppermute | solution.py:22
  193.4 1.0 copy-start.5
  193.4 1.2 copy-start.7
  194.6 1.0 copy-start.3
  194.6 1.2 copy-start.11
  195.8 1.0 copy-start.9
Sparse Core Ops, SparseCore 0:
  45.0 29.1 all-gather.9
  76.3 41.3 all-gather.11
  119.7 32.3 all-gather.13
  199.4 38.5 all-gather.7
